TPU v7x, 512 devices: a whole 4x8x8 slice. The times are simulated.
512 devices in a mesh: col: 16 (over y, core), row: 32 (over z, x).
Axes of the slice: x: 4, y: 8, z: 8, core: 2. Of those that a mesh axis runs over, the one named last changes fastest.
Arguments:
- pair_rep: float32 [512, 512, 128], P('row', 'col'), may hold values from -6 to 6
- cotangent: float32 [512, 512, 128], P('row', 'col'), may hold values from -6 to 6
- chain_ids: int32 [512], replicated, may hold values from 0 to 3, never falling along the last dimension, each value on 1 to 256 neighbouring positions
- template: int32 [8, 8], replicated, may hold values from 0 to 1
- norm_gain: float32 [128], replicated, may hold values from 0.25 to 1.75
- w_query: float32 [128, 128], replicated
- w_key: float32 [128, 128], replicated
- w_value: float32 [128, 128], replicated, may hold values from -0.5 to 0.5
- w_gate: float32 [128, 128], replicated, may hold values from -0.5 to 0.5
- gate_bias: float32 [128], replicated, may hold values from -4 to 4
- w_out: float32 [128, 128], replicated, may hold values from -0.5 to 0.5
- w_bias: float32 [4, 128], replicated, may hold values from -0.5 to 0.5
Outputs:
- update: float32 [512, 512, 128], P('row', 'col')
- grad_pair: float32 [512, 512, 128], P('row', 'col')
- grad_query: float32 [128, 128], replicated
- grad_key: float32 [128, 128], replicated
- grad_value: float32 [128, 128], replicated
- grad_gate: float32 [128, 128], replicated
- grad_gate_bias: float32 [128], replicated
- grad_out: float32 [128, 128], replicated
- grad_bias: float32 [4, 128], replicated
- grad_gain: float32 [128], replicated
All inputs are finite; a program needn't handle non-finite values.
Results may differ from a plain program's by a relative error of at most 0.0003.
Values sent between devices are 32-bit elements; how exact they have to be, the bound alone decides.
No kernel may reach another device: no remote copies, remote signals or barrier semaphores. Data moves between devices by JAX's collectives and lax.ppermute only.
A program may use at most 64 MiB of HBM per device.

v0:
```python
import jax
import jax.numpy as jnp
from jax import lax
from jax.sharding import PartitionSpec as P

HIGHEST = lax.Precision.HIGHEST
NEG_FILL = -1000000000.0


def matmul(left, right):
    return jnp.dot(left, right, precision=HIGHEST, preferred_element_type=jnp.float32)


def attend_dense(queries, keys_col, values_col, bias_rows, keep_col, factor):
    scores = jnp.einsum("ihd,khd->ihk", queries, keys_col, precision=HIGHEST) * factor + bias_rows
    scores = jnp.where(keep_col[None, None, :], scores, NEG_FILL)
    highest = jnp.max(scores, axis=2, keepdims=True)
    weights = jnp.exp(scores - highest)
    normed_weights = weights / jnp.sum(weights, axis=2, keepdims=True)
    output = jnp.einsum("ihk,khd->ihd", normed_weights, values_col, precision=HIGHEST)
    return (output, normed_weights)


def attend_dense_back(queries, keys_col, values_col, normed_weights, output, d_output, factor):
    d_weights = jnp.einsum("ihd,khd->ihk", d_output, values_col, precision=HIGHEST)
    centred = jnp.sum(d_output * output, axis=2, keepdims=True)
    d_scores = normed_weights * (d_weights - centred)
    d_query = jnp.einsum("ihk,khd->ihd", d_scores, keys_col, precision=HIGHEST) * factor
    d_key = jnp.einsum("ihk,ihd->khd", d_scores, queries, precision=HIGHEST) * factor
    d_value = jnp.einsum("ihk,ihd->khd", normed_weights, d_output, precision=HIGHEST)
    return (d_query, d_key, d_value, d_scores)


def body(
    pair_rep,
    cotangent,
    chain_ids,
    template,
    norm_gain,
    w_query,
    w_key,
    w_value,
    w_gate,
    gate_bias,
    w_out,
    w_bias,
):
    column_cells, upstream = (
        lax.all_to_all(pair_rep, "row", split_axis=1, concat_axis=0, tiled=True),
        lax.all_to_all(cotangent, "row", split_axis=1, concat_axis=0, tiled=True),
    )
    tokens, cols, width = column_cells.shape
    head_count = w_bias.shape[0]
    head_depth = width // head_count
    factor = head_depth ** (-0.5)
    row_count = lax.axis_size("row")
    linear = lax.axis_index("col") * row_count + lax.axis_index("row")
    first_col = linear * cols
    own_chain = lax.dynamic_slice_in_dim(chain_ids, first_col, cols, 0)
    same_chain = chain_ids[:, None] == own_chain[None, :]
    block_count = template.shape[0]
    block_width = tokens // block_count
    own_block = (first_col + jnp.arange(cols, dtype=jnp.int32)) // block_width
    picker = (jnp.arange(block_count, dtype=jnp.int32)[:, None] == own_block[None, :]).astype(
        jnp.int32
    )
    block_keep = jnp.sum(template[:, :, None] * picker[None, :, :], axis=1)
    keep_mask = same_chain | (jnp.repeat(block_keep, block_width, axis=0) > 0)
    cells = column_cells.reshape(tokens * cols, width)
    center = jnp.mean(cells, axis=-1, keepdims=True)
    shifted = cells - center
    spread = jnp.mean(shifted * shifted, axis=-1, keepdims=True)
    inverse = lax.rsqrt(spread + 1e-05)
    scaled = shifted * inverse
    normed = scaled * norm_gain
    queries = matmul(normed, w_query).reshape(tokens, cols, head_count, head_depth)
    keys_all = matmul(normed, w_key).reshape(tokens, cols, head_count, head_depth)
    values_all = matmul(normed, w_value).reshape(tokens, cols, head_count, head_depth)
    gate = jax.nn.sigmoid(matmul(normed, w_gate) + gate_bias)
    normed_cols = normed.reshape(tokens, cols, width)
    bias_piece = jnp.einsum("ktc,hc->thk", normed_cols, w_bias, precision=HIGHEST)
    bias_rows = lax.all_gather(bias_piece, ("col", "row"), axis=0, tiled=True)
    actives = []
    slot = 0
    keep_col = keep_mask[:, slot]
    active = jnp.any(keep_col.reshape(block_count, block_width), axis=1)
    actives.append(active)
    attended_slot, kept_stat = attend_dense(
        queries[:, slot], keys_all[:, slot], values_all[:, slot], bias_rows, keep_col, factor
    )
    outputs = [attended_slot]
    saved = [kept_stat]
    attended = jnp.stack(outputs, axis=1).reshape(tokens * cols, width)
    gated = gate * attended
    update_cols = matmul(gated, w_out).reshape(tokens, cols, width)
    update_block = lax.all_to_all(update_cols, "row", split_axis=0, concat_axis=1, tiled=True)
    d_cells = upstream.reshape(tokens * cols, width)
    d_gated = matmul(d_cells, jnp.transpose(w_out))
    grad_out_w = matmul(jnp.transpose(gated), d_cells)
    d_attended = (d_gated * gate).reshape(tokens, cols, head_count, head_depth)
    d_gate_pre = d_gated * attended * gate * (1.0 - gate)
    slot = 0
    query_grad, key_grad, value_grad, score_grad = attend_dense_back(
        queries[:, slot],
        keys_all[:, slot],
        values_all[:, slot],
        saved[slot],
        outputs[slot],
        d_attended[:, slot],
        factor,
    )
    d_queries = [query_grad]
    d_keys = [key_grad]
    d_values = [value_grad]
    d_query = jnp.stack(d_queries, axis=1).reshape(tokens * cols, width)
    d_key = jnp.stack(d_keys, axis=1).reshape(tokens * cols, width)
    d_value = jnp.stack(d_values, axis=1).reshape(tokens * cols, width)
    bias_grad = lax.psum_scatter(score_grad, ("col", "row"), scatter_dimension=0, tiled=True)
    bias_back = jnp.einsum("thk,hc->ktc", bias_grad, w_bias, precision=HIGHEST).reshape(
        tokens * cols, width
    )
    grad_bias_w = jnp.einsum("thk,ktc->hc", bias_grad, normed_cols, precision=HIGHEST)
    d_normed = (
        matmul(d_query, jnp.transpose(w_query))
        + matmul(d_key, jnp.transpose(w_key))
        + matmul(d_value, jnp.transpose(w_value))
        + matmul(d_gate_pre, jnp.transpose(w_gate))
        + bias_back
    )
    grad_query_w = matmul(jnp.transpose(normed), d_query)
    grad_key_w = matmul(jnp.transpose(normed), d_key)
    grad_value_w = matmul(jnp.transpose(normed), d_value)
    grad_gate_w = matmul(jnp.transpose(normed), d_gate_pre)
    grad_gate_shift = jnp.sum(d_gate_pre, axis=0)
    grad_gain_w = jnp.sum(d_normed * scaled, axis=0)
    d_scaled = d_normed * norm_gain
    mean_term = jnp.mean(d_scaled, axis=-1, keepdims=True)
    cross_term = jnp.mean(d_scaled * scaled, axis=-1, keepdims=True)
    d_input = inverse * (d_scaled - mean_term - scaled * cross_term)
    grad_block = lax.all_to_all(
        d_input.reshape(tokens, cols, width), "row", split_axis=0, concat_axis=1, tiled=True
    )
    summed = lax.psum(
        (
            grad_query_w,
            grad_key_w,
            grad_value_w,
            grad_gate_w,
            grad_gate_shift,
            grad_out_w,
            grad_bias_w,
            grad_gain_w,
        ),
        ("col", "row"),
    )
    return (
        update_block,
        grad_block,
        summed[0] / tokens,
        summed[1] / tokens,
        summed[2] / tokens,
        summed[3] / tokens,
        summed[4] / tokens,
        summed[5] / tokens,
        summed[6] / tokens,
        summed[7] / tokens,
    )


def solution(mesh):
    in_specs = (
        P("row", "col", None),
        P("row", "col", None),
        P(),
        P(),
        P(),
        P(),
        P(),
        P(),
        P(),
        P(),
        P(),
        P(),
    )
    out_specs = (
        P("row", "col", None),
        P("row", "col", None),
        P(),
        P(),
        P(),
        P(),
        P(),
        P(),
        P(),
        P(),
    )
    return jax.shard_map(body, mesh=mesh, in_specs=in_specs, out_specs=out_specs, check_vma=False)
```

profile of v0, /device:TPU:1, one launch (start us, length us, event | category | flops | bytes accessed | tf_op | source)
XLA Modules:
  0.0 607.2 jit_solution(17724313898719080265)
XLA Ops:
  7.2 1.1 copy.46
  8.4 24.7 %all_to_all.66 = f32[16,32,128]{2,0,1:T(8,128)S(1)} all-to-all(f32[16,32,128]{2,0,1:T(8,128)S(1)} %copy.46), channel_id=1, replica_groups=mesh['col'=16,'row'=32] {'row'}, dimensions={1} | all-to-all | bytes 524288 | tf_op jit(solution)/shard_map/all_to_all | solution.py:49
  33.8 1.6 convolution_bitcast_fusion
  35.5 1.8 copy.55
  37.3 4.8 all-to-all-start.2
  42.1 0.8 multiply_reduce_fusion.4
  43.1 0.9 copy.50
  44.0 0.9 copy.49
  45.0 0.9 copy.48
  45.9 1.3 dynamic_slice.3
  47.2 1.3 compare_or_fusion
  48.5 0.9 multiply_multiply_fusion
  50.6 1.9 all-to-all-done.2
  52.9 99.2 %all-gather.4.cloned.1.call-done = f32[512,4,512]{2,1,0:T(4,128)} async-done(((f32[1,4,512]{2,1,0:T(4,128)}), f32[512,4,512]{2,1,0:T(4,128)}) %all-gather.4.cloned.1.call-update) | async-done | bytes 4194320 | tf_op jit(solution)/shard_map/all_gather | solution.py:82
  152.1 5.3 copy.51
  157.3 6.0 fusion.36
  163.4 0.6 fusion.3
  163.9 3.0 fusion.32
  167.0 0.6 fusion.34
  167.7 4.1 fusion.30
  171.8 4.2 fusion
  176.0 4.1 convolution_multiply_fusion
  180.2 2.5 convolution_multiply_fusion.1
  182.6 5.4 copy.59
  188.1 1.0 fusion.46
  189.1 1.0 fusion.17
  190.2 1.2 fusion.43
  191.4 1.2 fusion.44
  192.6 1.2 fusion.45
  193.9 1.3 fusion.40
  195.2 6.8 %all-to-all-start.1 = ((f32[512,1,128]{2,1,0:T(1,128)}), f32[512,1,128]{2,1,0:T(1,128)S(1)}, u32[]{:S(2)}, u32[]{:S(2)}) async-start(f32[512,1,128]{2,1,0:T(1,128)} %bitcast.22), calls=%async_computation.1 | async-start | bytes 524288 | tf_op jit(solution)/shard_map/all_to_all | solution.py:96
  202.4 0.4 convolution_add_fusion.2
  203.2 11.1 %all-to-all-done.1 = f32[512,1,128]{2,1,0:T(1,128)S(1)} async-done(((f32[512,1,128]{2,1,0:T(1,128)}), f32[512,1,128]{2,1,0:T(1,128)S(1)}, u32[]{:S(2)}, u32[]{:S(2)}) %all-to-all-start.1) | async-done | bytes 262176 | tf_op jit(solution)/shard_map/all_to_all | solution.py:96
  214.3 0.8 copy.67
  215.1 264.2 %all-reduce.5.cloned.1.call-done = (f32[512,4,512]{2,1,0:T(4,128)}, f32[128,128]{1,0:T(8,128)}, f32[128,128]{1,0:T(8,128)}, f32[128,128]{1,0:T(8,128)}, f32[128,128]{1,0:T(8,128)}, /*index=5*/f32[128,128]{1,0:T(8,128)}) async-done(((f32[512,4,512]{2,1,0:T(4,128)}, f32[128,128]{1,0:T(8,128)}, f32[128,128]{1,0:T(8,128)}, f32[128,128]{1,0:T(8,128)}, f32[128,128]{1,0:T(8,128)}, ...) | async-done | bytes 4522000
  479.3 1.1 fusion.27
  480.4 1.1 fusion.9
  481.5 1.5 broadcast_multiply_fusion.4
  483.0 0.6 multiply_reduce_fusion
  483.6 97.9 %all-reduce.1 = (f32[128]{0:T(128)S(1)}, f32[4,128]{1,0:T(4,128)S(1)}, f32[128]{0:T(128)S(1)}) all-reduce(f32[128]{0:T(128)S(1)} %get-tuple-element.42, f32[4,128]{1,0:T(4,128)S(1)} %fusion.9, f32[128]{0:T(128)S(1)} %get-tuple-element.30), channel_id=1, replica_groups=mesh['col'=16,'row'=32] {'col','row'}, use_global_device_ids=true, to_apply=%region_14.15 | all-reduce | flops 768 | bytes 6144 | tf_op jit(solution)/shard_map/psum | solution.py:143
  581.4 0.6 broadcast_multiply_fusion.6
  582.1 0.8 copy.60
  582.9 5.6 all-to-all-start.3
  588.5 0.5 broadcast_multiply_fusion.9
  589.0 1.5 broadcast_multiply_fusion.2
  590.6 0.7 broadcast_multiply_fusion
  591.2 8.4 %all-to-all-done.3 = f32[512,1,128]{2,1,0:T(1,128)S(1)} async-done(((f32[512,1,128]{2,1,0:T(1,128)}), f32[512,1,128]{2,1,0:T(1,128)S(1)}, u32[]{:S(2)}, u32[]{:S(2)}) %all-to-all-start.3) | async-done | bytes 262176 | tf_op jit(solution)/shard_map/all_to_all | solution.py:140
  599.6 0.8 copy.61
  (46 shorter events, 3.5 us)
Async XLA Ops:
  7.2 159.8 %copy-start = (f32[128,128]{1,0:T(8,128)S(1)}, f32[128,128]{1,0:T(8,128)}, u32[]{:S(2)}) copy-start(f32[128,128]{1,0:T(8,128)} %param.20) | copy-start | bytes 196612
  7.2 45.3 %copy-start.2 = (f32[128,128]{1,0:T(8,128)S(1)}, f32[128,128]{1,0:T(8,128)}, u32[]{:S(2)}) copy-start(f32[128,128]{1,0:T(8,128)} %param.22) | copy-start | bytes 196612
  7.2 144.9 %all-gather.4.cloned.1.call-start = ((), (), s32[]{:S(2)}) async-start(), calls=%async_computation.4 | async-start | bytes 4202496 | tf_op jit(solution)/shard_map/all_gather | solution.py:82
  37.3 15.2 %all-to-all-start.2 = ((f32[16,32,128]{2,0,1:T(8,128)}), f32[16,32,128]{2,0,1:T(8,128)S(1)}, u32[]{:S(2)}, u32[]{:S(2)}) async-start(f32[16,32,128]{2,0,1:T(8,128)} %copy.55), calls=%async_computation.2 | async-start | bytes 524288 | tf_op jit(solution)/shard_map/all_to_all | solution.py:50
  42.1 437.2 %all-reduce.5.cloned.1.call-start = ((), (), s32[]{:S(2)}) async-start(), calls=%async_computation.5 | async-start | bytes 9043968
  163.9 3.0 copy-start.8
  163.9 3.0 copy-start.10
  176.0 4.2 copy-start.1
  188.1 13.9 %copy-start.3 = (f32[128,128]{1,0:T(8,128)S(1)}, f32[128,128]{1,0:T(8,128)}, u32[]{:S(2)}) copy-start(f32[128,128]{1,0:T(8,128)} %param.17) | copy-start | bytes 196612
  189.1 13.3 %copy-start.4 = (f32[128,128]{1,0:T(8,128)S(1)}, f32[128,128]{1,0:T(8,128)}, u32[]{:S(2)}) copy-start(f32[128,128]{1,0:T(8,128)} %param.18) | copy-start | bytes 196612
  191.4 11.4 %copy-start.5 = (f32[128,128]{1,0:T(8,128)S(1)}, f32[128,128]{1,0:T(8,128)}, u32[]{:S(2)}) copy-start(f32[128,128]{1,0:T(8,128)} %param.19) | copy-start | bytes 196612
  193.8 285.4 %copy-start.9 = (f32[4,128]{1,0:T(4,128)S(1)}, f32[4,128]{1,0:T(4,128)}, u32[]{:S(2)}) copy-start(f32[4,128]{1,0:T(4,128)} %param.23) | copy-start | bytes 6148
  195.2 19.1 %all-to-all-start.1 = ((f32[512,1,128]{2,1,0:T(1,128)}), f32[512,1,128]{2,1,0:T(1,128)S(1)}, u32[]{:S(2)}, u32[]{:S(2)}) async-start(f32[512,1,128]{2,1,0:T(1,128)} %bitcast.22), calls=%async_computation.1 | async-start | bytes 524288 | tf_op jit(solution)/shard_map/all_to_all | solution.py:96
  479.3 111.3 %copy-start.6 = (f32[128,128]{1,0:T(8,128)S(1)}, f32[128,128]{1,0:T(8,128)}, u32[]{:S(2)}) copy-start(f32[128,128]{1,0:T(8,128)} %get-tuple-element.40) | copy-start | bytes 196612
  479.3 111.3 %copy-start.7 = (f32[128,128]{1,0:T(8,128)S(1)}, f32[128,128]{1,0:T(8,128)}, u32[]{:S(2)}) copy-start(f32[128,128]{1,0:T(8,128)} %get-tuple-element.41) | copy-start | bytes 196612
  582.9 16.6 %all-to-all-start.3 = ((f32[512,1,128]{2,1,0:T(1,128)}), f32[512,1,128]{2,1,0:T(1,128)S(1)}, u32[]{:S(2)}, u32[]{:S(2)}) async-start(f32[512,1,128]{2,1,0:T(1,128)} %copy.60), calls=%async_computation.3 | async-start | bytes 524288 | tf_op jit(solution)/shard_map/all_to_all | solution.py:140
Sparse Core Ops, SparseCore 0:
  35.6 116.4 all-gather.3
  194.0 285.2 all-reduce.4
where the time goes:
time: 608 us; the launch traced here: 607 us
  waiting for transfers between devices  385 us (63%)
  blocking collectives  123 us (20%)
  matrix products  38.7 us (6%)
  local copies, waits for them, and re-layouts  20.6 us (3%)
  starting transfers between devices  17.2 us (3%)
  between operations  14.4 us (2%)
  other arithmetic  8.93 us (1%)
    unnamed x3, waiting for transfers between devices  264 us
    all_gather x1, waiting for transfers between devices, body(): bias_rows = lax.all_gather(bias_piece, ('col', 'row'), axis=0, tiled=True)  99.2 us
    psum x1, blocking collectives, body(): lax.psum((grad_query_w, grad_key_w, grad_value_w, grad_gate_w, grad_gate_...  97.9 us
    all_to_all x1, blocking collectives, body(): lax.all_to_all(pair_rep, 'row', split_axis=1, concat_axis=0, tiled=True)  24.7 us
  transfers between devices with their start and end apart: 5, of which 5 were waited for; matrix products, arithmetic and copies ran while one was open for 3% of the time, Pallas kernels for 0%

commit v1 on v0

v1 whole, which is shorter than its diff:
```python
import jax
import jax.numpy as jnp
from jax import lax
from jax.experimental import pallas as pl
from jax.experimental.pallas import tpu as pltpu
from jax.sharding import Mesh, PartitionSpec as P

F32 = jnp.float32
BF16 = jnp.bfloat16
NEG_FILL = -1000000000.0
ROWS = ("z", "x")
COLS = ("y", "core")
VMEM_BYTES = 48 * 1024 * 1024
NN = (((1,), (0,)), ((), ()))
NT = (((1,), (1,)), ((), ()))


def bdot(left, right, dims=NN):
    return lax.dot_general(left, right, dims, preferred_element_type=F32)


def split(value):
    high = value.astype(BF16)
    return high, (value - high.astype(F32)).astype(BF16)


def dot3(left, right, dims=NN):
    lh, ll = left if isinstance(left, tuple) else split(left)
    rh, rl = right if isinstance(right, tuple) else split(right)
    return bdot(lh, rh, dims) + (bdot(ll, rh, dims) + bdot(lh, rl, dims))


def lanes_of(shape):
    return lax.broadcasted_iota(jnp.int32, shape, 1)


def turn(value, amount):
    amount = amount % value.shape[1]
    return value if amount == 0 else pltpu.roll(value, amount, 1)


def head_weights(wq, wk, wv, wg, head, factor):
    lane = lanes_of(wq.shape)
    at = 32 * head
    out = jnp.where(lane < 32, turn(wq, -at) * factor, turn(wk, 32 - at))
    out = jnp.where(lane < 64, out, turn(wv, 64 - at))
    return jnp.where(lane < 96, out, turn(wg, 96 - at))


def project_kernel(
    factor, x_ref, cot_ref, gain_ref, wq_ref, wk_ref, wv_ref, wg_ref, gb_ref, wo_ref, wb_ref,
    send_ref, scaled_ref, inv_ref, gate_ref, dgated_ref,
):
    cells = jnp.swapaxes(x_ref[...], 0, 1).reshape(512, 128)
    cot = jnp.swapaxes(cot_ref[...], 0, 1).reshape(512, 128)
    center = jnp.mean(cells, axis=1, keepdims=True)
    shifted = cells - center
    spread = jnp.mean(shifted * shifted, axis=1, keepdims=True)
    inverse = lax.rsqrt(spread + 1e-05)
    scaled = shifted * inverse
    scaled_ref[...] = scaled
    inv_ref[...] = jnp.broadcast_to(inverse, (512, 128))
    normed = split(scaled * gain_ref[...])
    wq, wk, wv, wg = wq_ref[...], wk_ref[...], wv_ref[...], wg_ref[...]
    gate = jax.nn.sigmoid(dot3(normed, wg) + gb_ref[...])
    d_gated = dot3(cot, wo_ref[...], NT)
    gate_ref[...] = gate
    dgated_ref[...] = d_gated
    d_att = d_gated * gate
    bias = dot3(wb_ref[...], normed, NT)
    lane = lanes_of((512, 128))
    for head in range(4):
        weights = head_weights(wq, wk, wv, wg, head, factor)
        block = jnp.where(lane < 96, dot3(normed, weights), turn(d_att, 96 - 32 * head))
        send_ref[:, head, 0:64, :] = block.reshape(8, 64, 128)
        for part in range(4):
            row = bias[head : head + 1, part * 128 : (part + 1) * 128]
            send_ref[:, head, 64 + part, :] = jnp.broadcast_to(row, (8, 128))
        send_ref[:, head, 68:72, :] = jnp.zeros((8, 4, 128), F32)


def spread_lanes(value, group):
    lane = lanes_of(value.shape)
    kept = jnp.where((lane >= 32 * group) & (lane < 32 * group + 32), value, 0.0)
    kept = kept + pltpu.roll(kept, 32, 1)
    return kept + pltpu.roll(kept, 64, 1)


def parts_of(value):
    high = value.astype(BF16).astype(F32)
    return high, value - high


def attend_kernel(keep_ref, data_ref, bias_ref, out_ref, db_ref):
    column = pl.program_id(0)
    chunk = 256

    @pl.when(column == 0)
    def _():
        db_ref[...] = jnp.zeros_like(db_ref)

    data = data_ref[...].reshape(512, 128)
    lane = lanes_of((512, 128))
    odd = (lane // 32) % 2 == 1
    qh, ql = parts_of(spread_lanes(data, 0))
    kh, kl = parts_of(spread_lanes(data, 1))
    vh, vl = parts_of(spread_lanes(data, 2))
    q_left = jnp.where(odd, ql, qh)
    q_left16 = q_left.astype(BF16)
    k_right = jnp.where(lane < 64, kh, kl).astype(BF16)
    v_right = jnp.where(lane < 64, vh, vl).astype(BF16)
    k_first = jnp.where(lane < 32, kh, 0.0).astype(BF16)
    k_both = jnp.where(lane < 32, kh, jnp.where(lane < 64, kl, 0.0)).astype(BF16)
    v_first = jnp.where(lane >= 96, vh, 0.0).astype(BF16)
    v_both = jnp.where(lane >= 96, vh, jnp.where(lane >= 64, vl, 0.0)).astype(BF16)
    keep = keep_ref[pl.ds(column, 1), :] > 0
    dk_t = jnp.zeros((32, 512), F32)
    dv_t = jnp.zeros((32, 512), F32)
    heads = []
    for at in range(0, 512, chunk):
        rows = slice(at, at + chunk)
        pieces = [(core, y) for y in range(at // 64, (at + chunk) // 64) for core in range(2)]
        bias = jnp.concatenate([bias_ref[core, y] for core, y in pieces], axis=0)
        scores = bdot(q_left16[rows], k_right, NT) + bias
        scores = jnp.where(keep, scores, NEG_FILL)
        highest = jnp.max(scores, axis=1, keepdims=True)
        weights = jnp.exp(scores - highest)
        inv_total = 1.0 / jnp.sum(weights, axis=1, keepdims=True)
        wh, wl = split(weights)
        output = bdot(wh, v_both) + bdot(wl, v_first)
        sub = lanes_of((chunk, 128))
        output = (output + pltpu.roll(output, 32, 1)) * inv_total
        d_out = jnp.where(sub >= 96, data[rows], 0.0) * inv_total
        centred = jnp.sum(d_out * output, axis=1, keepdims=True)
        dh, dl = parts_of(spread_lanes(d_out, 3))
        d_left = jnp.where((sub // 32) % 2 == 1, dl, dh)
        d_scores = weights * (bdot(d_left.astype(BF16), v_right, NT) - centred)
        for place, (core, y) in enumerate(pieces):
            db_ref[core, y] += d_scores[place * 32 : (place + 1) * 32]
        sh, sl = split(d_scores)
        d_query = bdot(sh, k_both) + bdot(sl, k_first)
        d_query = d_query + pltpu.roll(d_query, 96, 1)
        heads.append(jnp.where(sub < 32, d_query, output))
        q_t = jnp.transpose(q_left[rows])[0:64].astype(BF16)
        d_t = jnp.transpose(d_left)[0:64].astype(BF16)
        both = bdot(q_t, sh)
        dk_t = dk_t + (both[0:32] + both[32:64] + bdot(q_t[0:32], sl))
        both = bdot(d_t, wh)
        dv_t = dv_t + (both[0:32] + both[32:64] + bdot(d_t[0:32], wl))
    zeros = jnp.zeros((32, 512), F32)
    turned = jnp.transpose(jnp.concatenate([zeros, dk_t, dv_t, zeros], axis=0))
    result = jnp.where(
        (lane >= 32) & (lane < 96), turned, jnp.concatenate(heads, axis=0)
    )
    out_ref[...] = result.reshape(32, 16, 128)


def block_kernel(
    factor, recv_ref, scaled_ref, gate_ref, dgated_ref, cot_ref, wq_ref, wk_ref, wv_ref, wg_ref, wo_ref,
    update_ref, dnorm_ref, param_ref, shift_ref,
):
    lane = lanes_of((512, 128))
    scaled = scaled_ref[...]
    gate = gate_ref[...]
    cot = jnp.swapaxes(cot_ref[...], 0, 1).reshape(512, 128)
    wq, wk, wv, wg = wq_ref[...], wk_ref[...], wv_ref[...], wg_ref[...]
    got = [recv_ref[:, head].reshape(512, 128) for head in range(4)]
    att = turn(got[3], 0)
    for head in range(3):
        moved = turn(got[head], 32 * head - 96)
        att = jnp.where((lane >= 32 * head) & (lane < 32 * head + 32), moved, att)
    gated = gate * att
    d_pre = dgated_ref[...] * att * gate * (1.0 - gate)
    shift_ref[...] = jnp.broadcast_to(jnp.sum(d_pre, axis=0, keepdims=True), (8, 128))
    update = dot3(gated, wo_ref[...])
    update_ref[...] = jnp.swapaxes(update.reshape(32, 16, 128), 0, 1)
    scaled_t = split(jnp.transpose(scaled))
    d_normed = jnp.zeros((512, 128), F32)
    for head in range(4):
        grads = split(jnp.where(lane < 96, got[head], turn(d_pre, 96 - 32 * head)))
        weights = head_weights(wq, wk, wv, wg, head, factor)
        d_normed = d_normed + dot3(grads, weights, NT)
        param_ref[head * 128 : (head + 1) * 128, :] = dot3(scaled_t, grads)
    param_ref[512:640, :] = dot3(jnp.transpose(gated), cot)
    dnorm_ref[...] = d_normed


def norm_kernel(
    recv_ref, dnorm_ref, scaled_ref, inv_ref, gain_ref, wb_ref, shift_ref, grad_ref, send_ref
):
    chunk = jnp.sum(recv_ref[:, 0:20, :], axis=0)
    rows = []
    for head in range(4):
        pieces = recv_ref[head, 20:24, :]
        for z in range(1, 8):
            pieces = pieces + recv_ref[z * 4 + head, 20:24, :]
        rows.append(jnp.concatenate([pieces[a : a + 1] for a in range(4)], axis=1))
    bias_t = jnp.concatenate(rows + [jnp.zeros((4, 512), F32)], axis=0)
    scaled = scaled_ref[...]
    wide = jnp.concatenate([bias_t, jnp.zeros((120, 512), F32)], axis=0)
    wb = jnp.concatenate([wb_ref[...], jnp.zeros((120, 128), F32)], axis=0)
    d_normed = dnorm_ref[...] + dot3(jnp.transpose(wide), wb)
    d_scaled = d_normed * gain_ref[...]
    mean_term = jnp.mean(d_scaled, axis=1, keepdims=True)
    cross_term = jnp.mean(d_scaled * scaled, axis=1, keepdims=True)
    d_input = inv_ref[...] * (d_scaled - mean_term - scaled * cross_term)
    grad_ref[...] = jnp.swapaxes(d_input.reshape(32, 16, 128), 0, 1)
    bias_w = dot3(bias_t, scaled)
    tail = jnp.concatenate(
        [chunk, bias_w[0:4], shift_ref[0:1], jnp.zeros((7, 128), F32)], axis=0
    )
    send_ref[...] = jnp.broadcast_to(tail[None], (16, 32, 128))


def share_kernel(recv_ref, send_ref):
    total = jnp.sum(recv_ref[...], axis=0)
    send_ref[...] = jnp.broadcast_to(total[None], (32, 32, 128))


def finish_kernel(
    factor, count, recv_ref, gain_ref, wq_ref, wk_ref, wv_ref, wg_ref, wb_ref,
    q_ref, k_ref, v_ref, g_ref, shift_ref, o_ref, b_ref, gain_out_ref, hold,
):
    for place in range(32):
        hold[place * 20 : (place + 1) * 20, :] = recv_ref[place, 0:20, :]
    rest = jnp.sum(recv_ref[:, 20:32, :], axis=0)
    wq, wk, wv, wg = wq_ref[...], wk_ref[...], wv_ref[...], wg_ref[...]
    lane = lanes_of((128, 128))
    gain_rows = jnp.transpose(jnp.broadcast_to(gain_ref[...], (128, 128)))
    blocks = [hold[head * 128 : (head + 1) * 128, :] for head in range(4)]
    scale = 1.0 / count
    gain_sum = jnp.zeros((128, 128), F32)
    for head in range(4):
        gain_sum = gain_sum + blocks[head] * head_weights(wq, wk, wv, wg, head, factor)
    for ref, group, times in ((q_ref, 0, factor), (k_ref, 1, 1.0), (v_ref, 2, 1.0), (g_ref, 3, 1.0)):
        full = turn(blocks[0], -32 * group)
        for head in range(1, 4):
            full = jnp.where(lane >= 32 * head, turn(blocks[head], 32 * (head - group)), full)
        ref[...] = full * gain_rows * (times * scale)
    o_ref[...] = hold[512:640, :] * scale
    b_ref[...] = rest[0:4] * gain_ref[...] * scale
    shift_ref[...] = rest[4:5] * scale
    gain_total = jnp.sum(jnp.transpose(gain_sum), axis=0, keepdims=True)
    gain_total = gain_total + jnp.sum(rest[0:4] * wb_ref[0:4], axis=0, keepdims=True)
    gain_out_ref[...] = gain_total * scale


def call(kernel, out_shape, name, **extra):
    return pl.pallas_call(
        kernel,
        out_shape=out_shape,
        name=name,
        compiler_params=pltpu.CompilerParams(vmem_limit_bytes=VMEM_BYTES),
        **extra,
    )


def shaped(*shape):
    return jax.ShapeDtypeStruct(shape, F32)


def swap(value, axes):
    return lax.all_to_all(value, axes, 0, 0, tiled=False)


def body(
    pair_rep, cotangent, chain_ids, template, norm_gain, w_query, w_key, w_value, w_gate, gate_bias, w_out, w_bias,
):
    factor = 32 ** (-0.5)
    tokens = chain_ids.shape[0]
    gain = norm_gain.reshape(1, 128)
    wb = jnp.concatenate([w_bias, jnp.zeros((4, 128), F32)], axis=0)

    send, scaled, inverse, gate, d_gated = call(
        lambda *refs: project_kernel(factor, *refs),
        [shaped(8, 4, 72, 128)] + [shaped(512, 128)] * 4,
        "project",
    )(pair_rep, cotangent, gain, w_query, w_key, w_value, w_gate, gate_bias.reshape(1, 128), w_out, wb)

    data = swap(send.reshape(32, 72, 128), ROWS)
    piece = data[:, 64:68, :].reshape(32, 32, 16)
    piece = jnp.transpose(piece, (1, 0, 2)).reshape(1, 32, 512)
    by_y = swap(jnp.broadcast_to(piece, (8, 32, 512)), "y")
    bias = swap(jnp.broadcast_to(by_y[None], (2, 8, 32, 512)), "core")

    first = (lax.axis_index("y") * 2 + lax.axis_index("core")) * 32 + lax.axis_index("z") * 4
    own_chain = lax.dynamic_slice_in_dim(chain_ids, first, 4, 0)
    own_block = lax.dynamic_slice_in_dim(template, first // 64, 1, 1)
    block_keep = jnp.broadcast_to(own_block, (8, 64)).reshape(1, 512) > 0
    keep = ((own_chain[:, None] == chain_ids[None, :]) | block_keep).astype(jnp.int32)

    back, d_bias = pl.pallas_call(
        attend_kernel,
        grid=(4,),
        in_specs=[
            pl.BlockSpec((4, 512), lambda j: (0, 0)),
            pl.BlockSpec((32, 16, 128), lambda j: (0, j, 0)),
            pl.BlockSpec((2, 8, 32, 512), lambda j: (0, 0, 0, 0)),
        ],
        out_specs=[
            pl.BlockSpec((32, 16, 128), lambda j: (0, j, 0)),
            pl.BlockSpec((2, 8, 32, 512), lambda j: (0, 0, 0, 0)),
        ],
        out_shape=[shaped(32, 64, 128), shaped(2, 8, 32, 512)],
        name="attend",
        compiler_params=pltpu.CompilerParams(vmem_limit_bytes=VMEM_BYTES),
    )(keep, data, bias)

    got = swap(back, ROWS)
    d_bias = jnp.sum(swap(d_bias, "core"), axis=0)
    d_bias = jnp.sum(swap(d_bias, "y"), axis=0)
    d_bias = jnp.transpose(d_bias.reshape(32, 32, 16), (1, 0, 2)).reshape(32, 4, 128)

    update, d_normed, params, d_shift = call(
        lambda *refs: block_kernel(factor, *refs),
        [shaped(16, 32, 128), shaped(512, 128), shaped(640, 128), shaped(8, 128)],
        "block_grads",
    )(got.reshape(8, 4, 64, 128), scaled, gate, d_gated, cotangent, w_query, w_key, w_value, w_gate, w_out)

    small = swap(jnp.concatenate([params.reshape(32, 20, 128), d_bias], axis=1), ROWS)
    grad_pair, tail = call(norm_kernel, [shaped(16, 32, 128), shaped(16, 32, 128)], "norm_back")(
        small, d_normed, scaled, inverse, gain, wb, d_shift
    )
    tail = swap(tail, COLS)
    tail = call(share_kernel, shaped(32, 32, 128), "share")(tail)
    tail = swap(tail, ROWS)
    square = shaped(128, 128)
    grads = call(
        lambda *refs: finish_kernel(factor, float(tokens), *refs),
        [square, square, square, square, shaped(1, 128), square, shaped(4, 128), shaped(1, 128)],
        "finish",
        scratch_shapes=[pltpu.VMEM((640, 128), F32)],
    )(tail, gain, w_query, w_key, w_value, w_gate, wb)
    gq, gk, gv, gg, gshift, go, gb, ggain = grads
    return update, grad_pair, gq, gk, gv, gg, gshift.reshape(128), go, gb, ggain.reshape(128)


def solution(mesh):
    fine = Mesh(mesh.devices.reshape(8, 2, 8, 4), ("y", "core", "z", "x"))
    block = P(ROWS, COLS, None)
    return jax.shard_map(
        body,
        mesh=fine,
        in_specs=(block, block) + (P(),) * 10,
        out_specs=(block, block) + (P(),) * 8,
        check_vma=False,
    )
```

time: 608 us -> 218 us (0.36)
  waiting for transfers between devices: 385 us -> 39.4 us
  matrix products: 38.7 us -> 0 us
  Pallas kernels: 0 us -> 19 us
  between operations: 14.4 us -> 0.86 us
  blocking collectives: 123 us -> 136 us
  local copies, waits for them, and re-layouts: 20.6 us -> 10.3 us
  other arithmetic: 8.93 us -> 0.46 us
    unnamed x3 -> x0, waiting for transfers between devices: 264 us -> none
    all_to_all x1 -> x7, blocking collectives: 24.7 us -> 136 us  [swap(): return lax.all_to_all(value, axes, 0, 0, tiled=False)]
    all_gather x1 -> x0, waiting for transfers between devices: 99.2 us -> none  [body(): bias_rows = lax.all_gather(bias_piece, ('col', 'row'), axis=0, tiled=True)]
    psum x1 -> x0, blocking collectives: 97.9 us -> none  [body(): lax.psum((grad_query_w, grad_key_w, grad_value_w, grad_gate_w, grad_gate_...]
    dot_general x24 -> x0, matrix products: 38.7 us -> none  [the longest x15 10.9 us: matmul(): jnp.dot(left, right, precision=HIGHEST, preferred_element_type=jnp.float32)]
    pallas_call x0 -> x6, Pallas kernels: none -> 19 us  [the longest x1 13.2 us: body(): pl.pallas_call(attend_kernel, grid=(4,), in_specs=[pl.BlockSpec((4, 512),...]
    all_to_all x3 -> x2, waiting for transfers between devices: 21.3 us -> 39.4 us  [swap(): return lax.all_to_all(value, axes, 0, 0, tiled=False)]
    all_to_all x3 -> x2, starting transfers between devices: 17.1 us -> 11.4 us  [swap(): return lax.all_to_all(value, axes, 0, 0, tiled=False)]
  transfers between devices with their start and end apart: 5 -> 2, of which waited for: 5 -> 2; matrix products, arithmetic and copies ran while one was open for 3% -> 0% of each run, Pallas kernels for 0% -> 0%
where the time goes in v1:
time: 218 us; the launch traced here: 217 us
  blocking collectives  136 us (62%)
  waiting for transfers between devices  39.4 us (18%)
  Pallas kernels  19 us (9%)
  starting transfers between devices  11.4 us (5%)
  local copies, waits for them, and re-layouts  10.3 us (5%)
    all_to_all x7, blocking collectives, swap(): return lax.all_to_all(value, axes, 0, 0, tiled=False)  136 us
    all_to_all x2, waiting for transfers between devices, swap(): return lax.all_to_all(value, axes, 0, 0, tiled=False)  39.4 us
    pallas_call x1, Pallas kernels, body(): pl.pallas_call(attend_kernel, grid=(4,), in_specs=[pl.BlockSpec((4, 512),...  13.2 us
    all_to_all x2, starting transfers between devices, swap(): return lax.all_to_all(value, axes, 0, 0, tiled=False)  11.4 us
    unnamed x36, local copies, waits for them, and re-layouts  7.46 us
  transfers between devices with their start and end apart: 2, of which 2 were waited for; matrix products, arithmetic and copies ran while one was open for 0% of the time, Pallas kernels for 0%

profile of v1, /device:TPU:1, one launch (start us, length us, event | category | flops | bytes accessed | tf_op | source)
XLA Modules:
  0.0 217.4 jit_solution(17620169549432245473)
XLA Ops:
  0.6 0.7 concatenate.6.refs_9_.wb_ref.refs_6_
  1.3 0.9 copy-done
  2.3 0.8 copy-done.2
  3.1 0.8 copy-done.4
  4.0 0.8 copy-done.6
  4.8 0.8 copy-done.8
  5.6 0.9 copy-done.10
  6.6 0.8 copy-done.11
  7.4 0.7 copy-done.13
  8.1 0.7 copy-done.15
  8.7 1.1 project.1
  9.8 44.6 %all_to_all.45.data_ref = f32[32,72,128]{2,1,0:T(8,128)S(1)} all-to-all(f32[32,72,128]{2,1,0:T(8,128)S(1)} %bitcast.15), channel_id=1, replica_groups=mesh['y'=8,'core'=2,'z'=8,'x'=4] {'z','x'}, dimensions={0} | all-to-all | bytes 2359296 | tf_op jit(solution)/shard_map/all_to_all | solution.py:263
  54.4 0.1 copy.27
  54.5 0.0 copy-start.16
  54.6 0.0 copy-start.17
  54.6 0.2 copy.28
  54.8 0.1 copy.29
  54.9 0.9 broadcast_in_dim.10
  55.7 6.8 %all-to-all-start.1 = ((f32[8,32,512]{2,1,0:T(8,128)}), f32[8,32,512]{2,1,0:T(8,128)S(1)}, u32[]{:S(2)}, u32[]{:S(2)}) async-start(f32[8,32,512]{2,1,0:T(8,128)} %broadcast_in_dim.10), calls=%async_computation.1 | async-start | bytes 1048576 | tf_op jit(solution)/shard_map/all_to_all | solution.py:263
  62.6 0.2 fusion
  62.8 0.1 broadcast_in_dim.8
  62.8 0.1 gt.21
  62.9 0.1 dynamic_slice.6
  63.0 0.1 or_convert_fusion.keep_ref
  63.1 13.7 %all-to-all-done.1 = f32[8,32,512]{2,1,0:T(8,128)S(1)} async-done(((f32[8,32,512]{2,1,0:T(8,128)}), f32[8,32,512]{2,1,0:T(8,128)S(1)}, u32[]{:S(2)}, u32[]{:S(2)}) %all-to-all-start.1) | async-done | bytes 524320 | tf_op jit(solution)/shard_map/all_to_all | solution.py:263
  76.8 0.1 broadcast_in_dim.11
  76.9 8.4 %all_to_all.46.bias_ref = f32[2,8,32,512]{3,2,1,0:T(8,128)S(1)} all-to-all(f32[2,8,32,512]{3,2,1,0:T(8,128)S(1)} %broadcast_in_dim.11), channel_id=1, replica_groups=mesh['y'=8,'core'=2,'z'=8,'x'=4] {'core'}, dimensions={0} | all-to-all | bytes 2097152 | tf_op jit(solution)/shard_map/all_to_all | solution.py:263
  85.4 13.2 %attend.1 = (f32[32,64,128]{2,1,0:T(8,128)}, f32[2,8,32,512]{3,2,1,0:T(8,128)S(1)}) custom-call(s32[4,512]{1,0:T(4,128)S(1)} %or_convert_fusion.keep_ref, f32[32,72,128]{2,1,0:T(8,128)S(1)} %all_to_all.45.data_ref, f32[2,8,32,512]{3,2,1,0:T(8,128)S(1)} %all_to_all.46.bias_ref), custom_call_target="tpu_custom_call" | custom-call | tf_op jit(solution)/shard_map/attend/pallas_call | solution.py:292
  98.5 4.6 %all_to_all.47 = f32[2,8,32,512]{3,2,1,0:T(8,128)S(1)} all-to-all(f32[2,8,32,512]{3,2,1,0:T(8,128)S(1)} %get-tuple-element.38), channel_id=1, replica_groups=mesh['y'=8,'core'=2,'z'=8,'x'=4] {'core'}, dimensions={0} | all-to-all | bytes 2097152 | tf_op jit(solution)/shard_map/all_to_all | solution.py:263
  103.1 0.1 reduce_sum.18
  103.2 20.4 %all_to_all.48 = f32[8,32,512]{2,1,0:T(8,128)S(1)} all-to-all(f32[8,32,512]{2,1,0:T(8,128)S(1)} %reduce_sum.18), channel_id=1, replica_groups=mesh['y'=8,'core'=2,'z'=8,'x'=4] {'y'}, dimensions={0} | all-to-all | bytes 1048576 | tf_op jit(solution)/shard_map/all_to_all | solution.py:263
  123.6 4.6 %all-to-all-start.3 = ((f32[32,64,128]{2,1,0:T(8,128)}), f32[32,64,128]{2,1,0:T(8,128)S(1)}, u32[]{:S(2)}, u32[]{:S(2)}) async-start(f32[32,64,128]{2,1,0:T(8,128)} %get-tuple-element.32), calls=%async_computation.3 | async-start | bytes 2097152 | tf_op jit(solution)/shard_map/all_to_all | solution.py:263
  128.2 0.0 copy-start.1
  128.2 0.0 copy-start.3
  128.2 0.0 copy-start.5
  128.2 0.0 copy-start.7
  128.2 0.0 copy-start.9
  128.3 0.1 copy.30
  128.4 0.2 copy.31
  128.6 0.1 copy.32
  128.8 25.6 %all-to-all-done.3 = f32[32,64,128]{2,1,0:T(8,128)S(1)} async-done(((f32[32,64,128]{2,1,0:T(8,128)}), f32[32,64,128]{2,1,0:T(8,128)S(1)}, u32[]{:S(2)}, u32[]{:S(2)}) %all-to-all-start.3) | async-done | bytes 1048608 | tf_op jit(solution)/shard_map/all_to_all | solution.py:263
  154.4 2.2 %block_grads.1 = (f32[16,32,128]{2,1,0:T(8,128)}, f32[512,128]{1,0:T(8,128)S(1)}, f32[640,128]{1,0:T(8,128)S(1)}, f32[8,128]{1,0:T(8,128)S(1)}) custom-call(f32[8,4,64,128]{3,2,1,0:T(8,128)S(1)} %bitcast.14, f32[512,128]{1,0:T(8,128)S(1)} %get-tuple-element.33.refs_1_.scaled_ref, f32[512,128]{1,0:T(8,128)S(1)} %get-tuple-element.34.refs_2_, ...), custom_call_target="tpu_custom_call" | custom-call | tf_op jit(solution)/shard_map/block_grads/pallas_call | solution.py:314
  156.7 19.3 %all_to_all.49.recv_ref = f32[32,24,128]{2,1,0:T(8,128)S(1)} all-to-all(f32[32,24,128]{2,1,0:T(8,128)S(1)} %pad_maximum_fusion), channel_id=1, replica_groups=mesh['y'=8,'core'=2,'z'=8,'x'=4] {'z','x'}, dimensions={0} | all-to-all | bytes 786432 | tf_op jit(solution)/shard_map/all_to_all | solution.py:263
  176.0 1.3 norm_back.1
  177.3 17.7 %all_to_all.50.recv_ref = f32[16,32,128]{2,1,0:T(8,128)S(1)} all-to-all(f32[16,32,128]{2,1,0:T(8,128)S(1)} %get-tuple-element.43), channel_id=1, replica_groups=mesh['y'=8,'core'=2,'z'=8,'x'=4] {'y','core'}, dimensions={0} | all-to-all | bytes 524288 | tf_op jit(solution)/shard_map/all_to_all | solution.py:263
  195.0 0.1 share.1
  195.1 21.2 %all_to_all.51.refs_0_ = f32[32,32,128]{2,1,0:T(8,128)S(1)} all-to-all(f32[32,32,128]{2,1,0:T(8,128)S(1)} %share.1), channel_id=1, replica_groups=mesh['y'=8,'core'=2,'z'=8,'x'=4] {'z','x'}, dimensions={0} | all-to-all | bytes 1048576 | tf_op jit(solution)/shard_map/all_to_all | solution.py:263
  216.2 1.2 finish.1
  (24 shorter events, 0.2 us)
Async XLA Ops:
  1.3 0.9 copy-start
  2.3 0.8 copy-start.2
  3.1 0.8 copy-start.4
  4.0 0.8 copy-start.6
  4.8 0.8 copy-start.8
  5.6 0.9 copy-start.10
  6.6 0.8 copy-start.11
  7.4 0.7 copy-start.13
  8.1 0.7 copy-start.15
  54.5 8.0 %copy-start.16 = (s32[8,8]{1,0:T(8,128)S(1)}, s32[8,8]{1,0:T(8,128)}, u32[]{:S(2)}) copy-start(s32[8,8]{1,0:T(8,128)} %param.15) | copy-start | bytes 772
  54.6 8.4 %copy-start.17 = (s32[512]{0:T(512)S(1)}, s32[512]{0:T(512)}, u32[]{:S(2)}) copy-start(s32[512]{0:T(512)} %param.14) | copy-start | bytes 6148
  55.7 21.1 %all-to-all-start.1 = ((f32[8,32,512]{2,1,0:T(8,128)}), f32[8,32,512]{2,1,0:T(8,128)S(1)}, u32[]{:S(2)}, u32[]{:S(2)}) async-start(f32[8,32,512]{2,1,0:T(8,128)} %broadcast_in_dim.10), calls=%async_computation.1 | async-start | bytes 1048576 | tf_op jit(solution)/shard_map/all_to_all | solution.py:263
  123.6 30.8 %all-to-all-start.3 = ((f32[32,64,128]{2,1,0:T(8,128)}), f32[32,64,128]{2,1,0:T(8,128)S(1)}, u32[]{:S(2)}, u32[]{:S(2)}) async-start(f32[32,64,128]{2,1,0:T(8,128)} %get-tuple-element.32), calls=%async_computation.3 | async-start | bytes 2097152 | tf_op jit(solution)/shard_map/all_to_all | solution.py:263
  128.2 26.2 %copy-start.1 = (f32[16,32,128]{2,1,0:T(8,128)S(1)}, f32[16,32,128]{2,1,0:T(8,128)}, u32[]{:S(2)}) copy-start(f32[16,32,128]{2,1,0:T(8,128)} %refs_4_.4) | copy-start | bytes 786436
  128.2 26.2 %copy-start.3 = (f32[128,128]{1,0:T(8,128)S(1)}, f32[128,128]{1,0:T(8,128)}, u32[]{:S(2)}) copy-start(f32[128,128]{1,0:T(8,128)} %refs_2_.1) | copy-start | bytes 196612
  128.2 26.2 %copy-start.5 = (f32[128,128]{1,0:T(8,128)S(1)}, f32[128,128]{1,0:T(8,128)}, u32[]{:S(2)}) copy-start(f32[128,128]{1,0:T(8,128)} %refs_3_.3) | copy-start | bytes 196612
  128.2 26.2 %copy-start.7 = (f32[128,128]{1,0:T(8,128)S(1)}, f32[128,128]{1,0:T(8,128)}, u32[]{:S(2)}) copy-start(f32[128,128]{1,0:T(8,128)} %refs_4_.5) | copy-start | bytes 196612
  128.2 26.2 %copy-start.9 = (f32[128,128]{1,0:T(8,128)S(1)}, f32[128,128]{1,0:T(8,128)}, u32[]{:S(2)}) copy-start(f32[128,128]{1,0:T(8,128)} %refs_5_.5) | copy-start | bytes 196612
  128.2 26.2 %copy-start.12 = (f32[128,128]{1,0:T(8,128)S(1)}, f32[128,128]{1,0:T(8,128)}, u32[]{:S(2)}) copy-start(f32[128,128]{1,0:T(8,128)} %refs_9_.1) | copy-start | bytes 196612
  156.6 19.4 %copy-start.14 = (f32[128]{0:T(128)S(1)}, f32[128]{0:T(128)}, u32[]{:S(2)}) copy-start(f32[128]{0:T(128)} %param.16) | copy-start | bytes 1540

commit v2 on v1

v2 whole, which is shorter than its diff:
```python
import jax
import jax.numpy as jnp
from jax import lax
from jax.experimental import pallas as pl
from jax.experimental.pallas import tpu as pltpu
from jax.sharding import Mesh, PartitionSpec as P

F32 = jnp.float32
BF16 = jnp.bfloat16
NEG_FILL = -1000000000.0
ROWS = ("z", "x")
COLS = ("y", "core")
VMEM_BYTES = 48 * 1024 * 1024
NN = (((1,), (0,)), ((), ()))
NT = (((1,), (1,)), ((), ()))


def bdot(left, right, dims=NN):
    return lax.dot_general(left, right, dims, preferred_element_type=F32)


def split(value):
    high = value.astype(BF16)
    return high, (value - high.astype(F32)).astype(BF16)


def dot3(left, right, dims=NN):
    lh, ll = left if isinstance(left, tuple) else split(left)
    rh, rl = right if isinstance(right, tuple) else split(right)
    return bdot(lh, rh, dims) + (bdot(ll, rh, dims) + bdot(lh, rl, dims))


def lanes_of(shape):
    return lax.broadcasted_iota(jnp.int32, shape, 1)


def turn(value, amount):
    amount = amount % value.shape[1]
    return value if amount == 0 else pltpu.roll(value, amount, 1)


def head_weights(wq, wk, wv, wg, head, factor):
    lane = lanes_of(wq.shape)
    at = 32 * head
    out = jnp.where(lane < 32, turn(wq, -at) * factor, turn(wk, 32 - at))
    out = jnp.where(lane < 64, out, turn(wv, 64 - at))
    return jnp.where(lane < 96, out, turn(wg, 96 - at))


def project_kernel(
    factor, x_in, cot_in, gain_in, wq_in, wk_in, wv_in, wg_in, gb_in, wo_in, wb_in,
    send_ref, piece_ref, scaled_ref, inv_ref, gate_ref, dgated_ref,
    x_ref, cot_ref, gain_ref, wq_ref, wk_ref, wv_ref, wg_ref, gb_ref, wo_ref, wb_ref, sems,
):
    sources = (x_in, gain_in, wb_in, wq_in, wk_in, wv_in, wg_in, gb_in, cot_in, wo_in)
    targets = (x_ref, gain_ref, wb_ref, wq_ref, wk_ref, wv_ref, wg_ref, gb_ref, cot_ref, wo_ref)
    copies = [
        pltpu.make_async_copy(source, target, sems.at[place])
        for place, (source, target) in enumerate(zip(sources, targets))
    ]
    for copy in copies:
        copy.start()
    for copy in copies:
        copy.wait()
    cells = jnp.swapaxes(x_ref[...], 0, 1).reshape(512, 128)
    cot = jnp.swapaxes(cot_ref[...], 0, 1).reshape(512, 128)
    center = jnp.mean(cells, axis=1, keepdims=True)
    shifted = cells - center
    spread = jnp.mean(shifted * shifted, axis=1, keepdims=True)
    inverse = lax.rsqrt(spread + 1e-05)
    scaled = shifted * inverse
    scaled_ref[...] = scaled
    inv_ref[...] = jnp.broadcast_to(inverse, (512, 128))
    normed = split(scaled * gain_ref[...])
    wq, wk, wv, wg = wq_ref[...], wk_ref[...], wv_ref[...], wg_ref[...]
    gate = jax.nn.sigmoid(dot3(normed, wg) + gb_ref[...])
    d_gated = dot3(cot, wo_ref[...], NT)
    gate_ref[...] = gate
    dgated_ref[...] = d_gated
    d_att = d_gated * gate
    wb = jnp.concatenate([wb_ref[...], jnp.zeros((4, 128), F32)], axis=0)
    bias = dot3(wb, normed, NT)
    lane = lanes_of((512, 128))
    for head in range(4):
        weights = head_weights(wq, wk, wv, wg, head, factor)
        block = jnp.where(lane < 96, dot3(normed, weights), turn(d_att, 96 - 32 * head))
        send_ref[:, head] = block.reshape(8, 64, 128)
        for part in range(4):
            row = bias[head : head + 1, part * 128 : (part + 1) * 128]
            piece_ref[:, head, part, :] = jnp.broadcast_to(row, (8, 128))


def spread_lanes(value, group):
    lane = lanes_of(value.shape)
    kept = jnp.where((lane >= 32 * group) & (lane < 32 * group + 32), value, 0.0)
    kept = kept + pltpu.roll(kept, 32, 1)
    return kept + pltpu.roll(kept, 64, 1)


def parts_of(value):
    high = value.astype(BF16).astype(F32)
    return high, value - high


def attend_kernel(place_ref, keep_ref, data_ref, own_ref, other_ref, out_ref, d_own_ref, d_other_ref):
    column = pl.program_id(0)
    y, core = place_ref[0], place_ref[1]

    @pl.when(column == 0)
    def _():
        d_own_ref[...] = jnp.zeros_like(d_own_ref)
        d_other_ref[...] = jnp.zeros_like(d_other_ref)

    data = data_ref[...].reshape(512, 128)
    lane = lanes_of((512, 128))
    kh, kl = parts_of(spread_lanes(data, 1))
    vh, vl = parts_of(spread_lanes(data, 2))
    k_right = jnp.where(lane < 64, kh, kl).astype(BF16)
    v_right = jnp.where(lane < 64, vh, vl).astype(BF16)
    k_first = jnp.where(lane < 32, kh, 0.0).astype(BF16)
    k_both = jnp.where(lane < 32, kh, jnp.where(lane < 64, kl, 0.0)).astype(BF16)
    v_first = jnp.where(lane >= 96, vh, 0.0).astype(BF16)
    v_both = jnp.where(lane >= 96, vh, jnp.where(lane >= 64, vl, 0.0)).astype(BF16)
    keep = keep_ref[pl.ds(column, 1), :] > 0
    sub = lanes_of((256, 128))
    odd = (sub // 32) % 2 == 1
    turned = []
    halves = []
    for side, (bias_ref, db_ref) in enumerate(((own_ref, d_own_ref), (other_ref, d_other_ref))):
        half = core if side == 0 else 1 - core
        starts = [(y ^ ((s >> 2) | (s & 2) | ((s & 1) << 2))) * 4 + half * 2 for s in range(8)]
        rows = jnp.concatenate([data_ref[pl.ds(start, 2)].reshape(32, 128) for start in starts], axis=0)
        qh, ql = parts_of(spread_lanes(rows, 0))
        q_left = jnp.where(odd, ql, qh)
        scores = bdot(q_left.astype(BF16), k_right, NT) + bias_ref[...].reshape(256, 512)
        scores = jnp.where(keep, scores, NEG_FILL)
        highest = jnp.max(scores, axis=1, keepdims=True)
        weights = jnp.exp(scores - highest)
        inv_total = 1.0 / jnp.sum(weights, axis=1, keepdims=True)
        wh, wl = split(weights)
        output = bdot(wh, v_both) + bdot(wl, v_first)
        output = (output + pltpu.roll(output, 32, 1)) * inv_total
        d_out = jnp.where(sub >= 96, rows, 0.0) * inv_total
        centred = jnp.sum(d_out * output, axis=1, keepdims=True)
        dh, dl = parts_of(spread_lanes(d_out, 3))
        d_left = jnp.where(odd, dl, dh)
        d_scores = weights * (bdot(d_left.astype(BF16), v_right, NT) - centred)
        db_ref[...] += d_scores.reshape(8, 32, 512)
        sh, sl = split(d_scores)
        d_query = bdot(sh, k_both) + bdot(sl, k_first)
        d_query = d_query + pltpu.roll(d_query, 96, 1)
        halves.append((starts, jnp.where(sub < 32, d_query, output)))
        q_t = jnp.transpose(q_left)[0:64].astype(BF16)
        d_t = jnp.transpose(d_left)[0:64].astype(BF16)
        both = bdot(q_t, sh)
        dk_t = both[0:32] + both[32:64] + bdot(q_t[0:32], sl)
        both = bdot(d_t, wh)
        dv_t = both[0:32] + both[32:64] + bdot(d_t[0:32], wl)
        turned.append((dk_t, dv_t))
    zeros = jnp.zeros((32, 512), F32)
    dk_t = turned[0][0] + turned[1][0]
    dv_t = turned[0][1] + turned[1][1]
    result = jnp.transpose(jnp.concatenate([zeros, dk_t, dv_t, zeros], axis=0))
    out_ref[...] = result.reshape(32, 16, 128)
    mixed = (sub >= 32) & (sub < 96)
    for starts, value in halves:
        held = jnp.concatenate([out_ref[pl.ds(start, 2)].reshape(32, 128) for start in starts], axis=0)
        value = jnp.where(mixed, held, value)
        for s, start in enumerate(starts):
            out_ref[pl.ds(start, 2)] = value[s * 32 : (s + 1) * 32].reshape(2, 16, 128)


def block_kernel(
    factor, recv_ref, scaled_ref, gate_ref, dgated_ref, cot_ref, wq_ref, wk_ref, wv_ref, wg_ref, wo_ref,
    update_ref, dnorm_ref, param_ref,
):
    lane = lanes_of((512, 128))
    scaled = scaled_ref[...]
    gate = gate_ref[...]
    cot = jnp.swapaxes(cot_ref[...], 0, 1).reshape(512, 128)
    wq, wk, wv, wg = wq_ref[...], wk_ref[...], wv_ref[...], wg_ref[...]
    got = [recv_ref[:, head].reshape(512, 128) for head in range(4)]
    att = turn(got[3], 0)
    for head in range(3):
        moved = turn(got[head], 32 * head - 96)
        att = jnp.where((lane >= 32 * head) & (lane < 32 * head + 32), moved, att)
    gated = gate * att
    d_pre = dgated_ref[...] * att * gate * (1.0 - gate)
    update = dot3(gated, wo_ref[...])
    update_ref[...] = jnp.swapaxes(update.reshape(32, 16, 128), 0, 1)
    scaled_t = split(jnp.transpose(jnp.where(lane == 127, 1.0, scaled)))
    d_normed = jnp.zeros((512, 128), F32)
    for head in range(4):
        grads = split(jnp.where(lane < 96, got[head], turn(d_pre, 96 - 32 * head)))
        weights = head_weights(wq, wk, wv, wg, head, factor)
        d_normed = d_normed + dot3(grads, weights, NT)
        param_ref[head * 128 : (head + 1) * 128, :] = dot3(scaled_t, grads)
    param_ref[512:640, :] = dot3(jnp.transpose(gated), cot)
    dnorm_ref[...] = d_normed


def norm_kernel(
    recv_ref, dnorm_ref, scaled_ref, inv_ref, gain_ref, wb_ref, grad_ref, send_ref
):
    chunk = jnp.sum(recv_ref[:, 0:20, :], axis=0)
    rows = []
    for head in range(4):
        pieces = recv_ref[head, 20:24, :]
        for z in range(1, 8):
            pieces = pieces + recv_ref[z * 4 + head, 20:24, :]
        rows.append(jnp.concatenate([pieces[a : a + 1] for a in range(4)], axis=1))
    bias_t = jnp.concatenate(rows + [jnp.zeros((4, 512), F32)], axis=0)
    scaled = scaled_ref[...]
    wide = jnp.concatenate([bias_t, jnp.zeros((120, 512), F32)], axis=0)
    wb = jnp.concatenate([wb_ref[...], jnp.zeros((124, 128), F32)], axis=0)
    d_normed = dnorm_ref[...] + dot3(jnp.transpose(wide), wb)
    d_scaled = d_normed * gain_ref[...]
    mean_term = jnp.mean(d_scaled, axis=1, keepdims=True)
    cross_term = jnp.mean(d_scaled * scaled, axis=1, keepdims=True)
    d_input = inv_ref[...] * (d_scaled - mean_term - scaled * cross_term)
    grad_ref[...] = jnp.swapaxes(d_input.reshape(32, 16, 128), 0, 1)
    bias_w = dot3(bias_t, scaled)
    tail = jnp.concatenate([chunk, bias_w[0:4]], axis=0)
    send_ref[...] = jnp.broadcast_to(tail[None], (16, 24, 128))


def share_kernel(recv_ref, send_ref):
    total = jnp.sum(recv_ref[...], axis=0)
    send_ref[...] = jnp.broadcast_to(total[None], (32, 24, 128))


def finish_kernel(
    factor, count, recv_ref, gain_ref, wq_ref, wk_ref, wv_ref, wg_ref, wb_ref,
    q_ref, k_ref, v_ref, g_ref, shift_ref, o_ref, b_ref, gain_out_ref, hold,
):
    for place in range(32):
        hold[place * 20 : (place + 1) * 20, :] = recv_ref[place, 0:20, :]
    bias_w = jnp.sum(recv_ref[:, 20:24, :], axis=0)
    wq, wk, wv, wg = wq_ref[...], wk_ref[...], wv_ref[...], wg_ref[...]
    lane = lanes_of((128, 128))
    gain_rows = jnp.transpose(jnp.broadcast_to(gain_ref[...], (128, 128)))
    last = lax.broadcasted_iota(jnp.int32, (128, 128), 0) == 127
    scale = 1.0 / count
    blocks = []
    shift = jnp.zeros((1, 128), F32)
    for head in range(4):
        block = hold[head * 128 : (head + 1) * 128, :]
        sums = turn(block[127:128], 32 * head - 96)
        shift = jnp.where((lane[0:1] >= 32 * head) & (lane[0:1] < 32 * head + 32), sums, shift)
        block = jnp.where(last, 0.0, block)
        blocks.append(jnp.where(last, -jnp.sum(block, axis=0, keepdims=True), block))
    gain_sum = jnp.zeros((128, 128), F32)
    for head in range(4):
        gain_sum = gain_sum + blocks[head] * head_weights(wq, wk, wv, wg, head, factor)
    for ref, group, times in ((q_ref, 0, factor), (k_ref, 1, 1.0), (v_ref, 2, 1.0), (g_ref, 3, 1.0)):
        full = turn(blocks[0], -32 * group)
        for head in range(1, 4):
            full = jnp.where(lane >= 32 * head, turn(blocks[head], 32 * (head - group)), full)
        ref[...] = full * gain_rows * (times * scale)
    o_ref[...] = hold[512:640, :] * scale
    b_ref[...] = bias_w * gain_ref[...] * scale
    shift_ref[...] = shift * scale
    gain_total = jnp.sum(jnp.transpose(gain_sum), axis=0, keepdims=True)
    gain_total = gain_total + jnp.sum(bias_w * wb_ref[...], axis=0, keepdims=True)
    gain_out_ref[...] = gain_total * scale


def call(kernel, out_shape, name, **extra):
    return pl.pallas_call(
        kernel,
        out_shape=out_shape,
        name=name,
        compiler_params=pltpu.CompilerParams(vmem_limit_bytes=VMEM_BYTES),
        **extra,
    )


def shaped(*shape):
    return jax.ShapeDtypeStruct(shape, F32)


def swap(value, axes):
    return lax.all_to_all(value, axes, 0, 0, tiled=False)


def partner(value, axis, flip):
    return lax.ppermute(value, axis, [(at, at ^ flip) for at in range(lax.axis_size(axis))])


def body(
    pair_rep, cotangent, chain_ids, template, norm_gain, w_query, w_key, w_value, w_gate, gate_bias, w_out, w_bias,
):
    factor = 32 ** (-0.5)
    tokens = chain_ids.shape[0]
    gain = norm_gain.reshape(1, 128)
    square = shaped(128, 128)
    row = shaped(1, 128)
    here = [shaped(16, 32, 128)] * 2 + [row] + [square] * 4 + [row, square, shaped(4, 128)]

    send, piece, scaled, inverse, gate, d_gated = call(
        lambda *refs: project_kernel(factor, *refs),
        [shaped(8, 4, 64, 128), shaped(8, 4, 4, 128)] + [shaped(512, 128)] * 4,
        "project",
        in_specs=[pl.BlockSpec(memory_space=pltpu.HBM)] * 10,
        scratch_shapes=[pltpu.VMEM(part.shape, F32) for part in here] + [pltpu.SemaphoreType.DMA((10,))],
    )(pair_rep, cotangent, gain, w_query, w_key, w_value, w_gate, gate_bias.reshape(1, 128), w_out, w_bias)

    piece = swap(piece.reshape(32, 4, 128), ROWS)
    piece, send = lax.optimization_barrier((piece, send))
    data = swap(send.reshape(32, 64, 128), ROWS)
    own = jnp.transpose(piece.reshape(32, 32, 16), (1, 0, 2)).reshape(1, 32, 512)
    for flip in (4, 2, 1):
        own = jnp.concatenate([own, partner(own, "y", flip)], axis=0)
    other = partner(own, "core", 1)

    y, core = lax.axis_index("y"), lax.axis_index("core")
    first = (y * 2 + core) * 32 + lax.axis_index("z") * 4
    own_chain = lax.dynamic_slice_in_dim(chain_ids, first, 4, 0)
    own_block = lax.dynamic_slice_in_dim(template, first // 64, 1, 1)
    block_keep = jnp.broadcast_to(own_block, (8, 64)).reshape(1, 512) > 0
    keep = ((own_chain[:, None] == chain_ids[None, :]) | block_keep).astype(jnp.int32)

    columns = pl.BlockSpec((32, 16, 128), lambda j: (0, j, 0))
    slots = pl.BlockSpec((8, 32, 512), lambda j: (0, 0, 0))
    back, d_own, d_other = pl.pallas_call(
        attend_kernel,
        grid=(4,),
        in_specs=[
            pl.BlockSpec(memory_space=pltpu.SMEM),
            pl.BlockSpec((4, 512), lambda j: (0, 0)),
            columns,
            slots,
            slots,
        ],
        out_specs=[columns, slots, slots],
        out_shape=[shaped(32, 64, 128), shaped(8, 32, 512), shaped(8, 32, 512)],
        name="attend",
        compiler_params=pltpu.CompilerParams(vmem_limit_bytes=VMEM_BYTES),
    )(jnp.stack([y, core]).astype(jnp.int32), keep, data, own, other)

    got = swap(back, ROWS)
    d_bias = d_own + partner(d_other, "core", 1)
    for flip in (1, 2, 4):
        half = d_bias.shape[0] // 2
        d_bias = d_bias[:half] + partner(d_bias[half:], "y", flip)
    d_bias = jnp.transpose(d_bias.reshape(32, 32, 16), (1, 0, 2)).reshape(32, 4, 128)

    update, d_normed, params = call(
        lambda *refs: block_kernel(factor, *refs),
        [shaped(16, 32, 128), shaped(512, 128), shaped(640, 128)],
        "block_grads",
    )(got.reshape(8, 4, 64, 128), scaled, gate, d_gated, cotangent, w_query, w_key, w_value, w_gate, w_out)

    small = swap(jnp.concatenate([params.reshape(32, 20, 128), d_bias], axis=1), ROWS)
    grad_pair, tail = call(norm_kernel, [shaped(16, 32, 128), shaped(16, 24, 128)], "norm_back")(
        small, d_normed, scaled, inverse, gain, w_bias
    )
    tail = swap(tail, COLS)
    tail = call(share_kernel, shaped(32, 24, 128), "share")(tail)
    tail = swap(tail, ROWS)
    grads = call(
        lambda *refs: finish_kernel(factor, float(tokens), *refs),
        [square, square, square, square, row, square, shaped(4, 128), row],
        "finish",
        scratch_shapes=[pltpu.VMEM((640, 128), F32)],
    )(tail, gain, w_query, w_key, w_value, w_gate, w_bias)
    gq, gk, gv, gg, gshift, go, gb, ggain = grads
    return update, grad_pair, gq, gk, gv, gg, gshift.reshape(128), go, gb, ggain.reshape(128)


def solution(mesh):
    fine = Mesh(mesh.devices.reshape(8, 2, 8, 4), ("y", "core", "z", "x"))
    block = P(ROWS, COLS, None)
    return jax.shard_map(
        body,
        mesh=fine,
        in_specs=(block, block) + (P(),) * 10,
        out_specs=(block, block) + (P(),) * 8,
        check_vma=False,
    )
```

time: 218 us -> 197 us (0.904)
  blocking collectives: 136 us -> 83.5 us
  starting transfers between devices: 11.4 us -> 51.3 us
  waiting for transfers between devices: 39.4 us -> 27.4 us
    all_to_all x7 -> x4, blocking collectives: 136 us -> 83.5 us  [swap(): return lax.all_to_all(value, axes, 0, 0, tiled=False)]
    all_to_all x2, waiting for transfers between devices: 39.4 us -> 0.01 us  [swap(): return lax.all_to_all(value, axes, 0, 0, tiled=False)]
    ppermute x0 -> x8, starting transfers between devices: none -> 37.8 us  [partner(): lax.ppermute(value, axis, [(at, at ^ flip) for at in range(lax.axis_size(...]
    ppermute x0 -> x8, waiting for transfers between devices: none -> 27.4 us  [partner(): lax.ppermute(value, axis, [(at, at ^ flip) for at in range(lax.axis_size(...]
    unnamed x36 -> x44, local copies, waits for them, and re-layouts: 7.46 us -> 9.61 us
  transfers between devices with their start and end apart: 2 -> 10, of which waited for: 2 -> 7; matrix products, arithmetic and copies ran while one was open for 0% -> 1% of each run, Pallas kernels for 0% -> 0%
where the time goes in v2:
time: 197 us; the launch traced here: 196 us
  blocking collectives  83.5 us (42%)
  starting transfers between devices  51.3 us (26%)
  waiting for transfers between devices  27.4 us (14%)
  Pallas kernels  21 us (11%)
  local copies, waits for them, and re-layouts  10.8 us (5%)
    all_to_all x4, blocking collectives, swap(): return lax.all_to_all(value, axes, 0, 0, tiled=False)  83.5 us
    ppermute x8, starting transfers between devices, partner(): lax.ppermute(value, axis, [(at, at ^ flip) for at in range(lax.axis_size(...  37.8 us
    ppermute x8, waiting for transfers between devices, partner(): lax.ppermute(value, axis, [(at, at ^ flip) for at in range(lax.axis_size(...  27.4 us
    pallas_call x1, Pallas kernels, body(): pl.pallas_call(attend_kernel, grid=(4,), in_specs=[pl.BlockSpec(memory_sp...  13.8 us
    all_to_all x2, starting transfers between devices, swap(): return lax.all_to_all(value, axes, 0, 0, tiled=False)  13.6 us
    unnamed x44, local copies, waits for them, and re-layouts  9.61 us
  transfers between devices with their start and end apart: 10, of which 7 were waited for; matrix products, arithmetic and copies ran while one was open for 1% of the time, Pallas kernels for 0%

profile of v2, /device:TPU:1, one launch (start us, length us, event | category | flops | bytes accessed | tf_op | source)
XLA Modules:
  0.0 195.6 jit_solution(7934961562725156031)
XLA Ops:
  0.7 0.7 copy-done.15
  1.3 0.9 copy-done
  2.3 0.8 copy-done.2
  3.1 0.8 copy-done.4
  4.0 0.8 copy-done.6
  4.8 0.8 copy-done.8
  5.6 0.9 copy-done.10
  6.6 0.8 copy-done.13
  7.4 2.6 %project.1 = (f32[8,4,64,128]{3,2,1,0:T(8,128)}, f32[8,4,4,128]{3,2,1,0:T(4,128)S(1)}, f32[512,128]{1,0:T(8,128)S(1)}, f32[512,128]{1,0:T(8,128)S(1)}, f32[512,128]{1,0:T(8,128)S(1)}, /*index=5*/f32[512,128]{1,0:T(8,128)S(1)}) custom-call(f32[16,32,128]{2,1,0:T(8,128)S(1)} %copy-done.10, f32[16,32,128]{2,1,0:T(8,128)S(1)} %copy-done, f32[1,128]{1,0:T(1,128)S(1)} %bitcast.19, ...), custom_call_target="tpu_custom_call" | custom-call | tf_op jit(solution)/shard_map/project/pallas_call | solution.py:300
  10.1 22.3 %all_to_all.30 = f32[32,4,128]{2,1,0:T(4,128)S(1)} all-to-all(f32[32,4,128]{2,1,0:T(4,128)S(1)} %bitcast.18), channel_id=1, replica_groups=mesh['y'=8,'core'=2,'z'=8,'x'=4] {'z','x'}, dimensions={0} | all-to-all | bytes 131072 | tf_op jit(solution)/shard_map/all_to_all | solution.py:283
  32.4 3.9 %all-to-all-start.1 = ((f32[32,64,128]{2,1,0:T(8,128)}), f32[32,64,128]{2,1,0:T(8,128)S(1)}, u32[]{:S(2)}, u32[]{:S(2)}) async-start(f32[32,64,128]{2,1,0:T(8,128)} %bitcast.5), calls=%async_computation.1 | async-start | bytes 2097152 | tf_op jit(solution)/shard_map/all_to_all | solution.py:283
  36.3 0.1 copy.32
  36.5 0.2 copy.33
  36.7 0.1 copy.37
  36.8 7.5 %collective-permute-start = (f32[1,32,512]{2,1,0:T(8,128)S(1)}, f32[1,32,512]{2,1,0:T(8,128)S(1)}, u32[]{:S(2)}, u32[]{:S(2)}) collective-permute-start(f32[1,32,512]{2,1,0:T(8,128)S(1)} %copy.37), channel_id=1, source_target_pairs={{0,256},{64,320},{128,384},{192,448},{256,0},{320,64},{384,128},{4... | collective-permute-start | bytes 196616 | tf_op jit(solution)/shard_map/ppermute | solution.py:287
  44.2 1.9 collective-permute-done
  46.2 4.7 %collective-permute-start.1 = (f32[2,32,512]{2,1,0:T(8,128)S(1)}, f32[2,32,512]{2,1,0:T(8,128)S(1)}, u32[]{:S(2)}, u32[]{:S(2)}) collective-permute-start(f32[2,32,512]{2,1,0:T(8,128)S(1)} %pad_maximum_fusion.3), channel_id=1, source_target_pairs={{0,128},{64,192},{128,0},{192,64},{256,384},{320,448},{384,256},{4... | collective-permute-start | bytes 393224 | tf_op jit(solution)/shard_map/ppermute | solution.py:287
  50.9 4.0 %collective-permute-done.1 = f32[2,32,512]{2,1,0:T(8,128)S(1)} collective-permute-done((f32[2,32,512]{2,1,0:T(8,128)S(1)}, f32[2,32,512]{2,1,0:T(8,128)S(1)}, u32[]{:S(2)}, u32[]{:S(2)}) %collective-permute-start.1) | collective-permute-done | bytes 131104 | tf_op jit(solution)/shard_map/ppermute | solution.py:287
  54.9 1.9 collective-permute-start.2
  56.9 5.5 %collective-permute-done.2 = f32[4,32,512]{2,1,0:T(8,128)S(1)} collective-permute-done((f32[4,32,512]{2,1,0:T(8,128)S(1)}, f32[4,32,512]{2,1,0:T(8,128)S(1)}, u32[]{:S(2)}, u32[]{:S(2)}) %collective-permute-start.2) | collective-permute-done | bytes 262176 | tf_op jit(solution)/shard_map/ppermute | solution.py:287
  62.4 6.2 %collective-permute-start.3 = (f32[8,32,512]{2,1,0:T(8,128)S(1)}, f32[8,32,512]{2,1,0:T(8,128)S(1)}, u32[]{:S(2)}, u32[]{:S(2)}) collective-permute-start(f32[8,32,512]{2,1,0:T(8,128)S(1)} %pad_maximum_fusion.own_ref), channel_id=1, source_target_pairs={{0,32},{32,0},{1,33},{33,1},{2,34},{34,2},{3,35},{35,3},{4,36},{36... | collective-permute-start | bytes 1572872 | tf_op jit(solution)/shard_map/ppermute | solution.py:287
  68.7 0.7 copy-done.20
  69.3 0.2 fusion
  69.6 0.1 gt.21
  69.7 0.5 copy-done.21
  70.4 13.8 %attend.1 = (f32[32,64,128]{2,1,0:T(8,128)}, f32[8,32,512]{2,1,0:T(8,128)S(1)}, f32[8,32,512]{2,1,0:T(8,128)S(1)}) custom-call(s32[2]{0:T(128)S(1)} %pad_add_fusion.place_ref, s32[4,512]{1,0:T(4,128)S(1)} %or_convert_fusion.keep_ref, f32[32,64,128]{2,1,0:T(8,128)S(1)} %all-to-all-done.1.data_ref, f32[8,32,512]{2,1,0:T(8,128)S(1)} %pad_maximum_fusion.own_ref, ...), custom_call_target="tpu_custom_call" | custom-call | tf_op jit(solution)/shard_map/attend/pallas_call | solution.py:325
  84.2 0.8 copy-done.18
  85.0 9.6 %all-to-all-start.2 = ((f32[32,64,128]{2,1,0:T(8,128)}), f32[32,64,128]{2,1,0:T(8,128)S(1)}, u32[]{:S(2)}, u32[]{:S(2)}) async-start(f32[32,64,128]{2,1,0:T(8,128)} %get-tuple-element.38), calls=%async_computation.2 | async-start | bytes 2097152 | tf_op jit(solution)/shard_map/all_to_all | solution.py:283
  94.6 2.2 %collective-permute-start.4 = (f32[8,32,512]{2,1,0:T(8,128)S(1)}, f32[8,32,512]{2,1,0:T(8,128)S(1)}, u32[]{:S(2)}, u32[]{:S(2)}) collective-permute-start(f32[8,32,512]{2,1,0:T(8,128)S(1)} %copy-done.19), channel_id=1, source_target_pairs={{0,32},{32,0},{1,33},{33,1},{2,34},{34,2},{3,35},{35,3},{4,36},{36... | collective-permute-start | bytes 1572872 | tf_op jit(solution)/shard_map/ppermute | solution.py:287
  96.9 1.5 collective-permute-done.4
  98.4 0.1 add.29
  98.5 2.5 %collective-permute-start.5 = (f32[4,32,512]{2,1,0:T(8,128)S(1)}, f32[4,32,512]{2,1,0:T(8,128)S(1)}, u32[]{:S(2)}, u32[]{:S(2)}) collective-permute-start(f32[4,32,512]{2,1,0:T(8,128)S(1)} %slice.25), channel_id=1, source_target_pairs={{0,64},{64,0},{128,192},{192,128},{256,320},{320,256},{384,448},{4... | collective-permute-start | bytes 786440 | tf_op jit(solution)/shard_map/ppermute | solution.py:287
  101.1 6.9 %collective-permute-done.5 = f32[4,32,512]{2,1,0:T(8,128)S(1)} collective-permute-done((f32[4,32,512]{2,1,0:T(8,128)S(1)}, f32[4,32,512]{2,1,0:T(8,128)S(1)}, u32[]{:S(2)}, u32[]{:S(2)}) %collective-permute-start.5) | collective-permute-done | bytes 262176 | tf_op jit(solution)/shard_map/ppermute | solution.py:287
  108.0 4.5 %collective-permute-start.6 = (f32[2,32,512]{2,1,0:T(8,128)S(1)}, f32[2,32,512]{2,1,0:T(8,128)S(1)}, u32[]{:S(2)}, u32[]{:S(2)}) collective-permute-start(f32[2,32,512]{2,1,0:T(8,128)S(1)} %slice.27), channel_id=1, source_target_pairs={{0,128},{64,192},{128,0},{192,64},{256,384},{320,448},{384,256},{4... | collective-permute-start | bytes 393224 | tf_op jit(solution)/shard_map/ppermute | solution.py:287
  112.6 5.8 %collective-permute-done.6 = f32[2,32,512]{2,1,0:T(8,128)S(1)} collective-permute-done((f32[2,32,512]{2,1,0:T(8,128)S(1)}, f32[2,32,512]{2,1,0:T(8,128)S(1)}, u32[]{:S(2)}, u32[]{:S(2)}) %collective-permute-start.6) | collective-permute-done | bytes 131104 | tf_op jit(solution)/shard_map/ppermute | solution.py:287
  118.4 8.2 %collective-permute-start.7 = (f32[1,32,512]{2,1,0:T(8,128)S(1)}, f32[1,32,512]{2,1,0:T(8,128)S(1)}, u32[]{:S(2)}, u32[]{:S(2)}) collective-permute-start(f32[1,32,512]{2,1,0:T(8,128)S(1)} %slice.29), channel_id=1, source_target_pairs={{0,256},{64,320},{128,384},{192,448},{256,0},{320,64},{384,128},{4... | collective-permute-start | bytes 196616 | tf_op jit(solution)/shard_map/ppermute | solution.py:287
  126.7 1.6 collective-permute-done.7
  128.3 0.1 copy.38
  128.5 0.2 copy.39
  128.7 0.1 copy.40
  128.9 0.4 copy-done.5
  129.4 0.3 copy-done.1
  129.7 2.1 %block_grads.1 = (f32[16,32,128]{2,1,0:T(8,128)}, f32[512,128]{1,0:T(8,128)S(1)}, f32[640,128]{1,0:T(8,128)S(1)}) custom-call(f32[8,4,64,128]{3,2,1,0:T(8,128)S(1)} %bitcast.17, f32[512,128]{1,0:T(8,128)S(1)} %get-tuple-element.39.refs_1_.scaled_ref, f32[512,128]{1,0:T(8,128)S(1)} %get-tuple-element.40.refs_2_, f32[512,128]{1,0:T(8,128)S(1)} %get-tuple-element.41.refs_3_, ...), custom_call_target="tpu_custom_call" | custom-call | tf_op jit(solution)/shard_map/block_grads/pallas_call | solution.py:348
  131.9 22.3 %all_to_all.31.recv_ref = f32[32,24,128]{2,1,0:T(8,128)S(1)} all-to-all(f32[32,24,128]{2,1,0:T(8,128)S(1)} %pad_maximum_fusion.1), channel_id=1, replica_groups=mesh['y'=8,'core'=2,'z'=8,'x'=4] {'z','x'}, dimensions={0} | all-to-all | bytes 786432 | tf_op jit(solution)/shard_map/all_to_all | solution.py:283
  154.2 1.2 norm_back.1
  155.5 20.4 %all_to_all.32.recv_ref = f32[16,24,128]{2,1,0:T(8,128)S(1)} all-to-all(f32[16,24,128]{2,1,0:T(8,128)S(1)} %get-tuple-element.49), channel_id=1, replica_groups=mesh['y'=8,'core'=2,'z'=8,'x'=4] {'y','core'}, dimensions={0} | all-to-all | bytes 393216 | tf_op jit(solution)/shard_map/all_to_all | solution.py:283
  175.9 18.5 %all_to_all.33.refs_0_ = f32[32,24,128]{2,1,0:T(8,128)S(1)} all-to-all(f32[32,24,128]{2,1,0:T(8,128)S(1)} %share.1), channel_id=1, replica_groups=mesh['y'=8,'core'=2,'z'=8,'x'=4] {'z','x'}, dimensions={0} | all-to-all | bytes 786432 | tf_op jit(solution)/shard_map/all_to_all | solution.py:283
  194.4 1.2 finish.1
  (50 shorter events, 0.7 us)
Async XLA Ops:
  0.6 0.7 copy-start.15
  0.7 0.7 copy-start.16
  0.7 0.7 copy-start.17
  1.3 1.0 copy-start
  2.3 0.8 copy-start.2
  3.1 0.8 copy-start.4
  4.0 0.8 copy-start.6
  4.8 0.8 copy-start.8
  5.6 0.9 copy-start.10
  6.6 0.8 copy-start.13
  10.0 22.3 %copy-start.11 = (f32[512,128]{1,0:T(8,128)}, f32[512,128]{1,0:T(8,128)S(1)}, u32[]{:S(2)}) copy-start(f32[512,128]{1,0:T(8,128)S(1)} %get-tuple-element.47.inv_ref) | copy-start | bytes 786436
  32.4 38.0 %all-to-all-start.1 = ((f32[32,64,128]{2,1,0:T(8,128)}), f32[32,64,128]{2,1,0:T(8,128)S(1)}, u32[]{:S(2)}, u32[]{:S(2)}) async-start(f32[32,64,128]{2,1,0:T(8,128)} %bitcast.5), calls=%async_computation.1 | async-start | bytes 2097152 | tf_op jit(solution)/shard_map/all_to_all | solution.py:283
  36.8 9.4 %collective-permute-start = (f32[1,32,512]{2,1,0:T(8,128)S(1)}, f32[1,32,512]{2,1,0:T(8,128)S(1)}, u32[]{:S(2)}, u32[]{:S(2)}) collective-permute-start(f32[1,32,512]{2,1,0:T(8,128)S(1)} %copy.37), channel_id=1, source_target_pairs={{0,256},{64,320},{128,384},{192,448},{256,0},{320,64},{384,128},{4... | collective-permute-start | bytes 196616 | tf_op jit(solution)/shard_map/ppermute | solution.py:287
  46.2 8.7 %collective-permute-start.1 = (f32[2,32,512]{2,1,0:T(8,128)S(1)}, f32[2,32,512]{2,1,0:T(8,128)S(1)}, u32[]{:S(2)}, u32[]{:S(2)}) collective-permute-start(f32[2,32,512]{2,1,0:T(8,128)S(1)} %pad_maximum_fusion.3), channel_id=1, source_target_pairs={{0,128},{64,192},{128,0},{192,64},{256,384},{320,448},{384,256},{4... | collective-permute-start | bytes 393224 | tf_op jit(solution)/shard_map/ppermute | solution.py:287
  54.9 7.4 %collective-permute-start.2 = (f32[4,32,512]{2,1,0:T(8,128)S(1)}, f32[4,32,512]{2,1,0:T(8,128)S(1)}, u32[]{:S(2)}, u32[]{:S(2)}) collective-permute-start(f32[4,32,512]{2,1,0:T(8,128)S(1)} %pad_maximum_fusion.2), channel_id=1, source_target_pairs={{0,64},{64,0},{128,192},{192,128},{256,320},{320,256},{384,448},{4... | collective-permute-start | bytes 786440 | tf_op jit(solution)/shard_map/ppermute | solution.py:287
  62.4 8.0 %collective-permute-start.3 = (f32[8,32,512]{2,1,0:T(8,128)S(1)}, f32[8,32,512]{2,1,0:T(8,128)S(1)}, u32[]{:S(2)}, u32[]{:S(2)}) collective-permute-start(f32[8,32,512]{2,1,0:T(8,128)S(1)} %pad_maximum_fusion.own_ref), channel_id=1, source_target_pairs={{0,32},{32,0},{1,33},{33,1},{2,34},{34,2},{3,35},{35,3},{4,36},{36... | collective-permute-start | bytes 1572872 | tf_op jit(solution)/shard_map/ppermute | solution.py:287
  68.6 0.7 copy-start.20
  69.5 0.7 copy-start.21
  84.2 0.8 copy-start.18
  85.0 9.6 %copy-start.19 = (f32[8,32,512]{2,1,0:T(8,128)S(1)}, f32[8,32,512]{2,1,0:T(8,128)}, u32[]{:S(2)}) copy-start(f32[8,32,512]{2,1,0:T(8,128)} %copy-done.18) | copy-start | bytes 1572868
  85.0 43.9 %all-to-all-start.2 = ((f32[32,64,128]{2,1,0:T(8,128)}), f32[32,64,128]{2,1,0:T(8,128)S(1)}, u32[]{:S(2)}, u32[]{:S(2)}) async-start(f32[32,64,128]{2,1,0:T(8,128)} %get-tuple-element.38), calls=%async_computation.2 | async-start | bytes 2097152 | tf_op jit(solution)/shard_map/all_to_all | solution.py:283
  94.6 3.8 %collective-permute-start.4 = (f32[8,32,512]{2,1,0:T(8,128)S(1)}, f32[8,32,512]{2,1,0:T(8,128)S(1)}, u32[]{:S(2)}, u32[]{:S(2)}) collective-permute-start(f32[8,32,512]{2,1,0:T(8,128)S(1)} %copy-done.19), channel_id=1, source_target_pairs={{0,32},{32,0},{1,33},{33,1},{2,34},{34,2},{3,35},{35,3},{4,36},{36... | collective-permute-start | bytes 1572872 | tf_op jit(solution)/shard_map/ppermute | solution.py:287
  98.5 9.5 %collective-permute-start.5 = (f32[4,32,512]{2,1,0:T(8,128)S(1)}, f32[4,32,512]{2,1,0:T(8,128)S(1)}, u32[]{:S(2)}, u32[]{:S(2)}) collective-permute-start(f32[4,32,512]{2,1,0:T(8,128)S(1)} %slice.25), channel_id=1, source_target_pairs={{0,64},{64,0},{128,192},{192,128},{256,320},{320,256},{384,448},{4... | collective-permute-start | bytes 786440 | tf_op jit(solution)/shard_map/ppermute | solution.py:287
  108.0 10.4 %collective-permute-start.6 = (f32[2,32,512]{2,1,0:T(8,128)S(1)}, f32[2,32,512]{2,1,0:T(8,128)S(1)}, u32[]{:S(2)}, u32[]{:S(2)}) collective-permute-start(f32[2,32,512]{2,1,0:T(8,128)S(1)} %slice.27), channel_id=1, source_target_pairs={{0,128},{64,192},{128,0},{192,64},{256,384},{320,448},{384,256},{4... | collective-permute-start | bytes 393224 | tf_op jit(solution)/shard_map/ppermute | solution.py:287
  118.4 9.9 %collective-permute-start.7 = (f32[1,32,512]{2,1,0:T(8,128)S(1)}, f32[1,32,512]{2,1,0:T(8,128)S(1)}, u32[]{:S(2)}, u32[]{:S(2)}) collective-permute-start(f32[1,32,512]{2,1,0:T(8,128)S(1)} %slice.29), channel_id=1, source_target_pairs={{0,256},{64,320},{128,384},{192,448},{256,0},{320,64},{384,128},{4... | collective-permute-start | bytes 196616 | tf_op jit(solution)/shard_map/ppermute | solution.py:287
  128.5 0.8 copy-start.5
  128.5 0.9 copy-start.7
  128.5 0.9 copy-start.9
  128.5 0.9 copy-start.14
  128.7 1.0 copy-start.1
  128.7 1.0 copy-start.3
  131.9 22.3 %copy-start.12 = (f32[512,128]{1,0:T(8,128)S(1)}, f32[512,128]{1,0:T(8,128)}, u32[]{:S(2)}) copy-start(f32[512,128]{1,0:T(8,128)} %copy-done.11) | copy-start | bytes 786436

commit v3 on v2

v3 whole, which is shorter than its diff:
```python
import jax
import jax.numpy as jnp
from jax import lax
from jax.experimental import pallas as pl
from jax.experimental.pallas import tpu as pltpu
from jax.sharding import Mesh, PartitionSpec as P

F32 = jnp.float32
BF16 = jnp.bfloat16
NEG_FILL = -1000000000.0
ROWS = ("z", "x")
COLS = ("y", "core")
VMEM_BYTES = 48 * 1024 * 1024
NN = (((1,), (0,)), ((), ()))
NT = (((1,), (1,)), ((), ()))


def bdot(left, right, dims=NN):
    return lax.dot_general(left, right, dims, preferred_element_type=F32)


def split(value):
    high = value.astype(BF16)
    return high, (value - high.astype(F32)).astype(BF16)


def dot3(left, right, dims=NN):
    lh, ll = left if isinstance(left, tuple) else split(left)
    rh, rl = right if isinstance(right, tuple) else split(right)
    return bdot(lh, rh, dims) + (bdot(ll, rh, dims) + bdot(lh, rl, dims))


def lanes_of(shape):
    return lax.broadcasted_iota(jnp.int32, shape, 1)


def turn(value, amount):
    amount = amount % value.shape[1]
    return value if amount == 0 else pltpu.roll(value, amount, 1)


def head_weights(wq, wk, wv, wg, head, factor):
    lane = lanes_of(wq.shape)
    at = 32 * head
    out = jnp.where(lane < 32, turn(wq, -at) * factor, turn(wk, 32 - at))
    out = jnp.where(lane < 64, out, turn(wv, 64 - at))
    return jnp.where(lane < 96, out, turn(wg, 96 - at))


def norm_kernel(x_ref, gain_ref, wb_ref, piece_ref, scaled_ref, inv_ref):
    cells = jnp.swapaxes(x_ref[...], 0, 1).reshape(512, 128)
    center = jnp.mean(cells, axis=1, keepdims=True)
    shifted = cells - center
    spread = jnp.mean(shifted * shifted, axis=1, keepdims=True)
    inverse = lax.rsqrt(spread + 1e-05)
    scaled = shifted * inverse
    scaled_ref[...] = scaled
    inv_ref[...] = jnp.broadcast_to(inverse, (512, 128))
    wb = jnp.concatenate([wb_ref[...], jnp.zeros((4, 128), F32)], axis=0)
    bias = dot3(wb, scaled * gain_ref[...], NT)
    for head in range(4):
        for part in range(4):
            row = bias[head : head + 1, part * 128 : (part + 1) * 128]
            piece_ref[:, head, part, :] = jnp.broadcast_to(row, (8, 128))


def project_kernel(
    factor, place_ref, scaled_ref, cot_ref, gain_ref, wq_ref, wk_ref, wv_ref, wg_ref, gb_ref, wo_ref,
    chain_ref, template_ref, send_ref, gate_ref, dgated_ref, keep_ref,
):
    cot = jnp.swapaxes(cot_ref[...], 0, 1).reshape(512, 128)
    normed = split(scaled_ref[...] * gain_ref[...])
    wq, wk, wv, wg = wq_ref[...], wk_ref[...], wv_ref[...], wg_ref[...]
    gate = jax.nn.sigmoid(dot3(normed, wg) + gb_ref[...])
    d_gated = dot3(cot, wo_ref[...], NT)
    gate_ref[...] = gate
    dgated_ref[...] = d_gated
    d_att = d_gated * gate
    lane = lanes_of((512, 128))
    for head in range(4):
        weights = head_weights(wq, wk, wv, wg, head, factor)
        block = jnp.where(lane < 96, dot3(normed, weights), turn(d_att, 96 - 32 * head))
        send_ref[:, head] = block.reshape(8, 64, 128)
    first = place_ref[2]
    chain = chain_ref[...]
    token = lanes_of((1, 512))
    near = lanes_of((8, 8)) == first // 64
    blocks = jnp.max(jnp.where(near, template_ref[...], 0), axis=1, keepdims=True)
    open_block = jnp.zeros((1, 512), jnp.int32)
    for block in range(8):
        open_block = jnp.where(token // 64 == block, blocks[block : block + 1], open_block)
    for column in range(4):
        own = jnp.max(jnp.where(token == first + column, chain, 0), axis=1, keepdims=True)
        keep_ref[column : column + 1, :] = jnp.where(chain == own, 1, open_block)


def spread_lanes(value, group):
    lane = lanes_of(value.shape)
    kept = jnp.where((lane >= 32 * group) & (lane < 32 * group + 32), value, 0.0)
    kept = kept + pltpu.roll(kept, 32, 1)
    return kept + pltpu.roll(kept, 64, 1)


def parts_of(value):
    high = value.astype(BF16).astype(F32)
    return high, value - high


def attend_kernel(place_ref, keep_ref, data_ref, own_ref, other_ref, out_ref, d_own_ref, d_other_ref):
    column = pl.program_id(0)
    y, core = place_ref[0], place_ref[1]

    @pl.when(column == 0)
    def _():
        d_own_ref[...] = jnp.zeros_like(d_own_ref)
        d_other_ref[...] = jnp.zeros_like(d_other_ref)

    data = data_ref[...].reshape(512, 128)
    lane = lanes_of((512, 128))
    kh, kl = parts_of(spread_lanes(data, 1))
    vh, vl = parts_of(spread_lanes(data, 2))
    k_right = jnp.where(lane < 64, kh, kl).astype(BF16)
    v_right = jnp.where(lane < 64, vh, vl).astype(BF16)
    k_first = jnp.where(lane < 32, kh, 0.0).astype(BF16)
    k_both = jnp.where(lane < 32, kh, jnp.where(lane < 64, kl, 0.0)).astype(BF16)
    v_first = jnp.where(lane >= 96, vh, 0.0).astype(BF16)
    v_both = jnp.where(lane >= 96, vh, jnp.where(lane >= 64, vl, 0.0)).astype(BF16)
    keep = keep_ref[pl.ds(column, 1), :] > 0
    chunk_rows = 256
    per = chunk_rows // 32
    sub = lanes_of((chunk_rows, 128))
    odd = (sub // 32) % 2 == 1
    chunks = []
    for side, (bias_ref, db_ref) in enumerate(((own_ref, d_own_ref), (other_ref, d_other_ref))):
        half = core if side == 0 else 1 - core
        for s0 in range(0, 8, per):
            starts = [(y ^ ((s >> 2) | (s & 2) | ((s & 1) << 2))) * 4 + half * 2 for s in range(s0, s0 + per)]
            chunks.append((starts, bias_ref, db_ref, s0))

    def first(chunk):
        starts, bias_ref, db_ref, s0 = chunk
        rows = jnp.concatenate([data_ref[pl.ds(start, 2)].reshape(32, 128) for start in starts], axis=0)
        qh, ql = parts_of(spread_lanes(rows, 0))
        q_left = jnp.where(odd, ql, qh)
        scores = bdot(q_left.astype(BF16), k_right, NT) + bias_ref[s0 : s0 + per].reshape(chunk_rows, 512)
        return rows, q_left, jnp.where(keep, scores, NEG_FILL)

    def second(state):
        rows, q_left, scores = state
        highest = jnp.max(scores, axis=1, keepdims=True)
        weights = jnp.exp(scores - highest)
        inv_total = 1.0 / jnp.sum(weights, axis=1, keepdims=True)
        wh, wl = split(weights)
        output = bdot(wh, v_both) + bdot(wl, v_first)
        output = (output + pltpu.roll(output, 32, 1)) * inv_total
        d_out = jnp.where(sub >= 96, rows, 0.0) * inv_total
        centred = jnp.sum(d_out * output, axis=1, keepdims=True)
        dh, dl = parts_of(spread_lanes(d_out, 3))
        d_left = jnp.where(odd, dl, dh)
        d_weights = bdot(d_left.astype(BF16), v_right, NT)
        d_t = jnp.transpose(d_left)[0:64].astype(BF16)
        both = bdot(d_t, wh)
        dv_t = both[0:32] + both[32:64] + bdot(d_t[0:32], wl)
        return weights, output, d_weights, centred, dv_t, q_left

    def third(chunk, state):
        starts, bias_ref, db_ref, s0 = chunk
        weights, output, d_weights, centred, dv_t, q_left = state
        d_scores = weights * (d_weights - centred)
        db_ref[s0 : s0 + per] += d_scores.reshape(per, 32, 512)
        sh, sl = split(d_scores)
        d_query = bdot(sh, k_both) + bdot(sl, k_first)
        d_query = d_query + pltpu.roll(d_query, 96, 1)
        q_t = jnp.transpose(q_left)[0:64].astype(BF16)
        both = bdot(q_t, sh)
        dk_t = both[0:32] + both[32:64] + bdot(q_t[0:32], sl)
        return jnp.where(sub < 32, d_query, output), dk_t, dv_t

    n = len(chunks)
    ones, twos, dones = {}, {}, {}
    for step in range(n + 2):
        if step < n:
            ones[step] = first(chunks[step])
        if 0 <= step - 1 < n:
            twos[step - 1] = second(ones.pop(step - 1))
        if 0 <= step - 2 < n:
            dones[step - 2] = third(chunks[step - 2], twos.pop(step - 2))
    zeros = jnp.zeros((32, 512), F32)
    dk_t = sum(dones[c][1] for c in range(n))
    dv_t = sum(dones[c][2] for c in range(n))
    result = jnp.transpose(jnp.concatenate([zeros, dk_t, dv_t, zeros], axis=0))
    out_ref[...] = result.reshape(32, 16, 128)
    mixed = (sub >= 32) & (sub < 96)
    for c in range(n):
        starts = chunks[c][0]
        held = jnp.concatenate([out_ref[pl.ds(start, 2)].reshape(32, 128) for start in starts], axis=0)
        value = jnp.where(mixed, held, dones[c][0])
        for s, start in enumerate(starts):
            out_ref[pl.ds(start, 2)] = value[s * 32 : (s + 1) * 32].reshape(2, 16, 128)


def block_kernel(
    factor, place_ref, recv_ref, scaled_ref, gate_ref, dgated_ref, cot_ref, wq_ref, wk_ref, wv_ref, wg_ref, wo_ref,
    update_ref, dnorm_ref, keep_ref, give_ref, param_ref,
):
    lane = lanes_of((512, 128))
    scaled = scaled_ref[...]
    gate = gate_ref[...]
    cot = jnp.swapaxes(cot_ref[...], 0, 1).reshape(512, 128)
    wq, wk, wv, wg = wq_ref[...], wk_ref[...], wv_ref[...], wg_ref[...]
    got = [recv_ref[:, head].reshape(512, 128) for head in range(4)]
    att = turn(got[3], 0)
    for head in range(3):
        moved = turn(got[head], 32 * head - 96)
        att = jnp.where((lane >= 32 * head) & (lane < 32 * head + 32), moved, att)
    gated = gate * att
    d_pre = dgated_ref[...] * att * gate * (1.0 - gate)
    update = dot3(gated, wo_ref[...])
    update_ref[...] = jnp.swapaxes(update.reshape(32, 16, 128), 0, 1)
    scaled_t = split(jnp.transpose(jnp.where(lane == 127, 1.0, scaled)))
    d_normed = jnp.zeros((512, 128), F32)
    for head in range(4):
        grads = split(jnp.where(lane < 96, got[head], turn(d_pre, 96 - 32 * head)))
        weights = head_weights(wq, wk, wv, wg, head, factor)
        d_normed = d_normed + dot3(grads, weights, NT)
        param_ref[head * 128 : (head + 1) * 128, :] = dot3(scaled_t, grads)
    param_ref[512:640, :] = dot3(jnp.transpose(gated), cot)
    dnorm_ref[...] = d_normed
    core = place_ref[1]
    keep_ref[...] = param_ref[pl.ds(pl.multiple_of(core * 320, 8), 320), :]
    give_ref[...] = param_ref[pl.ds(pl.multiple_of((1 - core) * 320, 8), 320), :]


def close_kernel(
    recv_ref, dnorm_ref, scaled_ref, inv_ref, gain_ref, wb_ref, grad_ref, send_ref
):
    chunk = jnp.sum(recv_ref[:, 0:10, :], axis=0)
    rows = []
    for head in range(4):
        pieces = recv_ref[head, 10:14, :]
        for z in range(1, 8):
            pieces = pieces + recv_ref[z * 4 + head, 10:14, :]
        rows.append(jnp.concatenate([pieces[a : a + 1] for a in range(4)], axis=1))
    bias_t = jnp.concatenate(rows + [jnp.zeros((4, 512), F32)], axis=0)
    scaled = scaled_ref[...]
    wide = jnp.concatenate([bias_t, jnp.zeros((120, 512), F32)], axis=0)
    wb = jnp.concatenate([wb_ref[...], jnp.zeros((124, 128), F32)], axis=0)
    d_normed = dnorm_ref[...] + dot3(jnp.transpose(wide), wb)
    d_scaled = d_normed * gain_ref[...]
    mean_term = jnp.mean(d_scaled, axis=1, keepdims=True)
    cross_term = jnp.mean(d_scaled * scaled, axis=1, keepdims=True)
    d_input = inv_ref[...] * (d_scaled - mean_term - scaled * cross_term)
    grad_ref[...] = jnp.swapaxes(d_input.reshape(32, 16, 128), 0, 1)
    bias_w = dot3(bias_t, scaled)
    tail = jnp.concatenate([chunk, bias_w[0:4], jnp.zeros((2, 128), F32)], axis=0)
    send_ref[...] = jnp.broadcast_to(tail[None], (8, 16, 128))


def share_kernel(recv_ref, send_ref):
    total = jnp.sum(recv_ref[...], axis=0)
    send_ref[...] = jnp.broadcast_to(total[None], (32, 16, 128))


def finish_kernel(
    factor, count, place_ref, own_ref, other_ref, gain_ref, wq_ref, wk_ref, wv_ref, wg_ref, wb_ref,
    q_ref, k_ref, v_ref, g_ref, shift_ref, o_ref, b_ref, gain_out_ref, own_rows, other_rows,
):
    for at in range(32):
        own_rows[at * 10 : (at + 1) * 10, :] = own_ref[at, 0:10, :]
        other_rows[at * 10 : (at + 1) * 10, :] = other_ref[at, 0:10, :]
    bias_w = jnp.sum(own_ref[:, 10:14, :], axis=0) + jnp.sum(other_ref[:, 10:14, :], axis=0)
    low_half = place_ref[1] == 0
    own_half, other_half = own_rows[...], other_rows[...]
    hold = jnp.concatenate(
        [jnp.where(low_half, own_half, other_half), jnp.where(low_half, other_half, own_half)], axis=0
    )
    wq, wk, wv, wg = wq_ref[...], wk_ref[...], wv_ref[...], wg_ref[...]
    lane = lanes_of((128, 128))
    gain_rows = jnp.transpose(jnp.broadcast_to(gain_ref[...], (128, 128)))
    last = lax.broadcasted_iota(jnp.int32, (128, 128), 0) == 127
    scale = 1.0 / count
    blocks = []
    shift = jnp.zeros((1, 128), F32)
    for head in range(4):
        block = hold[head * 128 : (head + 1) * 128, :]
        sums = turn(block[127:128], 32 * head - 96)
        shift = jnp.where((lane[0:1] >= 32 * head) & (lane[0:1] < 32 * head + 32), sums, shift)
        block = jnp.where(last, 0.0, block)
        blocks.append(jnp.where(last, -jnp.sum(block, axis=0, keepdims=True), block))
    gain_sum = jnp.zeros((128, 128), F32)
    for head in range(4):
        gain_sum = gain_sum + blocks[head] * head_weights(wq, wk, wv, wg, head, factor)
    for ref, group, times in ((q_ref, 0, factor), (k_ref, 1, 1.0), (v_ref, 2, 1.0), (g_ref, 3, 1.0)):
        full = turn(blocks[0], -32 * group)
        for head in range(1, 4):
            full = jnp.where(lane >= 32 * head, turn(blocks[head], 32 * (head - group)), full)
        ref[...] = full * gain_rows * (times * scale)
    o_ref[...] = hold[512:640, :] * scale
    b_ref[...] = bias_w * gain_ref[...] * scale
    shift_ref[...] = shift * scale
    gain_total = jnp.sum(jnp.transpose(gain_sum), axis=0, keepdims=True)
    gain_total = gain_total + jnp.sum(bias_w * wb_ref[...], axis=0, keepdims=True)
    gain_out_ref[...] = gain_total * scale


def cost(us):
    return pl.CostEstimate(flops=int(us * 1e9), bytes_accessed=int(us * 2e6), transcendentals=0)


def call(kernel, out_shape, name, us, **extra):
    return pl.pallas_call(
        kernel,
        out_shape=out_shape,
        name=name,
        cost_estimate=cost(us),
        compiler_params=pltpu.CompilerParams(vmem_limit_bytes=VMEM_BYTES),
        **extra,
    )


def shaped(*shape):
    return jax.ShapeDtypeStruct(shape, F32)


def attend_call(place, keep, data, own, other):
    columns = pl.BlockSpec((32, 16, 128), lambda j: (0, j, 0))
    slots = pl.BlockSpec((8, 32, 512), lambda j: (0, 0, 0))
    return pl.pallas_call(
        attend_kernel,
        grid=(4,),
        in_specs=[
            pl.BlockSpec(memory_space=pltpu.SMEM),
            pl.BlockSpec((4, 512), lambda j: (0, 0)),
            columns,
            slots,
            slots,
        ],
        out_specs=[columns, slots, slots],
        out_shape=[shaped(32, 64, 128), shaped(8, 32, 512), shaped(8, 32, 512)],
        name="attend",
        cost_estimate=cost(12),
        compiler_params=pltpu.CompilerParams(vmem_limit_bytes=VMEM_BYTES),
    )(place, keep, data, own, other)


def swap(value, axes):
    return lax.all_to_all(value, axes, 0, 0, tiled=False)


def partner(value, axis, flip):
    return lax.ppermute(value, axis, [(at, at ^ flip) for at in range(lax.axis_size(axis))])


def body(
    pair_rep, cotangent, chain_ids, template, norm_gain, w_query, w_key, w_value, w_gate, gate_bias, w_out, w_bias,
):
    factor = 32 ** (-0.5)
    tokens = chain_ids.shape[0]
    gain = norm_gain.reshape(1, 128)
    square = shaped(128, 128)
    row = shaped(1, 128)

    y, core = lax.axis_index("y"), lax.axis_index("core")
    first = (y * 2 + core) * 32 + lax.axis_index("z") * 4
    place = jnp.stack([y, core, first]).astype(jnp.int32)

    piece, scaled, inverse = call(
        norm_kernel, [shaped(8, 4, 4, 128), shaped(512, 128), shaped(512, 128)], "norm_bias", 1
    )(pair_rep, gain, w_bias)
    vmem = pl.BlockSpec(memory_space=pltpu.VMEM)
    send, gate, d_gated, keep = call(
        lambda *refs: project_kernel(factor, *refs),
        [shaped(8, 4, 64, 128), shaped(512, 128), shaped(512, 128), jax.ShapeDtypeStruct((4, 512), jnp.int32)],
        "project",
        2,
        in_specs=[pl.BlockSpec(memory_space=pltpu.SMEM)] + [vmem] * 11,
    )(
        place, scaled, cotangent, gain, w_query, w_key, w_value, w_gate, gate_bias.reshape(1, 128), w_out,
        chain_ids.reshape(1, 512), template,
    )

    piece = swap(piece.reshape(32, 4, 128), ROWS)
    piece, send = lax.optimization_barrier((piece, send))
    data = swap(send.reshape(32, 64, 128), ROWS)
    own = jnp.transpose(piece.reshape(32, 32, 16), (1, 0, 2)).reshape(1, 32, 512)
    own = jnp.concatenate([own] + [partner(own, "y", flip) for flip in (4, 2, 6)], axis=0)
    own = jnp.concatenate([own, partner(own, "y", 1)], axis=0)
    other = partner(own, "core", 1)

    back, d_own, d_other = attend_call(place, keep, data, own, other)

    got = swap(back, ROWS)
    d_bias = d_own + partner(d_other, "core", 1)
    d_bias = d_bias[:4] + partner(d_bias[4:], "y", 1)
    d_bias = d_bias[0] + sum(partner(d_bias[s], "y", flip) for s, flip in ((1, 4), (2, 2), (3, 6)))
    d_bias = jnp.transpose(d_bias.reshape(32, 32, 16), (1, 0, 2)).reshape(32, 4, 128)

    update, d_normed, params, give = call(
        lambda *refs: block_kernel(factor, *refs),
        [shaped(16, 32, 128), shaped(512, 128), shaped(320, 128), shaped(320, 128)],
        "block_grads",
        2,
        in_specs=[pl.BlockSpec(memory_space=pltpu.SMEM)] + [vmem] * 10,
        scratch_shapes=[pltpu.VMEM((640, 128), F32)],
    )(place, got.reshape(8, 4, 64, 128), scaled, gate, d_gated, cotangent, w_query, w_key, w_value, w_gate, w_out)

    params = params + partner(give, "core", 1)
    small = swap(jnp.concatenate([params.reshape(32, 10, 128), d_bias], axis=1), ROWS)
    grad_pair, tail = call(close_kernel, [shaped(16, 32, 128), shaped(8, 16, 128)], "norm_back", 1)(
        small, d_normed, scaled, inverse, gain, w_bias
    )
    tail = swap(tail, "y")
    tail = call(share_kernel, shaped(32, 16, 128), "share", 0.1)(tail)
    tail = swap(tail, ROWS)
    grads = call(
        lambda *refs: finish_kernel(factor, float(tokens), *refs),
        [square, square, square, square, row, square, shaped(4, 128), row],
        "finish",
        1,
        in_specs=[pl.BlockSpec(memory_space=pltpu.SMEM)] + [vmem] * 8,
        scratch_shapes=[pltpu.VMEM((320, 128), F32)] * 2,
    )(place, tail, partner(tail, "core", 1), gain, w_query, w_key, w_value, w_gate, w_bias)
    gq, gk, gv, gg, gshift, go, gb, ggain = grads
    return update, grad_pair, gq, gk, gv, gg, gshift.reshape(128), go, gb, ggain.reshape(128)


def solution(mesh):
    fine = Mesh(mesh.devices.reshape(8, 2, 8, 4), ("y", "core", "z", "x"))
    block = P(ROWS, COLS, None)
    return jax.shard_map(
        body,
        mesh=fine,
        in_specs=(block, block) + (P(),) * 10,
        out_specs=(block, block) + (P(),) * 8,
        check_vma=False,
    )
```

time: 197 us -> 181 us (0.919)
  blocking collectives: 83.5 us -> 44.2 us
  starting transfers between devices: 51.3 us -> 75.1 us
  local copies, waits for them, and re-layouts: 10.8 us -> 6.7 us
    all_to_all x4 -> x3, blocking collectives: 83.5 us -> 44.2 us  [swap(): return lax.all_to_all(value, axes, 0, 0, tiled=False)]
    all_to_all x2 -> x3, starting transfers between devices: 13.6 us -> 28.3 us  [swap(): return lax.all_to_all(value, axes, 0, 0, tiled=False)]
    ppermute x8 -> x12, starting transfers between devices: 37.8 us -> 46.8 us  [partner(): lax.ppermute(value, axis, [(at, at ^ flip) for at in range(lax.axis_size(...]
    all_to_all x2 -> x3, waiting for transfers between devices: 0.01 us -> 4.81 us  [swap(): return lax.all_to_all(value, axes, 0, 0, tiled=False)]
    unnamed x44 -> x52, local copies, waits for them, and re-layouts: 9.61 us -> 5.13 us
    ppermute x8 -> x12, waiting for transfers between devices: 27.4 us -> 24.3 us  [partner(): lax.ppermute(value, axis, [(at, at ^ flip) for at in range(lax.axis_size(...]
    pallas_call x3 -> x4, Pallas kernels: 15.1 us -> 15.4 us  [the longest x1 13 us: attend_call(): pl.pallas_call(attend_kernel, grid=(4,), in_specs=[pl.BlockSpec(memory_sp...]
  transfers between devices with their start and end apart: 10 -> 15, of which waited for: 7 -> 9; matrix products, arithmetic and copies ran while one was open for 1% -> 2% of each run, Pallas kernels for 0% -> 3%
where the time goes in v3:
time: 181 us; the launch traced here: 180 us
  starting transfers between devices  75.1 us (41%)
  blocking collectives  44.2 us (24%)
  waiting for transfers between devices  29.1 us (16%)
  Pallas kernels  22.2 us (12%)
  local copies, waits for them, and re-layouts  6.7 us (4%)
    ppermute x12, starting transfers between devices, partner(): lax.ppermute(value, axis, [(at, at ^ flip) for at in range(lax.axis_size(...  46.8 us
    all_to_all x3, blocking collectives, swap(): return lax.all_to_all(value, axes, 0, 0, tiled=False)  44.2 us
    all_to_all x3, starting transfers between devices, swap(): return lax.all_to_all(value, axes, 0, 0, tiled=False)  28.3 us
    ppermute x12, waiting for transfers between devices, partner(): lax.ppermute(value, axis, [(at, at ^ flip) for at in range(lax.axis_size(...  24.3 us
    pallas_call x1, Pallas kernels, attend_call(): pl.pallas_call(attend_kernel, grid=(4,), in_specs=[pl.BlockSpec(memory_sp...  13 us
    unnamed x52, local copies, waits for them, and re-layouts  5.13 us
    all_to_all x3, waiting for transfers between devices, swap(): return lax.all_to_all(value, axes, 0, 0, tiled=False)  4.81 us
  transfers between devices with their start and end apart: 15, of which 9 were waited for; matrix products, arithmetic and copies ran while one was open for 2% of the time, Pallas kernels for 3%

profile of v3, /device:TPU:1, one launch (start us, length us, event | category | flops | bytes accessed | tf_op | source)
XLA Modules:
  0.0 179.7 jit_solution(4258549286393418469)
XLA Ops:
  0.7 0.6 copy-done.15
  1.3 0.9 copy-done
  2.3 0.7 copy-done.12
  2.9 1.1 norm_bias.1
  4.1 13.9 %all-to-all-start = ((f32[32,4,128]{2,1,0:T(4,128)}), f32[32,4,128]{2,1,0:T(4,128)S(1)}, u32[]{:S(2)}, u32[]{:S(2)}) async-start(f32[32,4,128]{2,1,0:T(4,128)} %bitcast.6), calls=%async_computation | async-start | bytes 131072 | tf_op jit(solution)/shard_map/all_to_all | solution.py:347
  18.1 0.5 copy-done.10
  18.7 2.3 %project.1 = (f32[8,4,64,128]{3,2,1,0:T(8,128)}, f32[512,128]{1,0:T(8,128)S(1)}, f32[512,128]{1,0:T(8,128)S(1)}, s32[4,512]{1,0:T(4,128)S(1)}) custom-call(s32[3]{0:T(128)S(1)} %pad_add_fusion.refs_0_.place_ref, f32[512,128]{1,0:T(8,128)S(1)} %get-tuple-element.36.refs_1_.refs_2_.scaled_ref, f32[16,32,128]{2,1,0:T(8,128)S(1)} %copy-done.1, ...), custom_call_target="tpu_custom_call" | custom-call | flops 2000000000 | bytes 4000000 | tf_op jit(solution)/shard_map/project/pallas_call | solution.py:371
  21.1 0.7 copy-done.20
  21.8 0.7 copy-done.22
  22.5 4.3 %all-to-all-done = f32[32,4,128]{2,1,0:T(4,128)S(1)} async-done(((f32[32,4,128]{2,1,0:T(4,128)}), f32[32,4,128]{2,1,0:T(4,128)S(1)}, u32[]{:S(2)}, u32[]{:S(2)}) %all-to-all-start) | async-done | bytes 65568 | tf_op jit(solution)/shard_map/all_to_all | solution.py:347
  26.7 5.0 %all-to-all-start.1 = ((f32[32,64,128]{2,1,0:T(8,128)}), f32[32,64,128]{2,1,0:T(8,128)S(1)}, u32[]{:S(2)}, u32[]{:S(2)}) async-start(f32[32,64,128]{2,1,0:T(8,128)} %bitcast.7), calls=%async_computation.1 | async-start | bytes 2097152 | tf_op jit(solution)/shard_map/all_to_all | solution.py:347
  31.7 0.1 copy.33
  31.9 0.2 copy.34
  32.1 0.1 copy.39
  32.2 5.9 %collective-permute-start.2 = (f32[1,32,512]{2,1,0:T(8,128)S(1)}, f32[1,32,512]{2,1,0:T(8,128)S(1)}, u32[]{:S(2)}, u32[]{:S(2)}) collective-permute-start(f32[1,32,512]{2,1,0:T(8,128)S(1)} %copy.39), channel_id=1, source_target_pairs={{0,384},{64,448},{128,256},{192,320},{256,128},{320,192},{384,0},{... | collective-permute-start | bytes 196616 | tf_op jit(solution)/shard_map/ppermute | solution.py:351
  38.0 3.8 %collective-permute-start.1 = (f32[1,32,512]{2,1,0:T(8,128)S(1)}, f32[1,32,512]{2,1,0:T(8,128)S(1)}, u32[]{:S(2)}, u32[]{:S(2)}) collective-permute-start(f32[1,32,512]{2,1,0:T(8,128)S(1)} %copy.39), channel_id=1, source_target_pairs={{0,128},{64,192},{128,0},{192,64},{256,384},{320,448},{384,256},{4... | collective-permute-start | bytes 196616 | tf_op jit(solution)/shard_map/ppermute | solution.py:351
  41.8 2.1 %collective-permute-start = (f32[1,32,512]{2,1,0:T(8,128)S(1)}, f32[1,32,512]{2,1,0:T(8,128)S(1)}, u32[]{:S(2)}, u32[]{:S(2)}) collective-permute-start(f32[1,32,512]{2,1,0:T(8,128)S(1)} %copy.39), channel_id=1, source_target_pairs={{0,256},{64,320},{128,384},{192,448},{256,0},{320,64},{384,128},{4... | collective-permute-start | bytes 196616 | tf_op jit(solution)/shard_map/ppermute | solution.py:351
  44.0 1.0 collective-permute-done.1
  45.0 6.4 %collective-permute-done = f32[1,32,512]{2,1,0:T(8,128)S(1)} collective-permute-done((f32[1,32,512]{2,1,0:T(8,128)S(1)}, f32[1,32,512]{2,1,0:T(8,128)S(1)}, u32[]{:S(2)}, u32[]{:S(2)}) %collective-permute-start) | collective-permute-done | bytes 65568 | tf_op jit(solution)/shard_map/ppermute | solution.py:351
  51.3 2.0 %collective-permute-start.3 = (f32[4,32,512]{2,1,0:T(8,128)S(1)}, f32[4,32,512]{2,1,0:T(8,128)S(1)}, u32[]{:S(2)}, u32[]{:S(2)}) collective-permute-start(f32[4,32,512]{2,1,0:T(8,128)S(1)} %pad_maximum_fusion), channel_id=1, source_target_pairs={{0,64},{64,0},{128,192},{192,128},{256,320},{320,256},{384,448},{4... | collective-permute-start | bytes 786440 | tf_op jit(solution)/shard_map/ppermute | solution.py:351
  53.4 5.3 %collective-permute-done.3 = f32[4,32,512]{2,1,0:T(8,128)S(1)} collective-permute-done((f32[4,32,512]{2,1,0:T(8,128)S(1)}, f32[4,32,512]{2,1,0:T(8,128)S(1)}, u32[]{:S(2)}, u32[]{:S(2)}) %collective-permute-start.3) | collective-permute-done | bytes 262176 | tf_op jit(solution)/shard_map/ppermute | solution.py:351
  58.8 6.1 %collective-permute-start.4 = (f32[8,32,512]{2,1,0:T(8,128)S(1)}, f32[8,32,512]{2,1,0:T(8,128)S(1)}, u32[]{:S(2)}, u32[]{:S(2)}) collective-permute-start(f32[8,32,512]{2,1,0:T(8,128)S(1)} %constant_dynamic-update-slice_fusion.own_ref), channel_id=1, source_target_pairs={{0,32},{32,0},{1,33},{33,1},{2,34},{34,2},{3,35},{35,3},{4,36},{36... | collective-permute-start | bytes 1572872 | tf_op jit(solution)/shard_map/ppermute | solution.py:351
  64.9 1.5 collective-permute-done.4.other_ref
  66.4 13.0 %attend.1 = (f32[32,64,128]{2,1,0:T(8,128)}, f32[8,32,512]{2,1,0:T(8,128)S(1)}, f32[8,32,512]{2,1,0:T(8,128)S(1)}) custom-call(s32[3]{0:T(128)S(1)} %pad_add_fusion.refs_0_.place_ref, s32[4,512]{1,0:T(4,128)S(1)} %get-tuple-element.37.keep_ref, f32[32,64,128]{2,1,0:T(8,128)S(1)} %all-to-all-done.1.data_ref, ...), custom_call_target="tpu_custom_call" | custom-call | flops 12000000000 | bytes 24000000 | tf_op jit(solution)/shard_map/attend/pallas_call | solution.py:328
  79.4 9.5 %all-to-all-start.2 = ((f32[32,64,128]{2,1,0:T(8,128)}), f32[32,64,128]{2,1,0:T(8,128)S(1)}, u32[]{:S(2)}, u32[]{:S(2)}) async-start(f32[32,64,128]{2,1,0:T(8,128)} %get-tuple-element.42), calls=%async_computation.2 | async-start | bytes 2097152 | tf_op jit(solution)/shard_map/all_to_all | solution.py:347
  88.9 2.6 %collective-permute-start.6 = (f32[8,32,512]{2,1,0:T(8,128)S(1)}, f32[8,32,512]{2,1,0:T(8,128)S(1)}, u32[]{:S(2)}, u32[]{:S(2)}) collective-permute-start(f32[8,32,512]{2,1,0:T(8,128)S(1)} %get-tuple-element.49), channel_id=1, source_target_pairs={{0,32},{32,0},{1,33},{33,1},{2,34},{34,2},{3,35},{35,3},{4,36},{36... | collective-permute-start | bytes 1572872 | tf_op jit(solution)/shard_map/ppermute | solution.py:351
  91.5 1.5 collective-permute-done.6
  93.1 1.9 %collective-permute-start.7 = (f32[4,32,512]{2,1,0:T(8,128)S(1)}, f32[4,32,512]{2,1,0:T(8,128)S(1)}, u32[]{:S(2)}, u32[]{:S(2)}) collective-permute-start(f32[4,32,512]{2,1,0:T(8,128)S(1)} %slice.25), channel_id=1, source_target_pairs={{0,64},{64,0},{128,192},{192,128},{256,320},{320,256},{384,448},{4... | collective-permute-start | bytes 786440 | tf_op jit(solution)/shard_map/ppermute | solution.py:351
  95.1 7.5 %collective-permute-done.7 = f32[4,32,512]{2,1,0:T(8,128)S(1)} collective-permute-done((f32[4,32,512]{2,1,0:T(8,128)S(1)}, f32[4,32,512]{2,1,0:T(8,128)S(1)}, u32[]{:S(2)}, u32[]{:S(2)}) %collective-permute-start.7) | collective-permute-done | bytes 262176 | tf_op jit(solution)/shard_map/ppermute | solution.py:351
  102.6 0.7 slice_bitcast_fusion.1
  103.3 1.9 %collective-permute-start.9 = (f32[32,512]{1,0:T(8,128)}, f32[32,512]{1,0:T(8,128)}, u32[]{:S(2)}, u32[]{:S(2)}) collective-permute-start(f32[32,512]{1,0:T(8,128)} %get-tuple-element.62), channel_id=1, source_target_pairs={{0,128},{64,192},{128,0},{192,64},{256,384},{320,448},{384,256},{4... | collective-permute-start | bytes 196616 | tf_op jit(solution)/shard_map/ppermute | solution.py:351
  105.2 2.0 %collective-permute-start.10 = (f32[32,512]{1,0:T(8,128)}, f32[32,512]{1,0:T(8,128)}, u32[]{:S(2)}, u32[]{:S(2)}) collective-permute-start(f32[32,512]{1,0:T(8,128)} %get-tuple-element.63), channel_id=1, source_target_pairs={{0,384},{64,448},{128,256},{192,320},{256,128},{320,192},{384,0},{... | collective-permute-start | bytes 196616 | tf_op jit(solution)/shard_map/ppermute | solution.py:351
  107.2 7.5 %collective-permute-start.8 = (f32[32,512]{1,0:T(8,128)S(1)}, f32[32,512]{1,0:T(8,128)}, u32[]{:S(2)}, u32[]{:S(2)}) collective-permute-start(f32[32,512]{1,0:T(8,128)S(1)} %get-tuple-element.64), channel_id=1, source_target_pairs={{0,256},{64,320},{128,384},{192,448},{256,0},{320,64},{384,128},{4... | collective-permute-start | bytes 196616 | tf_op jit(solution)/shard_map/ppermute | solution.py:351
  114.7 0.6 all-to-all-done.2
  115.3 2.7 %block_grads.1 = (f32[16,32,128]{2,1,0:T(8,128)}, f32[512,128]{1,0:T(8,128)S(1)}, f32[320,128]{1,0:T(8,128)S(1)}, f32[320,128]{1,0:T(8,128)S(1)}) custom-call(s32[3]{0:T(128)S(1)} %pad_add_fusion.refs_0_.place_ref, f32[8,4,64,128]{3,2,1,0:T(8,128)S(1)} %bitcast.29, f32[512,128]{1,0:T(8,128)S(1)} %copy-done.17, f32[512,128]{1,0:T(8,128)S(1)} %copy-done.21, ...), custom_call_target="tpu_custom_call" | custom-call | flops 2000000000 | bytes 4000000 | tf_op jit(solution)/shard_map/block_grads/pallas_call | solution.py:398
  118.0 4.6 %collective-permute-start.5 = (f32[320,128]{1,0:T(8,128)S(1)}, f32[320,128]{1,0:T(8,128)S(1)}, u32[]{:S(2)}, u32[]{:S(2)}) collective-permute-start(f32[320,128]{1,0:T(8,128)S(1)} %get-tuple-element.47), channel_id=1, source_target_pairs={{0,32},{32,0},{1,33},{33,1},{2,34},{34,2},{3,35},{35,3},{4,36},{36... | collective-permute-start | bytes 491528 | tf_op jit(solution)/shard_map/ppermute | solution.py:351
  122.6 0.9 fusion
  123.5 0.1 copy.40
  123.7 0.2 copy.41
  123.9 0.1 copy.42
  124.1 20.3 %all_to_all.30.recv_ref = f32[32,14,128]{2,1,0:T(8,128)S(1)} all-to-all(f32[32,14,128]{2,1,0:T(8,128)S(1)} %pad_maximum_fusion.1), channel_id=1, replica_groups=mesh['y'=8,'core'=2,'z'=8,'x'=4] {'z','x'}, dimensions={0} | all-to-all | bytes 458752 | tf_op jit(solution)/shard_map/all_to_all | solution.py:347
  144.4 0.7 copy-done.13
  145.1 1.3 norm_back.1
  146.3 9.6 %all_to_all.31.recv_ref = f32[8,16,128]{2,1,0:T(8,128)S(1)} all-to-all(f32[8,16,128]{2,1,0:T(8,128)S(1)} %get-tuple-element.53), channel_id=1, replica_groups=mesh['y'=8,'core'=2,'z'=8,'x'=4] {'y'}, dimensions={0} | all-to-all | bytes 131072 | tf_op jit(solution)/shard_map/all_to_all | solution.py:347
  155.9 14.4 %all_to_all.32.refs_1_ = f32[32,16,128]{2,1,0:T(8,128)S(1)} all-to-all(f32[32,16,128]{2,1,0:T(8,128)S(1)} %share.1), channel_id=1, replica_groups=mesh['y'=8,'core'=2,'z'=8,'x'=4] {'z','x'}, dimensions={0} | all-to-all | bytes 524288 | tf_op jit(solution)/shard_map/all_to_all | solution.py:347
  170.3 6.4 %collective-permute-start.11 = (f32[32,16,128]{2,1,0:T(8,128)S(1)}, f32[32,16,128]{2,1,0:T(8,128)S(1)}, u32[]{:S(2)}, u32[]{:S(2)}) collective-permute-start(f32[32,16,128]{2,1,0:T(8,128)S(1)} %all_to_all.32.refs_1_), channel_id=1, source_target_pairs={{0,32},{32,0},{1,33},{33,1},{2,34},{34,2},{3,35},{35,3},{4,36},{36... | collective-permute-start | bytes 786440 | tf_op jit(solution)/shard_map/ppermute | solution.py:351
  176.8 1.1 collective-permute-done.11.refs_2_
  177.9 1.8 finish.1
  (61 shorter events, 0.6 us)
Async XLA Ops:
  0.6 0.7 copy-start.15
  1.3 0.9 copy-start
  2.2 0.7 copy-start.12
  2.9 15.1 %copy-start.1 = (f32[16,32,128]{2,1,0:T(8,128)S(1)}, f32[16,32,128]{2,1,0:T(8,128)}, u32[]{:S(2)}) copy-start(f32[16,32,128]{2,1,0:T(8,128)} %refs_5_.4) | copy-start | bytes 786436
  2.9 15.1 %copy-start.4 = (f32[128,128]{1,0:T(8,128)S(1)}, f32[128,128]{1,0:T(8,128)}, u32[]{:S(2)}) copy-start(f32[128,128]{1,0:T(8,128)} %refs_5_.5) | copy-start | bytes 196612
  2.9 15.1 %copy-start.6 = (f32[128,128]{1,0:T(8,128)S(1)}, f32[128,128]{1,0:T(8,128)}, u32[]{:S(2)}) copy-start(f32[128,128]{1,0:T(8,128)} %refs_6_.5) | copy-start | bytes 196612
  2.9 15.1 %copy-start.8 = (f32[128,128]{1,0:T(8,128)S(1)}, f32[128,128]{1,0:T(8,128)}, u32[]{:S(2)}) copy-start(f32[128,128]{1,0:T(8,128)} %refs_7_.5) | copy-start | bytes 196612
  4.0 17.0 %copy-start.16 = (f32[512,128]{1,0:T(8,128)}, f32[512,128]{1,0:T(8,128)S(1)}, u32[]{:S(2)}) copy-start(f32[512,128]{1,0:T(8,128)S(1)} %get-tuple-element.36.refs_1_.refs_2_.scaled_ref) | copy-start | bytes 786436
  4.1 17.0 %copy-start.18 = (f32[512,128]{1,0:T(8,128)}, f32[512,128]{1,0:T(8,128)S(1)}, u32[]{:S(2)}) copy-start(f32[512,128]{1,0:T(8,128)S(1)} %get-tuple-element.51.inv_ref) | copy-start | bytes 786436
  4.1 14.0 %copy-start.2 = (f32[128,128]{1,0:T(8,128)S(1)}, f32[128,128]{1,0:T(8,128)}, u32[]{:S(2)}) copy-start(f32[128,128]{1,0:T(8,128)} %refs_10_.1) | copy-start | bytes 196612
  4.1 14.0 %copy-start.3 = (f32[128,128]{1,0:T(8,128)S(1)}, f32[128,128]{1,0:T(8,128)}, u32[]{:S(2)}) copy-start(f32[128,128]{1,0:T(8,128)} %refs_4_.3) | copy-start | bytes 196612
  4.1 22.7 %all-to-all-start = ((f32[32,4,128]{2,1,0:T(4,128)}), f32[32,4,128]{2,1,0:T(4,128)S(1)}, u32[]{:S(2)}, u32[]{:S(2)}) async-start(f32[32,4,128]{2,1,0:T(4,128)} %bitcast.6), calls=%async_computation | async-start | bytes 131072 | tf_op jit(solution)/shard_map/all_to_all | solution.py:347
  17.9 0.7 copy-start.10
  18.0 0.7 copy-start.11
  18.0 0.7 copy-start.14
  21.0 0.7 copy-start.20
  21.8 0.7 copy-start.22
  26.7 39.6 %all-to-all-start.1 = ((f32[32,64,128]{2,1,0:T(8,128)}), f32[32,64,128]{2,1,0:T(8,128)S(1)}, u32[]{:S(2)}, u32[]{:S(2)}) async-start(f32[32,64,128]{2,1,0:T(8,128)} %bitcast.7), calls=%async_computation.1 | async-start | bytes 2097152 | tf_op jit(solution)/shard_map/all_to_all | solution.py:347
  32.2 11.8 %collective-permute-start.2 = (f32[1,32,512]{2,1,0:T(8,128)S(1)}, f32[1,32,512]{2,1,0:T(8,128)S(1)}, u32[]{:S(2)}, u32[]{:S(2)}) collective-permute-start(f32[1,32,512]{2,1,0:T(8,128)S(1)} %copy.39), channel_id=1, source_target_pairs={{0,384},{64,448},{128,256},{192,320},{256,128},{320,192},{384,0},{... | collective-permute-start | bytes 196616 | tf_op jit(solution)/shard_map/ppermute | solution.py:351
  38.0 6.9 %collective-permute-start.1 = (f32[1,32,512]{2,1,0:T(8,128)S(1)}, f32[1,32,512]{2,1,0:T(8,128)S(1)}, u32[]{:S(2)}, u32[]{:S(2)}) collective-permute-start(f32[1,32,512]{2,1,0:T(8,128)S(1)} %copy.39), channel_id=1, source_target_pairs={{0,128},{64,192},{128,0},{192,64},{256,384},{320,448},{384,256},{4... | collective-permute-start | bytes 196616 | tf_op jit(solution)/shard_map/ppermute | solution.py:351
  41.8 9.5 %collective-permute-start = (f32[1,32,512]{2,1,0:T(8,128)S(1)}, f32[1,32,512]{2,1,0:T(8,128)S(1)}, u32[]{:S(2)}, u32[]{:S(2)}) collective-permute-start(f32[1,32,512]{2,1,0:T(8,128)S(1)} %copy.39), channel_id=1, source_target_pairs={{0,256},{64,320},{128,384},{192,448},{256,0},{320,64},{384,128},{4... | collective-permute-start | bytes 196616 | tf_op jit(solution)/shard_map/ppermute | solution.py:351
  51.3 7.4 %collective-permute-start.3 = (f32[4,32,512]{2,1,0:T(8,128)S(1)}, f32[4,32,512]{2,1,0:T(8,128)S(1)}, u32[]{:S(2)}, u32[]{:S(2)}) collective-permute-start(f32[4,32,512]{2,1,0:T(8,128)S(1)} %pad_maximum_fusion), channel_id=1, source_target_pairs={{0,64},{64,0},{128,192},{192,128},{256,320},{320,256},{384,448},{4... | collective-permute-start | bytes 786440 | tf_op jit(solution)/shard_map/ppermute | solution.py:351
  58.8 7.6 %collective-permute-start.4 = (f32[8,32,512]{2,1,0:T(8,128)S(1)}, f32[8,32,512]{2,1,0:T(8,128)S(1)}, u32[]{:S(2)}, u32[]{:S(2)}) collective-permute-start(f32[8,32,512]{2,1,0:T(8,128)S(1)} %constant_dynamic-update-slice_fusion.own_ref), channel_id=1, source_target_pairs={{0,32},{32,0},{1,33},{33,1},{2,34},{34,2},{3,35},{35,3},{4,36},{36... | collective-permute-start | bytes 1572872 | tf_op jit(solution)/shard_map/ppermute | solution.py:351
  79.4 35.8 %all-to-all-start.2 = ((f32[32,64,128]{2,1,0:T(8,128)}), f32[32,64,128]{2,1,0:T(8,128)S(1)}, u32[]{:S(2)}, u32[]{:S(2)}) async-start(f32[32,64,128]{2,1,0:T(8,128)} %get-tuple-element.42), calls=%async_computation.2 | async-start | bytes 2097152 | tf_op jit(solution)/shard_map/all_to_all | solution.py:347
  88.9 4.1 %collective-permute-start.6 = (f32[8,32,512]{2,1,0:T(8,128)S(1)}, f32[8,32,512]{2,1,0:T(8,128)S(1)}, u32[]{:S(2)}, u32[]{:S(2)}) collective-permute-start(f32[8,32,512]{2,1,0:T(8,128)S(1)} %get-tuple-element.49), channel_id=1, source_target_pairs={{0,32},{32,0},{1,33},{33,1},{2,34},{34,2},{3,35},{35,3},{4,36},{36... | collective-permute-start | bytes 1572872 | tf_op jit(solution)/shard_map/ppermute | solution.py:351
  93.1 9.4 %collective-permute-start.7 = (f32[4,32,512]{2,1,0:T(8,128)S(1)}, f32[4,32,512]{2,1,0:T(8,128)S(1)}, u32[]{:S(2)}, u32[]{:S(2)}) collective-permute-start(f32[4,32,512]{2,1,0:T(8,128)S(1)} %slice.25), channel_id=1, source_target_pairs={{0,64},{64,0},{128,192},{192,128},{256,320},{320,256},{384,448},{4... | collective-permute-start | bytes 786440 | tf_op jit(solution)/shard_map/ppermute | solution.py:351
  102.6 12.7 %copy-start.17 = (f32[512,128]{1,0:T(8,128)S(1)}, f32[512,128]{1,0:T(8,128)}, u32[]{:S(2)}) copy-start(f32[512,128]{1,0:T(8,128)} %copy-done.16) | copy-start | bytes 786436
  102.6 12.7 %copy-start.21 = (f32[512,128]{1,0:T(8,128)S(1)}, f32[512,128]{1,0:T(8,128)}, u32[]{:S(2)}) copy-start(f32[512,128]{1,0:T(8,128)} %copy-done.20) | copy-start | bytes 786436
  102.6 12.7 %copy-start.23 = (f32[512,128]{1,0:T(8,128)S(1)}, f32[512,128]{1,0:T(8,128)}, u32[]{:S(2)}) copy-start(f32[512,128]{1,0:T(8,128)} %copy-done.22) | copy-start | bytes 786436
  102.6 12.7 %copy-start.5 = (f32[128,128]{1,0:T(8,128)S(1)}, f32[128,128]{1,0:T(8,128)}, u32[]{:S(2)}) copy-start(f32[128,128]{1,0:T(8,128)} %refs_5_.5) | copy-start | bytes 196612
  102.6 12.7 %copy-start.7 = (f32[128,128]{1,0:T(8,128)S(1)}, f32[128,128]{1,0:T(8,128)}, u32[]{:S(2)}) copy-start(f32[128,128]{1,0:T(8,128)} %refs_6_.5) | copy-start | bytes 196612
  102.6 12.7 %copy-start.9 = (f32[128,128]{1,0:T(8,128)S(1)}, f32[128,128]{1,0:T(8,128)}, u32[]{:S(2)}) copy-start(f32[128,128]{1,0:T(8,128)} %refs_7_.5) | copy-start | bytes 196612
  103.3 19.3 %collective-permute-start.9 = (f32[32,512]{1,0:T(8,128)}, f32[32,512]{1,0:T(8,128)}, u32[]{:S(2)}, u32[]{:S(2)}) collective-permute-start(f32[32,512]{1,0:T(8,128)} %get-tuple-element.62), channel_id=1, source_target_pairs={{0,128},{64,192},{128,0},{192,64},{256,384},{320,448},{384,256},{4... | collective-permute-start | bytes 196616 | tf_op jit(solution)/shard_map/ppermute | solution.py:351
  105.2 17.4 %collective-permute-start.10 = (f32[32,512]{1,0:T(8,128)}, f32[32,512]{1,0:T(8,128)}, u32[]{:S(2)}, u32[]{:S(2)}) collective-permute-start(f32[32,512]{1,0:T(8,128)} %get-tuple-element.63), channel_id=1, source_target_pairs={{0,384},{64,448},{128,256},{192,320},{256,128},{320,192},{384,0},{... | collective-permute-start | bytes 196616 | tf_op jit(solution)/shard_map/ppermute | solution.py:351
  107.2 15.4 %collective-permute-start.8 = (f32[32,512]{1,0:T(8,128)S(1)}, f32[32,512]{1,0:T(8,128)}, u32[]{:S(2)}, u32[]{:S(2)}) collective-permute-start(f32[32,512]{1,0:T(8,128)S(1)} %get-tuple-element.64), channel_id=1, source_target_pairs={{0,256},{64,320},{128,384},{192,448},{256,0},{320,64},{384,128},{4... | collective-permute-start | bytes 196616 | tf_op jit(solution)/shard_map/ppermute | solution.py:351
  118.0 6.0 %collective-permute-start.5 = (f32[320,128]{1,0:T(8,128)S(1)}, f32[320,128]{1,0:T(8,128)S(1)}, u32[]{:S(2)}, u32[]{:S(2)}) collective-permute-start(f32[320,128]{1,0:T(8,128)S(1)} %get-tuple-element.47), channel_id=1, source_target_pairs={{0,32},{32,0},{1,33},{33,1},{2,34},{34,2},{3,35},{35,3},{4,36},{36... | collective-permute-start | bytes 491528 | tf_op jit(solution)/shard_map/ppermute | solution.py:351
  124.1 20.3 %copy-start.19 = (f32[512,128]{1,0:T(8,128)S(1)}, f32[512,128]{1,0:T(8,128)}, u32[]{:S(2)}) copy-start(f32[512,128]{1,0:T(8,128)} %copy-done.18) | copy-start | bytes 786436
  144.4 0.7 copy-start.13
  170.3 7.6 %collective-permute-start.11 = (f32[32,16,128]{2,1,0:T(8,128)S(1)}, f32[32,16,128]{2,1,0:T(8,128)S(1)}, u32[]{:S(2)}, u32[]{:S(2)}) collective-permute-start(f32[32,16,128]{2,1,0:T(8,128)S(1)} %all_to_all.32.refs_1_), channel_id=1, source_target_pairs={{0,32},{32,0},{1,33},{33,1},{2,34},{34,2},{3,35},{35,3},{4,36},{36... | collective-permute-start | bytes 786440 | tf_op jit(solution)/shard_map/ppermute | solution.py:351

commit v4 on v3

--- a/solution.py
+++ b/solution.py
@@ -11,6 +11,7 @@
 ROWS = ("z", "x")
 COLS = ("y", "core")
 VMEM_BYTES = 48 * 1024 * 1024
+MOST_VMEM = 60 * 1024 * 1024
 NN = (((1,), (0,)), ((), ()))
 NT = (((1,), (1,)), ((), ()))
 
@@ -94,42 +95,55 @@
         keep_ref[column : column + 1, :] = jnp.where(chain == own, 1, open_block)
 
 
-def spread_lanes(value, group):
-    lane = lanes_of(value.shape)
-    kept = jnp.where((lane >= 32 * group) & (lane < 32 * group + 32), value, 0.0)
-    kept = kept + pltpu.roll(kept, 32, 1)
-    return kept + pltpu.roll(kept, 64, 1)
-
-
-def parts_of(value):
-    high = value.astype(BF16).astype(F32)
-    return high, value - high
-
-
-def attend_kernel(place_ref, keep_ref, data_ref, own_ref, other_ref, out_ref, d_own_ref, d_other_ref):
-    column = pl.program_id(0)
+def picker(groups):
+    shape = (256, 128)
+    source, lane = lax.broadcasted_iota(jnp.int32, shape, 0), lanes_of(shape)
+    wanted = jnp.full(shape, -1, jnp.int32)
+    for group, pick in enumerate(groups):
+        if pick is not None:
+            wanted = jnp.where(lane // 32 == group, pick[0] * 128 + pick[1] * 32 + lane % 32, wanted)
+    return jnp.where(source == wanted, 1.0, 0.0)
+
+
+def left(group):
+    return [(0, group), (1, group), (0, group), (1, group)]
+
+
+def right(group):
+    return [(0, group), (0, group), (1, group), (1, group)]
+
+
+def fill_pickers(keys_ref, rows_ref, turns_ref):
+    keys = [
+        right(1),
+        right(2),
+        [(0, 1), (1, 1), None, None],
+        [(0, 1), None, None, None],
+        [None, None, (1, 2), (0, 2)],
+        [None, None, None, (0, 2)],
+    ]
+    for at, groups in enumerate(keys):
+        keys_ref[:, at * 128 : (at + 1) * 128] = picker(groups).astype(BF16)
+    for at, group in enumerate((0, 3)):
+        pick = picker(left(group))
+        rows_ref[:, at * 128 : (at + 1) * 128] = pick.astype(BF16)
+        turns_ref[at * 64 : (at + 1) * 64, :] = jnp.transpose(pick)[0:64].astype(BF16)
+
+
+def halves_of(value):
+    high = value.astype(BF16)
+    return jnp.concatenate([high, (value - high.astype(F32)).astype(BF16)], axis=1)
+
+
+def attend_kernel(
+    place_ref, keep_ref, data_ref, own_ref, other_ref, out_ref, d_own_ref, d_other_ref,
+    keys_ref, rows_ref, turns_ref,
+):
     y, core = place_ref[0], place_ref[1]
-
-    @pl.when(column == 0)
-    def _():
-        d_own_ref[...] = jnp.zeros_like(d_own_ref)
-        d_other_ref[...] = jnp.zeros_like(d_other_ref)
-
-    data = data_ref[...].reshape(512, 128)
-    lane = lanes_of((512, 128))
-    kh, kl = parts_of(spread_lanes(data, 1))
-    vh, vl = parts_of(spread_lanes(data, 2))
-    k_right = jnp.where(lane < 64, kh, kl).astype(BF16)
-    v_right = jnp.where(lane < 64, vh, vl).astype(BF16)
-    k_first = jnp.where(lane < 32, kh, 0.0).astype(BF16)
-    k_both = jnp.where(lane < 32, kh, jnp.where(lane < 64, kl, 0.0)).astype(BF16)
-    v_first = jnp.where(lane >= 96, vh, 0.0).astype(BF16)
-    v_both = jnp.where(lane >= 96, vh, jnp.where(lane >= 64, vl, 0.0)).astype(BF16)
-    keep = keep_ref[pl.ds(column, 1), :] > 0
+    fill_pickers(keys_ref, rows_ref, turns_ref)
     chunk_rows = 256
     per = chunk_rows // 32
     sub = lanes_of((chunk_rows, 128))
-    odd = (sub // 32) % 2 == 1
     chunks = []
     for side, (bias_ref, db_ref) in enumerate(((own_ref, d_own_ref), (other_ref, d_other_ref))):
         half = core if side == 0 else 1 - core
@@ -137,16 +151,25 @@
             starts = [(y ^ ((s >> 2) | (s & 2) | ((s & 1) << 2))) * 4 + half * 2 for s in range(s0, s0 + per)]
             chunks.append((starts, bias_ref, db_ref, s0))
 
-    def first(chunk):
+    def column_keys(column):
+        here = pl.ds(column * 16, 16)
+        picked = bdot(halves_of(data_ref[:, here].reshape(512, 128)), keys_ref[...]).astype(BF16)
+        return [picked[:, at * 128 : (at + 1) * 128] for at in range(6)] + [keep_ref[column : column + 1, :] > 0]
+
+    def first(column, keys, chunk):
+        k_right, v_right, k_both, k_first, v_both, v_first, keep = keys
         starts, bias_ref, db_ref, s0 = chunk
-        rows = jnp.concatenate([data_ref[pl.ds(start, 2)].reshape(32, 128) for start in starts], axis=0)
-        qh, ql = parts_of(spread_lanes(rows, 0))
-        q_left = jnp.where(odd, ql, qh)
-        scores = bdot(q_left.astype(BF16), k_right, NT) + bias_ref[s0 : s0 + per].reshape(chunk_rows, 512)
-        return rows, q_left, jnp.where(keep, scores, NEG_FILL)
-
-    def second(state):
-        rows, q_left, scores = state
+        here = pl.ds(column * 16, 16)
+        rows = jnp.concatenate([data_ref[pl.ds(start, 2), here].reshape(32, 128) for start in starts], axis=0)
+        both = halves_of(rows)
+        q_left = bdot(both, rows_ref[:, 0:128]).astype(BF16)
+        q_t = bdot(turns_ref[0:64], both, NT).astype(BF16)
+        scores = bdot(q_left, k_right, NT) + bias_ref[s0 : s0 + per].reshape(chunk_rows, 512)
+        return rows, q_t, jnp.where(keep, scores, NEG_FILL)
+
+    def second(keys, state):
+        k_right, v_right, k_both, k_first, v_both, v_first, keep = keys
+        rows, q_t, scores = state
         highest = jnp.max(scores, axis=1, keepdims=True)
         weights = jnp.exp(scores - highest)
         inv_total = 1.0 / jnp.sum(weights, axis=1, keepdims=True)
@@ -155,85 +178,102 @@
         output = (output + pltpu.roll(output, 32, 1)) * inv_total
         d_out = jnp.where(sub >= 96, rows, 0.0) * inv_total
         centred = jnp.sum(d_out * output, axis=1, keepdims=True)
-        dh, dl = parts_of(spread_lanes(d_out, 3))
-        d_left = jnp.where(odd, dl, dh)
-        d_weights = bdot(d_left.astype(BF16), v_right, NT)
-        d_t = jnp.transpose(d_left)[0:64].astype(BF16)
+        d_both = halves_of(d_out)
+        d_left = bdot(d_both, rows_ref[:, 128:256]).astype(BF16)
+        d_weights = bdot(d_left, v_right, NT)
+        d_t = bdot(turns_ref[64:128], d_both, NT).astype(BF16)
         both = bdot(d_t, wh)
         dv_t = both[0:32] + both[32:64] + bdot(d_t[0:32], wl)
-        return weights, output, d_weights, centred, dv_t, q_left
-
-    def third(chunk, state):
+        return weights, output, d_weights, centred, dv_t, q_t
+
+    def third(column, keys, chunk, state):
+        k_right, v_right, k_both, k_first, v_both, v_first, keep = keys
         starts, bias_ref, db_ref, s0 = chunk
-        weights, output, d_weights, centred, dv_t, q_left = state
+        weights, output, d_weights, centred, dv_t, q_t = state
         d_scores = weights * (d_weights - centred)
-        db_ref[s0 : s0 + per] += d_scores.reshape(per, 32, 512)
+        if column == 0:
+            db_ref[s0 : s0 + per] = d_scores.reshape(per, 32, 512)
+        else:
+            db_ref[s0 : s0 + per] += d_scores.reshape(per, 32, 512)
         sh, sl = split(d_scores)
         d_query = bdot(sh, k_both) + bdot(sl, k_first)
         d_query = d_query + pltpu.roll(d_query, 96, 1)
-        q_t = jnp.transpose(q_left)[0:64].astype(BF16)
         both = bdot(q_t, sh)
         dk_t = both[0:32] + both[32:64] + bdot(q_t[0:32], sl)
         return jnp.where(sub < 32, d_query, output), dk_t, dv_t
 
-    n = len(chunks)
-    ones, twos, dones = {}, {}, {}
-    for step in range(n + 2):
-        if step < n:
-            ones[step] = first(chunks[step])
-        if 0 <= step - 1 < n:
-            twos[step - 1] = second(ones.pop(step - 1))
-        if 0 <= step - 2 < n:
-            dones[step - 2] = third(chunks[step - 2], twos.pop(step - 2))
-    zeros = jnp.zeros((32, 512), F32)
-    dk_t = sum(dones[c][1] for c in range(n))
-    dv_t = sum(dones[c][2] for c in range(n))
-    result = jnp.transpose(jnp.concatenate([zeros, dk_t, dv_t, zeros], axis=0))
-    out_ref[...] = result.reshape(32, 16, 128)
     mixed = (sub >= 32) & (sub < 96)
-    for c in range(n):
-        starts = chunks[c][0]
-        held = jnp.concatenate([out_ref[pl.ds(start, 2)].reshape(32, 128) for start in starts], axis=0)
-        value = jnp.where(mixed, held, dones[c][0])
-        for s, start in enumerate(starts):
-            out_ref[pl.ds(start, 2)] = value[s * 32 : (s + 1) * 32].reshape(2, 16, 128)
-
-
-def block_kernel(
-    factor, place_ref, recv_ref, scaled_ref, gate_ref, dgated_ref, cot_ref, wq_ref, wk_ref, wv_ref, wg_ref, wo_ref,
-    update_ref, dnorm_ref, keep_ref, give_ref, param_ref,
-):
+
+    def finish(column, done):
+        here = pl.ds(column * 16, 16)
+        zeros = jnp.zeros((32, 512), F32)
+        dk_t = sum(part[1] for part in done)
+        dv_t = sum(part[2] for part in done)
+        result = jnp.transpose(jnp.concatenate([zeros, dk_t, dv_t, zeros], axis=0))
+        out_ref[:, here] = result.reshape(32, 16, 128)
+        for (starts, _, _, _), part in zip(chunks, done):
+            held = jnp.concatenate([out_ref[pl.ds(start, 2), here].reshape(32, 128) for start in starts], axis=0)
+            value = jnp.where(mixed, held, part[0])
+            for s, start in enumerate(starts):
+                out_ref[pl.ds(start, 2), here] = value[s * 32 : (s + 1) * 32].reshape(2, 16, 128)
+
+    work = [(column, chunk) for column in range(4) for chunk in chunks]
+    keys, ones, twos, dones = {}, {}, {}, {}
+    for step in range(len(work) + 2):
+        if step < len(work):
+            column, chunk = work[step]
+            if column not in keys:
+                keys[column] = column_keys(column)
+            ones[step] = first(column, keys[column], chunk)
+        if 0 <= step - 1 < len(work):
+            twos[step - 1] = second(keys[work[step - 1][0]], ones.pop(step - 1))
+        if 0 <= step - 2 < len(work):
+            column, chunk = work[step - 2]
+            dones.setdefault(column, []).append(third(column, keys[column], chunk, twos.pop(step - 2)))
+            if len(dones[column]) == len(chunks):
+                finish(column, dones.pop(column))
+
+
+def gate_back(got_ref, gate_ref, dgated_ref):
     lane = lanes_of((512, 128))
-    scaled = scaled_ref[...]
     gate = gate_ref[...]
-    cot = jnp.swapaxes(cot_ref[...], 0, 1).reshape(512, 128)
-    wq, wk, wv, wg = wq_ref[...], wk_ref[...], wv_ref[...], wg_ref[...]
-    got = [recv_ref[:, head].reshape(512, 128) for head in range(4)]
-    att = turn(got[3], 0)
+    got = [got_ref[:, head].reshape(512, 128) for head in range(4)]
+    att = got[3]
     for head in range(3):
         moved = turn(got[head], 32 * head - 96)
         att = jnp.where((lane >= 32 * head) & (lane < 32 * head + 32), moved, att)
-    gated = gate * att
     d_pre = dgated_ref[...] * att * gate * (1.0 - gate)
-    update = dot3(gated, wo_ref[...])
-    update_ref[...] = jnp.swapaxes(update.reshape(32, 16, 128), 0, 1)
-    scaled_t = split(jnp.transpose(jnp.where(lane == 127, 1.0, scaled)))
-    d_normed = jnp.zeros((512, 128), F32)
-    for head in range(4):
-        grads = split(jnp.where(lane < 96, got[head], turn(d_pre, 96 - 32 * head)))
-        weights = head_weights(wq, wk, wv, wg, head, factor)
-        d_normed = d_normed + dot3(grads, weights, NT)
-        param_ref[head * 128 : (head + 1) * 128, :] = dot3(scaled_t, grads)
+    grads = [jnp.where(lane < 96, got[head], turn(d_pre, 96 - 32 * head)) for head in range(4)]
+    return grads, gate * att
+
+
+def param_kernel(place_ref, got_ref, scaled_ref, gate_ref, dgated_ref, cot_ref, keep_ref, give_ref, param_ref):
+    grads, gated = gate_back(got_ref, gate_ref, dgated_ref)
+    cot = jnp.swapaxes(cot_ref[...], 0, 1).reshape(512, 128)
+    scaled = jnp.where(lanes_of((512, 128)) == 127, 1.0, scaled_ref[...])
+    scaled_t = split(jnp.transpose(scaled))
+    for head in range(4):
+        param_ref[head * 128 : (head + 1) * 128, :] = dot3(scaled_t, grads[head])
     param_ref[512:640, :] = dot3(jnp.transpose(gated), cot)
-    dnorm_ref[...] = d_normed
     core = place_ref[1]
     keep_ref[...] = param_ref[pl.ds(pl.multiple_of(core * 320, 8), 320), :]
     give_ref[...] = param_ref[pl.ds(pl.multiple_of((1 - core) * 320, 8), 320), :]
 
 
-def close_kernel(
-    recv_ref, dnorm_ref, scaled_ref, inv_ref, gain_ref, wb_ref, grad_ref, send_ref
+def update_kernel(
+    factor, got_ref, gate_ref, dgated_ref, wq_ref, wk_ref, wv_ref, wg_ref, wo_ref, update_ref, dnorm_ref
 ):
+    grads, gated = gate_back(got_ref, gate_ref, dgated_ref)
+    wq, wk, wv, wg = wq_ref[...], wk_ref[...], wv_ref[...], wg_ref[...]
+    update = dot3(gated, wo_ref[...])
+    update_ref[...] = jnp.swapaxes(update.reshape(32, 16, 128), 0, 1)
+    d_normed = jnp.zeros((512, 128), F32)
+    for head in range(4):
+        d_normed = d_normed + dot3(grads[head], head_weights(wq, wk, wv, wg, head, factor), NT)
+    dnorm_ref[...] = d_normed
+
+
+def tail_kernel(recv_ref, scaled_ref, send_ref, bias_ref):
     chunk = jnp.sum(recv_ref[:, 0:10, :], axis=0)
     rows = []
     for head in range(4):
@@ -242,8 +282,15 @@
             pieces = pieces + recv_ref[z * 4 + head, 10:14, :]
         rows.append(jnp.concatenate([pieces[a : a + 1] for a in range(4)], axis=1))
     bias_t = jnp.concatenate(rows + [jnp.zeros((4, 512), F32)], axis=0)
+    bias_ref[...] = bias_t
+    bias_w = dot3(bias_t, scaled_ref[...])
+    tail = jnp.concatenate([chunk, bias_w[0:4], jnp.zeros((2, 128), F32)], axis=0)
+    send_ref[...] = jnp.broadcast_to(tail[None], (8, 16, 128))
+
+
+def close_kernel(bias_ref, dnorm_ref, scaled_ref, inv_ref, gain_ref, wb_ref, grad_ref):
     scaled = scaled_ref[...]
-    wide = jnp.concatenate([bias_t, jnp.zeros((120, 512), F32)], axis=0)
+    wide = jnp.concatenate([bias_ref[...], jnp.zeros((120, 512), F32)], axis=0)
     wb = jnp.concatenate([wb_ref[...], jnp.zeros((124, 128), F32)], axis=0)
     d_normed = dnorm_ref[...] + dot3(jnp.transpose(wide), wb)
     d_scaled = d_normed * gain_ref[...]
@@ -251,9 +298,6 @@
     cross_term = jnp.mean(d_scaled * scaled, axis=1, keepdims=True)
     d_input = inv_ref[...] * (d_scaled - mean_term - scaled * cross_term)
     grad_ref[...] = jnp.swapaxes(d_input.reshape(32, 16, 128), 0, 1)
-    bias_w = dot3(bias_t, scaled)
-    tail = jnp.concatenate([chunk, bias_w[0:4], jnp.zeros((2, 128), F32)], axis=0)
-    send_ref[...] = jnp.broadcast_to(tail[None], (8, 16, 128))
 
 
 def share_kernel(recv_ref, send_ref):
@@ -307,13 +351,13 @@
     return pl.CostEstimate(flops=int(us * 1e9), bytes_accessed=int(us * 2e6), transcendentals=0)
 
 
-def call(kernel, out_shape, name, us, **extra):
+def call(kernel, out_shape, name, us, vmem=VMEM_BYTES, **extra):
     return pl.pallas_call(
         kernel,
         out_shape=out_shape,
         name=name,
         cost_estimate=cost(us),
-        compiler_params=pltpu.CompilerParams(vmem_limit_bytes=VMEM_BYTES),
+        compiler_params=pltpu.CompilerParams(vmem_limit_bytes=vmem),
         **extra,
     )
 
@@ -323,23 +367,14 @@
 
 
 def attend_call(place, keep, data, own, other):
-    columns = pl.BlockSpec((32, 16, 128), lambda j: (0, j, 0))
-    slots = pl.BlockSpec((8, 32, 512), lambda j: (0, 0, 0))
-    return pl.pallas_call(
+    smem, vmem = pl.BlockSpec(memory_space=pltpu.SMEM), pl.BlockSpec(memory_space=pltpu.VMEM)
+    return call(
         attend_kernel,
-        grid=(4,),
-        in_specs=[
-            pl.BlockSpec(memory_space=pltpu.SMEM),
-            pl.BlockSpec((4, 512), lambda j: (0, 0)),
-            columns,
-            slots,
-            slots,
-        ],
-        out_specs=[columns, slots, slots],
-        out_shape=[shaped(32, 64, 128), shaped(8, 32, 512), shaped(8, 32, 512)],
-        name="attend",
-        cost_estimate=cost(12),
-        compiler_params=pltpu.CompilerParams(vmem_limit_bytes=VMEM_BYTES),
+        [shaped(32, 64, 128), shaped(8, 32, 512), shaped(8, 32, 512)],
+        "attend",
+        12,
+        in_specs=[smem] + [vmem] * 4,
+        scratch_shapes=[pltpu.VMEM(shape, BF16) for shape in ((256, 768), (256, 256), (128, 256))],
     )(place, keep, data, own, other)
 
 
@@ -365,7 +400,7 @@
     place = jnp.stack([y, core, first]).astype(jnp.int32)
 
     piece, scaled, inverse = call(
-        norm_kernel, [shaped(8, 4, 4, 128), shaped(512, 128), shaped(512, 128)], "norm_bias", 1
+        norm_kernel, [shaped(8, 4, 4, 128), shaped(512, 128), shaped(512, 128)], "norm_bias", 1, MOST_VMEM
     )(pair_rep, gain, w_bias)
     vmem = pl.BlockSpec(memory_space=pltpu.VMEM)
     send, gate, d_gated, keep = call(
@@ -373,6 +408,7 @@
         [shaped(8, 4, 64, 128), shaped(512, 128), shaped(512, 128), jax.ShapeDtypeStruct((4, 512), jnp.int32)],
         "project",
         2,
+        MOST_VMEM,
         in_specs=[pl.BlockSpec(memory_space=pltpu.SMEM)] + [vmem] * 11,
     )(
         place, scaled, cotangent, gain, w_query, w_key, w_value, w_gate, gate_bias.reshape(1, 128), w_out,
@@ -395,21 +431,27 @@
     d_bias = d_bias[0] + sum(partner(d_bias[s], "y", flip) for s, flip in ((1, 4), (2, 2), (3, 6)))
     d_bias = jnp.transpose(d_bias.reshape(32, 32, 16), (1, 0, 2)).reshape(32, 4, 128)
 
-    update, d_normed, params, give = call(
-        lambda *refs: block_kernel(factor, *refs),
-        [shaped(16, 32, 128), shaped(512, 128), shaped(320, 128), shaped(320, 128)],
-        "block_grads",
+    got = got.reshape(8, 4, 64, 128)
+    params, give = call(
+        param_kernel,
+        [shaped(320, 128), shaped(320, 128)],
+        "param_grads",
         2,
-        in_specs=[pl.BlockSpec(memory_space=pltpu.SMEM)] + [vmem] * 10,
+        in_specs=[pl.BlockSpec(memory_space=pltpu.SMEM)] + [vmem] * 5,
         scratch_shapes=[pltpu.VMEM((640, 128), F32)],
-    )(place, got.reshape(8, 4, 64, 128), scaled, gate, d_gated, cotangent, w_query, w_key, w_value, w_gate, w_out)
+    )(place, got, scaled, gate, d_gated, cotangent)
+    update, d_normed = call(
+        lambda *refs: update_kernel(factor, *refs), [shaped(16, 32, 128), shaped(512, 128)], "update", 1.5
+    )(got, gate, d_gated, w_query, w_key, w_value, w_gate, w_out)
 
     params = params + partner(give, "core", 1)
     small = swap(jnp.concatenate([params.reshape(32, 10, 128), d_bias], axis=1), ROWS)
-    grad_pair, tail = call(close_kernel, [shaped(16, 32, 128), shaped(8, 16, 128)], "norm_back", 1)(
-        small, d_normed, scaled, inverse, gain, w_bias
+    tail, bias_t = call(tail_kernel, [shaped(8, 16, 128), shaped(8, 512)], "tail", 0.5)(small, scaled)
+    grad_pair = call(close_kernel, shaped(16, 32, 128), "norm_back", 1)(
+        bias_t, d_normed, scaled, inverse, gain, w_bias
     )
     tail = swap(tail, "y")
+    tail, update, grad_pair = lax.optimization_barrier((tail, update, grad_pair))
     tail = call(share_kernel, shaped(32, 16, 128), "share", 0.1)(tail)
     tail = swap(tail, ROWS)
     grads = call(

time: 181 us -> 174 us (0.961)
  blocking collectives: 44.2 us -> 34.3 us
  local copies, waits for them, and re-layouts: 6.7 us -> 1.69 us
  waiting for transfers between devices: 29.1 us -> 33.4 us
  starting transfers between devices: 75.1 us -> 79 us
    all_to_all x3 -> x2, blocking collectives: 44.2 us -> 34.3 us  [swap(): return lax.all_to_all(value, axes, 0, 0, tiled=False)]
    all_to_all x3 -> x4, waiting for transfers between devices: 4.81 us -> 9.93 us  [swap(): return lax.all_to_all(value, axes, 0, 0, tiled=False)]
    unnamed x52 -> x32, local copies, waits for them, and re-layouts: 5.13 us -> 0.76 us
    all_to_all x3 -> x4, starting transfers between devices: 28.3 us -> 30.6 us  [swap(): return lax.all_to_all(value, axes, 0, 0, tiled=False)]
    pallas_call x3 -> x5, Pallas kernels: 17 us -> 15.8 us  [the longest x1 10.6 us: attend_call(): call(attend_kernel, [shaped(32, 64, 128), shaped(8, 32, 512), shaped(8, 3...]
  transfers between devices with their start and end apart: 15 -> 16, of which waited for: 9 -> 11; matrix products, arithmetic and copies ran while one was open for 2% -> 1% of each run, Pallas kernels for 3% -> 4%
where the time goes in v4:
time: 174 us; the launch traced here: 173 us
  starting transfers between devices  79 us (45%)
  blocking collectives  34.3 us (20%)
  waiting for transfers between devices  33.4 us (19%)
  Pallas kernels  22.6 us (13%)
    ppermute x12, starting transfers between devices, partner(): lax.ppermute(value, axis, [(at, at ^ flip) for at in range(lax.axis_size(...  48.4 us
    all_to_all x2, blocking collectives, swap(): return lax.all_to_all(value, axes, 0, 0, tiled=False)  34.3 us
    all_to_all x4, starting transfers between devices, swap(): return lax.all_to_all(value, axes, 0, 0, tiled=False)  30.6 us
    ppermute x12, waiting for transfers between devices, partner(): lax.ppermute(value, axis, [(at, at ^ flip) for at in range(lax.axis_size(...  23.4 us
    pallas_call x1, Pallas kernels, attend_call(): call(attend_kernel, [shaped(32, 64, 128), shaped(8, 32, 512), shaped(8, 3...  10.6 us
    all_to_all x4, waiting for transfers between devices, swap(): return lax.all_to_all(value, axes, 0, 0, tiled=False)  9.93 us
  transfers between devices with their start and end apart: 16, of which 11 were waited for; matrix products, arithmetic and copies ran while one was open for 1% of the time, Pallas kernels for 4%

profile of v4, /device:TPU:1, one launch (start us, length us, event | category | flops | bytes accessed | tf_op | source)
XLA Modules:
  0.0 172.8 jit_solution(11488157457137781678)
XLA Ops:
  0.6 2.1 %norm_bias.1 = (f32[8,4,4,128]{3,2,1,0:T(4,128)}, f32[512,128]{1,0:T(8,128)}, f32[512,128]{1,0:T(8,128)}) custom-call(f32[16,32,128]{2,1,0:T(8,128)} %x_ref.1, f32[1,128]{1,0:T(1,128)} %bitcast.31, f32[4,128]{1,0:T(4,128)} %refs_8_.1), custom_call_target="tpu_custom_call" | custom-call | flops 1000000000 | bytes 2000000 | tf_op jit(solution)/shard_map/norm_bias/pallas_call | solution.py:402
  2.7 13.7 %all-to-all-start = ((f32[32,4,128]{2,1,0:T(4,128)}), f32[32,4,128]{2,1,0:T(4,128)S(1)}, u32[]{:S(2)}, u32[]{:S(2)}) async-start(f32[32,4,128]{2,1,0:T(4,128)} %bitcast.40), calls=%async_computation | async-start | bytes 131072 | tf_op jit(solution)/shard_map/all_to_all | solution.py:382
  16.4 0.6 pad_add_fusion.refs_0_.place_ref
  17.0 2.9 %project.1 = (f32[8,4,64,128]{3,2,1,0:T(8,128)}, f32[512,128]{1,0:T(8,128)}, f32[512,128]{1,0:T(8,128)}, s32[4,512]{1,0:T(4,128)}) custom-call(s32[3]{0:T(128)} %pad_add_fusion.refs_0_.place_ref, f32[512,128]{1,0:T(8,128)} %get-tuple-element.39.refs_1_.scaled_ref, f32[16,32,128]{2,1,0:T(8,128)} %cot_ref.1, f32[1,128]{1,0:T(1,128)} %bitcast.32, ...), custom_call_target="tpu_custom_call" | custom-call | flops 2000000000 | bytes 4000000 | tf_op jit(solution)/shard_map/project/pallas_call | solution.py:406
  20.0 5.3 %all-to-all-done = f32[32,4,128]{2,1,0:T(4,128)S(1)} async-done(((f32[32,4,128]{2,1,0:T(4,128)}), f32[32,4,128]{2,1,0:T(4,128)S(1)}, u32[]{:S(2)}, u32[]{:S(2)}) %all-to-all-start) | async-done | bytes 65568 | tf_op jit(solution)/shard_map/all_to_all | solution.py:382
  25.3 3.9 %all-to-all-start.1 = ((f32[32,64,128]{2,1,0:T(8,128)}), f32[32,64,128]{2,1,0:T(8,128)S(1)}, u32[]{:S(2)}, u32[]{:S(2)}) async-start(f32[32,64,128]{2,1,0:T(8,128)} %bitcast.39), calls=%async_computation.1 | async-start | bytes 2097152 | tf_op jit(solution)/shard_map/all_to_all | solution.py:382
  29.2 0.1 copy.33
  29.3 0.2 copy.34
  29.5 0.1 copy.39
  29.6 5.9 %collective-permute-start.2 = (f32[1,32,512]{2,1,0:T(8,128)S(1)}, f32[1,32,512]{2,1,0:T(8,128)S(1)}, u32[]{:S(2)}, u32[]{:S(2)}) collective-permute-start(f32[1,32,512]{2,1,0:T(8,128)S(1)} %copy.39), channel_id=1, source_target_pairs={{0,384},{64,448},{128,256},{192,320},{256,128},{320,192},{384,0},{... | collective-permute-start | bytes 196616 | tf_op jit(solution)/shard_map/ppermute | solution.py:386
  35.5 3.8 %collective-permute-start.1 = (f32[1,32,512]{2,1,0:T(8,128)S(1)}, f32[1,32,512]{2,1,0:T(8,128)S(1)}, u32[]{:S(2)}, u32[]{:S(2)}) collective-permute-start(f32[1,32,512]{2,1,0:T(8,128)S(1)} %copy.39), channel_id=1, source_target_pairs={{0,128},{64,192},{128,0},{192,64},{256,384},{320,448},{384,256},{4... | collective-permute-start | bytes 196616 | tf_op jit(solution)/shard_map/ppermute | solution.py:386
  39.3 2.1 %collective-permute-start = (f32[1,32,512]{2,1,0:T(8,128)S(1)}, f32[1,32,512]{2,1,0:T(8,128)S(1)}, u32[]{:S(2)}, u32[]{:S(2)}) collective-permute-start(f32[1,32,512]{2,1,0:T(8,128)S(1)} %copy.39), channel_id=1, source_target_pairs={{0,256},{64,320},{128,384},{192,448},{256,0},{320,64},{384,128},{4... | collective-permute-start | bytes 196616 | tf_op jit(solution)/shard_map/ppermute | solution.py:386
  41.5 0.3 collective-permute-done.1
  41.8 6.4 %collective-permute-done = f32[1,32,512]{2,1,0:T(8,128)S(1)} collective-permute-done((f32[1,32,512]{2,1,0:T(8,128)S(1)}, f32[1,32,512]{2,1,0:T(8,128)S(1)}, u32[]{:S(2)}, u32[]{:S(2)}) %collective-permute-start) | collective-permute-done | bytes 65568 | tf_op jit(solution)/shard_map/ppermute | solution.py:386
  48.2 2.7 %collective-permute-start.3 = (f32[4,32,512]{2,1,0:T(8,128)S(1)}, f32[4,32,512]{2,1,0:T(8,128)S(1)}, u32[]{:S(2)}, u32[]{:S(2)}) collective-permute-start(f32[4,32,512]{2,1,0:T(8,128)S(1)} %pad_maximum_fusion), channel_id=1, source_target_pairs={{0,64},{64,0},{128,192},{192,128},{256,320},{320,256},{384,448},{4... | collective-permute-start | bytes 786440 | tf_op jit(solution)/shard_map/ppermute | solution.py:386
  51.0 4.6 %collective-permute-done.3 = f32[4,32,512]{2,1,0:T(8,128)S(1)} collective-permute-done((f32[4,32,512]{2,1,0:T(8,128)S(1)}, f32[4,32,512]{2,1,0:T(8,128)S(1)}, u32[]{:S(2)}, u32[]{:S(2)}) %collective-permute-start.3) | collective-permute-done | bytes 262176 | tf_op jit(solution)/shard_map/ppermute | solution.py:386
  55.7 0.0 copy-start
  55.7 7.2 %collective-permute-start.4 = (f32[8,32,512]{2,1,0:T(8,128)S(1)}, f32[8,32,512]{2,1,0:T(8,128)S(1)}, u32[]{:S(2)}, u32[]{:S(2)}) collective-permute-start(f32[8,32,512]{2,1,0:T(8,128)S(1)} %constant_dynamic-update-slice_fusion.own_ref), channel_id=1, source_target_pairs={{0,32},{32,0},{1,33},{33,1},{2,34},{34,2},{3,35},{35,3},{4,36},{36... | collective-permute-start | bytes 1572872 | tf_op jit(solution)/shard_map/ppermute | solution.py:386
  62.9 1.5 collective-permute-done.4.other_ref
  64.5 10.6 %attend.1 = (f32[32,64,128]{2,1,0:T(8,128)}, f32[8,32,512]{2,1,0:T(8,128)S(1)}, f32[8,32,512]{2,1,0:T(8,128)S(1)}) custom-call(s32[3]{0:T(128)S(1)} %copy-done, s32[4,512]{1,0:T(4,128)S(1)} %copy-done.13, f32[32,64,128]{2,1,0:T(8,128)S(1)} %all-to-all-done.1.data_ref, f32[8,32,512]{2,1,0:T(8,128)S(1)} %constant_dynamic-update-slice_fusion.own_ref, ...), custom_call_target="tpu_custom_call" | custom-call | flops 12000000000 | bytes 24000000 | tf_op jit(solution)/shard_map/attend/pallas_call | solution.py:371
  75.1 9.5 %all-to-all-start.2 = ((f32[32,64,128]{2,1,0:T(8,128)}), f32[32,64,128]{2,1,0:T(8,128)S(1)}, u32[]{:S(2)}, u32[]{:S(2)}) async-start(f32[32,64,128]{2,1,0:T(8,128)} %get-tuple-element.45), calls=%async_computation.2 | async-start | bytes 2097152 | tf_op jit(solution)/shard_map/all_to_all | solution.py:382
  84.6 2.6 %collective-permute-start.6 = (f32[8,32,512]{2,1,0:T(8,128)S(1)}, f32[8,32,512]{2,1,0:T(8,128)S(1)}, u32[]{:S(2)}, u32[]{:S(2)}) collective-permute-start(f32[8,32,512]{2,1,0:T(8,128)S(1)} %get-tuple-element.51), channel_id=1, source_target_pairs={{0,32},{32,0},{1,33},{33,1},{2,34},{34,2},{3,35},{35,3},{4,36},{36... | collective-permute-start | bytes 1572872 | tf_op jit(solution)/shard_map/ppermute | solution.py:386
  87.1 1.5 collective-permute-done.6
  88.6 0.1 add.27
  88.8 2.0 %collective-permute-start.7 = (f32[4,32,512]{2,1,0:T(8,128)S(1)}, f32[4,32,512]{2,1,0:T(8,128)S(1)}, u32[]{:S(2)}, u32[]{:S(2)}) collective-permute-start(f32[4,32,512]{2,1,0:T(8,128)S(1)} %slice.25), channel_id=1, source_target_pairs={{0,64},{64,0},{128,192},{192,128},{256,320},{320,256},{384,448},{4... | collective-permute-start | bytes 786440 | tf_op jit(solution)/shard_map/ppermute | solution.py:386
  90.7 7.4 %collective-permute-done.7 = f32[4,32,512]{2,1,0:T(8,128)S(1)} collective-permute-done((f32[4,32,512]{2,1,0:T(8,128)S(1)}, f32[4,32,512]{2,1,0:T(8,128)S(1)}, u32[]{:S(2)}, u32[]{:S(2)}) %collective-permute-start.7) | collective-permute-done | bytes 262176 | tf_op jit(solution)/shard_map/ppermute | solution.py:386
  98.2 0.0 copy-start.1
  98.3 2.1 %collective-permute-start.9 = (f32[32,512]{1,0:T(8,128)S(1)}, f32[32,512]{1,0:T(8,128)S(1)}, u32[]{:S(2)}, u32[]{:S(2)}) collective-permute-start(f32[32,512]{1,0:T(8,128)S(1)} %get-tuple-element.68), channel_id=1, source_target_pairs={{0,128},{64,192},{128,0},{192,64},{256,384},{320,448},{384,256},{4... | collective-permute-start | bytes 196616 | tf_op jit(solution)/shard_map/ppermute | solution.py:386
  100.3 2.2 %collective-permute-start.10 = (f32[32,512]{1,0:T(8,128)S(1)}, f32[32,512]{1,0:T(8,128)S(1)}, u32[]{:S(2)}, u32[]{:S(2)}) collective-permute-start(f32[32,512]{1,0:T(8,128)S(1)} %get-tuple-element.69), channel_id=1, source_target_pairs={{0,384},{64,448},{128,256},{192,320},{256,128},{320,192},{384,0},{... | collective-permute-start | bytes 196616 | tf_op jit(solution)/shard_map/ppermute | solution.py:386
  102.5 7.5 %collective-permute-start.8 = (f32[32,512]{1,0:T(8,128)S(1)}, f32[32,512]{1,0:T(8,128)S(1)}, u32[]{:S(2)}, u32[]{:S(2)}) collective-permute-start(f32[32,512]{1,0:T(8,128)S(1)} %get-tuple-element.70), channel_id=1, source_target_pairs={{0,256},{64,320},{128,384},{192,448},{256,0},{320,64},{384,128},{4... | collective-permute-start | bytes 196616 | tf_op jit(solution)/shard_map/ppermute | solution.py:386
  110.0 0.9 all-to-all-done.2
  110.9 1.7 param_grads.1
  112.6 4.6 %collective-permute-start.5 = (f32[320,128]{1,0:T(8,128)S(1)}, f32[320,128]{1,0:T(8,128)S(1)}, u32[]{:S(2)}, u32[]{:S(2)}) collective-permute-start(f32[320,128]{1,0:T(8,128)S(1)} %get-tuple-element.49), channel_id=1, source_target_pairs={{0,32},{32,0},{1,33},{33,1},{2,34},{34,2},{3,35},{35,3},{4,36},{36... | collective-permute-start | bytes 491528 | tf_op jit(solution)/shard_map/ppermute | solution.py:386
  117.3 0.1 copy.40
  117.4 0.2 copy.41
  117.6 0.1 copy.42
  117.7 0.5 collective-permute-done.5
  118.3 19.4 %all_to_all.30.recv_ref = f32[32,14,128]{2,1,0:T(8,128)S(1)} all-to-all(f32[32,14,128]{2,1,0:T(8,128)S(1)} %pad_maximum_fusion.1), channel_id=1, replica_groups=mesh['y'=8,'core'=2,'z'=8,'x'=4] {'z','x'}, dimensions={0} | all-to-all | bytes 458752 | tf_op jit(solution)/shard_map/all_to_all | solution.py:382
  137.7 0.8 tail.1
  138.5 3.5 %all-to-all-start.4 = ((f32[8,16,128]{2,1,0:T(8,128)}), f32[8,16,128]{2,1,0:T(8,128)S(1)}, u32[]{:S(2)}, u32[]{:S(2)}) async-start(f32[8,16,128]{2,1,0:T(8,128)} %get-tuple-element.52), calls=%async_computation.4 | async-start | bytes 131072 | tf_op jit(solution)/shard_map/all_to_all | solution.py:382
  142.1 1.4 update.1
  143.5 0.7 copy-done.7
  144.2 1.2 norm_back.1
  145.4 3.7 %all-to-all-done.4.recv_ref = f32[8,16,128]{2,1,0:T(8,128)S(1)} async-done(((f32[8,16,128]{2,1,0:T(8,128)}), f32[8,16,128]{2,1,0:T(8,128)S(1)}, u32[]{:S(2)}, u32[]{:S(2)}) %all-to-all-start.4) | async-done | bytes 65568 | tf_op jit(solution)/shard_map/all_to_all | solution.py:382
  149.2 14.9 %all_to_all.31.refs_1_ = f32[32,16,128]{2,1,0:T(8,128)S(1)} all-to-all(f32[32,16,128]{2,1,0:T(8,128)S(1)} %share.1), channel_id=1, replica_groups=mesh['y'=8,'core'=2,'z'=8,'x'=4] {'z','x'}, dimensions={0} | all-to-all | bytes 524288 | tf_op jit(solution)/shard_map/all_to_all | solution.py:382
  164.1 5.8 %collective-permute-start.11 = (f32[32,16,128]{2,1,0:T(8,128)S(1)}, f32[32,16,128]{2,1,0:T(8,128)S(1)}, u32[]{:S(2)}, u32[]{:S(2)}) collective-permute-start(f32[32,16,128]{2,1,0:T(8,128)S(1)} %all_to_all.31.refs_1_), channel_id=1, source_target_pairs={{0,32},{32,0},{1,33},{33,1},{2,34},{34,2},{3,35},{35,3},{4,36},{36... | collective-permute-start | bytes 786440 | tf_op jit(solution)/shard_map/ppermute | solution.py:386
  169.8 1.1 collective-permute-done.11.refs_2_
  171.0 1.8 %finish.1 = (f32[128,128]{1,0:T(8,128)}, f32[128,128]{1,0:T(8,128)}, f32[128,128]{1,0:T(8,128)}, f32[128,128]{1,0:T(8,128)}, f32[1,128]{1,0:T(1,128)}, /*index=5...) custom-call(s32[3]{0:T(128)S(1)} %copy-done, f32[32,16,128]{2,1,0:T(8,128)S(1)} %all_to_all.31.refs_1_, ...), custom_call_target="tpu_custom_call" | custom-call | flops 1000000000 | bytes 2000000 | tf_op jit(solution)/shard_map/finish/pallas_call | solution.py:457
  (44 shorter events, 0.3 us)
Async XLA Ops:
  2.7 22.5 %all-to-all-start = ((f32[32,4,128]{2,1,0:T(4,128)}), f32[32,4,128]{2,1,0:T(4,128)S(1)}, u32[]{:S(2)}, u32[]{:S(2)}) async-start(f32[32,4,128]{2,1,0:T(4,128)} %bitcast.40), calls=%async_computation | async-start | bytes 131072 | tf_op jit(solution)/shard_map/all_to_all | solution.py:382
  25.3 39.2 %all-to-all-start.1 = ((f32[32,64,128]{2,1,0:T(8,128)}), f32[32,64,128]{2,1,0:T(8,128)S(1)}, u32[]{:S(2)}, u32[]{:S(2)}) async-start(f32[32,64,128]{2,1,0:T(8,128)} %bitcast.39), calls=%async_computation.1 | async-start | bytes 2097152 | tf_op jit(solution)/shard_map/all_to_all | solution.py:382
  29.6 11.8 %collective-permute-start.2 = (f32[1,32,512]{2,1,0:T(8,128)S(1)}, f32[1,32,512]{2,1,0:T(8,128)S(1)}, u32[]{:S(2)}, u32[]{:S(2)}) collective-permute-start(f32[1,32,512]{2,1,0:T(8,128)S(1)} %copy.39), channel_id=1, source_target_pairs={{0,384},{64,448},{128,256},{192,320},{256,128},{320,192},{384,0},{... | collective-permute-start | bytes 196616 | tf_op jit(solution)/shard_map/ppermute | solution.py:386
  35.5 6.3 %collective-permute-start.1 = (f32[1,32,512]{2,1,0:T(8,128)S(1)}, f32[1,32,512]{2,1,0:T(8,128)S(1)}, u32[]{:S(2)}, u32[]{:S(2)}) collective-permute-start(f32[1,32,512]{2,1,0:T(8,128)S(1)} %copy.39), channel_id=1, source_target_pairs={{0,128},{64,192},{128,0},{192,64},{256,384},{320,448},{384,256},{4... | collective-permute-start | bytes 196616 | tf_op jit(solution)/shard_map/ppermute | solution.py:386
  39.3 8.9 %collective-permute-start = (f32[1,32,512]{2,1,0:T(8,128)S(1)}, f32[1,32,512]{2,1,0:T(8,128)S(1)}, u32[]{:S(2)}, u32[]{:S(2)}) collective-permute-start(f32[1,32,512]{2,1,0:T(8,128)S(1)} %copy.39), channel_id=1, source_target_pairs={{0,256},{64,320},{128,384},{192,448},{256,0},{320,64},{384,128},{4... | collective-permute-start | bytes 196616 | tf_op jit(solution)/shard_map/ppermute | solution.py:386
  48.2 7.4 %collective-permute-start.3 = (f32[4,32,512]{2,1,0:T(8,128)S(1)}, f32[4,32,512]{2,1,0:T(8,128)S(1)}, u32[]{:S(2)}, u32[]{:S(2)}) collective-permute-start(f32[4,32,512]{2,1,0:T(8,128)S(1)} %pad_maximum_fusion), channel_id=1, source_target_pairs={{0,64},{64,0},{128,192},{192,128},{256,320},{320,256},{384,448},{4... | collective-permute-start | bytes 786440 | tf_op jit(solution)/shard_map/ppermute | solution.py:386
  51.0 13.4 %copy-start.13 = (s32[4,512]{1,0:T(4,128)S(1)}, s32[4,512]{1,0:T(4,128)}, u32[]{:S(2)}) copy-start(s32[4,512]{1,0:T(4,128)} %get-tuple-element.40.keep_ref) | copy-start | bytes 24580
  55.7 8.8 %copy-start = (s32[3]{0:T(128)S(1)}, s32[3]{0:T(128)}, u32[]{:S(2)}) copy-start(s32[3]{0:T(128)} %pad_add_fusion.refs_0_.place_ref) | copy-start | bytes 40
  55.7 8.8 %collective-permute-start.4 = (f32[8,32,512]{2,1,0:T(8,128)S(1)}, f32[8,32,512]{2,1,0:T(8,128)S(1)}, u32[]{:S(2)}, u32[]{:S(2)}) collective-permute-start(f32[8,32,512]{2,1,0:T(8,128)S(1)} %constant_dynamic-update-slice_fusion.own_ref), channel_id=1, source_target_pairs={{0,32},{32,0},{1,33},{33,1},{2,34},{34,2},{3,35},{35,3},{4,36},{36... | collective-permute-start | bytes 1572872 | tf_op jit(solution)/shard_map/ppermute | solution.py:386
  75.1 35.8 %all-to-all-start.2 = ((f32[32,64,128]{2,1,0:T(8,128)}), f32[32,64,128]{2,1,0:T(8,128)S(1)}, u32[]{:S(2)}, u32[]{:S(2)}) async-start(f32[32,64,128]{2,1,0:T(8,128)} %get-tuple-element.45), calls=%async_computation.2 | async-start | bytes 2097152 | tf_op jit(solution)/shard_map/all_to_all | solution.py:382
  84.6 4.1 %collective-permute-start.6 = (f32[8,32,512]{2,1,0:T(8,128)S(1)}, f32[8,32,512]{2,1,0:T(8,128)S(1)}, u32[]{:S(2)}, u32[]{:S(2)}) collective-permute-start(f32[8,32,512]{2,1,0:T(8,128)S(1)} %get-tuple-element.51), channel_id=1, source_target_pairs={{0,32},{32,0},{1,33},{33,1},{2,34},{34,2},{3,35},{35,3},{4,36},{36... | collective-permute-start | bytes 1572872 | tf_op jit(solution)/shard_map/ppermute | solution.py:386
  88.8 9.4 %collective-permute-start.7 = (f32[4,32,512]{2,1,0:T(8,128)S(1)}, f32[4,32,512]{2,1,0:T(8,128)S(1)}, u32[]{:S(2)}, u32[]{:S(2)}) collective-permute-start(f32[4,32,512]{2,1,0:T(8,128)S(1)} %slice.25), channel_id=1, source_target_pairs={{0,64},{64,0},{128,192},{192,128},{256,320},{320,256},{384,448},{4... | collective-permute-start | bytes 786440 | tf_op jit(solution)/shard_map/ppermute | solution.py:386
  98.2 12.7 %copy-start.9 = (f32[512,128]{1,0:T(8,128)S(1)}, f32[512,128]{1,0:T(8,128)}, u32[]{:S(2)}) copy-start(f32[512,128]{1,0:T(8,128)} %get-tuple-element.39.refs_1_.scaled_ref) | copy-start | bytes 786436
  98.2 12.7 %copy-start.11 = (f32[512,128]{1,0:T(8,128)S(1)}, f32[512,128]{1,0:T(8,128)}, u32[]{:S(2)}) copy-start(f32[512,128]{1,0:T(8,128)} %get-tuple-element.46.gate_ref.refs_1_) | copy-start | bytes 786436
  98.2 12.7 %copy-start.12 = (f32[512,128]{1,0:T(8,128)S(1)}, f32[512,128]{1,0:T(8,128)}, u32[]{:S(2)}) copy-start(f32[512,128]{1,0:T(8,128)} %get-tuple-element.47.dgated_ref.refs_2_) | copy-start | bytes 786436
  98.2 12.7 %copy-start.1 = (f32[16,32,128]{2,1,0:T(8,128)S(1)}, f32[16,32,128]{2,1,0:T(8,128)}, u32[]{:S(2)}) copy-start(f32[16,32,128]{2,1,0:T(8,128)} %cot_ref.1) | copy-start | bytes 786436
  98.3 19.0 %collective-permute-start.9 = (f32[32,512]{1,0:T(8,128)S(1)}, f32[32,512]{1,0:T(8,128)S(1)}, u32[]{:S(2)}, u32[]{:S(2)}) collective-permute-start(f32[32,512]{1,0:T(8,128)S(1)} %get-tuple-element.68), channel_id=1, source_target_pairs={{0,128},{64,192},{128,0},{192,64},{256,384},{320,448},{384,256},{4... | collective-permute-start | bytes 196616 | tf_op jit(solution)/shard_map/ppermute | solution.py:386
  100.3 16.9 %collective-permute-start.10 = (f32[32,512]{1,0:T(8,128)S(1)}, f32[32,512]{1,0:T(8,128)S(1)}, u32[]{:S(2)}, u32[]{:S(2)}) collective-permute-start(f32[32,512]{1,0:T(8,128)S(1)} %get-tuple-element.69), channel_id=1, source_target_pairs={{0,384},{64,448},{128,256},{192,320},{256,128},{320,192},{384,0},{... | collective-permute-start | bytes 196616 | tf_op jit(solution)/shard_map/ppermute | solution.py:386
  102.5 14.7 %collective-permute-start.8 = (f32[32,512]{1,0:T(8,128)S(1)}, f32[32,512]{1,0:T(8,128)S(1)}, u32[]{:S(2)}, u32[]{:S(2)}) collective-permute-start(f32[32,512]{1,0:T(8,128)S(1)} %get-tuple-element.70), channel_id=1, source_target_pairs={{0,256},{64,320},{128,384},{192,448},{256,0},{320,64},{384,128},{4... | collective-permute-start | bytes 196616 | tf_op jit(solution)/shard_map/ppermute | solution.py:386
  112.6 5.6 %collective-permute-start.5 = (f32[320,128]{1,0:T(8,128)S(1)}, f32[320,128]{1,0:T(8,128)S(1)}, u32[]{:S(2)}, u32[]{:S(2)}) collective-permute-start(f32[320,128]{1,0:T(8,128)S(1)} %get-tuple-element.49), channel_id=1, source_target_pairs={{0,32},{32,0},{1,33},{33,1},{2,34},{34,2},{3,35},{35,3},{4,36},{36... | collective-permute-start | bytes 491528 | tf_op jit(solution)/shard_map/ppermute | solution.py:386
  137.7 4.3 %copy-start.4 = (f32[128,128]{1,0:T(8,128)S(1)}, f32[128,128]{1,0:T(8,128)}, u32[]{:S(2)}) copy-start(f32[128,128]{1,0:T(8,128)} %refs_5_.5) | copy-start | bytes 196612
  137.7 4.3 %copy-start.5 = (f32[128,128]{1,0:T(8,128)S(1)}, f32[128,128]{1,0:T(8,128)}, u32[]{:S(2)}) copy-start(f32[128,128]{1,0:T(8,128)} %refs_6_.5) | copy-start | bytes 196612
  137.7 4.3 %copy-start.6 = (f32[128,128]{1,0:T(8,128)S(1)}, f32[128,128]{1,0:T(8,128)}, u32[]{:S(2)}) copy-start(f32[128,128]{1,0:T(8,128)} %refs_7_.5) | copy-start | bytes 196612
  138.5 3.5 %copy-start.2 = (f32[128,128]{1,0:T(8,128)S(1)}, f32[128,128]{1,0:T(8,128)}, u32[]{:S(2)}) copy-start(f32[128,128]{1,0:T(8,128)} %refs_7_.4) | copy-start | bytes 196612
  138.5 3.5 %copy-start.3 = (f32[128,128]{1,0:T(8,128)S(1)}, f32[128,128]{1,0:T(8,128)}, u32[]{:S(2)}) copy-start(f32[128,128]{1,0:T(8,128)} %refs_4_.5) | copy-start | bytes 196612
  138.5 10.6 %all-to-all-start.4 = ((f32[8,16,128]{2,1,0:T(8,128)}), f32[8,16,128]{2,1,0:T(8,128)S(1)}, u32[]{:S(2)}, u32[]{:S(2)}) async-start(f32[8,16,128]{2,1,0:T(8,128)} %get-tuple-element.52), calls=%async_computation.4 | async-start | bytes 131072 | tf_op jit(solution)/shard_map/all_to_all | solution.py:382
  142.1 1.5 copy-start.10
  143.5 0.7 copy-start.7
  143.5 0.7 copy-start.8
  164.1 6.9 %collective-permute-start.11 = (f32[32,16,128]{2,1,0:T(8,128)S(1)}, f32[32,16,128]{2,1,0:T(8,128)S(1)}, u32[]{:S(2)}, u32[]{:S(2)}) collective-permute-start(f32[32,16,128]{2,1,0:T(8,128)S(1)} %all_to_all.31.refs_1_), channel_id=1, source_target_pairs={{0,32},{32,0},{1,33},{33,1},{2,34},{34,2},{3,35},{35,3},{4,36},{36... | collective-permute-start | bytes 786440 | tf_op jit(solution)/shard_map/ppermute | solution.py:386

commit v5 on v4

--- a/solution.py
+++ b/solution.py
@@ -136,7 +136,8 @@
 
 
 def attend_kernel(
-    place_ref, keep_ref, data_ref, own_ref, other_ref, out_ref, d_own_ref, d_other_ref,
+    place_ref, keep_ref, data_ref, own_low_ref, own_high_ref, other_low_ref, other_high_ref,
+    out_ref, d_own_ref, d_other_ref,
     keys_ref, rows_ref, turns_ref,
 ):
     y, core = place_ref[0], place_ref[1]
@@ -145,11 +146,12 @@
     per = chunk_rows // 32
     sub = lanes_of((chunk_rows, 128))
     chunks = []
-    for side, (bias_ref, db_ref) in enumerate(((own_ref, d_own_ref), (other_ref, d_other_ref))):
+    sides = (((own_low_ref, own_high_ref), d_own_ref), ((other_low_ref, other_high_ref), d_other_ref))
+    for side, (bias_refs, db_ref) in enumerate(sides):
         half = core if side == 0 else 1 - core
         for s0 in range(0, 8, per):
             starts = [(y ^ ((s >> 2) | (s & 2) | ((s & 1) << 2))) * 4 + half * 2 for s in range(s0, s0 + per)]
-            chunks.append((starts, bias_ref, db_ref, s0))
+            chunks.append((starts, bias_refs, db_ref, s0))
 
     def column_keys(column):
         here = pl.ds(column * 16, 16)
@@ -158,13 +160,14 @@
 
     def first(column, keys, chunk):
         k_right, v_right, k_both, k_first, v_both, v_first, keep = keys
-        starts, bias_ref, db_ref, s0 = chunk
+        starts, bias_refs, db_ref, s0 = chunk
         here = pl.ds(column * 16, 16)
         rows = jnp.concatenate([data_ref[pl.ds(start, 2), here].reshape(32, 128) for start in starts], axis=0)
         both = halves_of(rows)
         q_left = bdot(both, rows_ref[:, 0:128]).astype(BF16)
         q_t = bdot(turns_ref[0:64], both, NT).astype(BF16)
-        scores = bdot(q_left, k_right, NT) + bias_ref[s0 : s0 + per].reshape(chunk_rows, 512)
+        bias = jnp.concatenate([ref[...].reshape(128, 512) for ref in bias_refs], axis=0)
+        scores = bdot(q_left, k_right, NT) + bias
         return rows, q_t, jnp.where(keep, scores, NEG_FILL)
 
     def second(keys, state):
@@ -188,7 +191,7 @@
 
     def third(column, keys, chunk, state):
         k_right, v_right, k_both, k_first, v_both, v_first, keep = keys
-        starts, bias_ref, db_ref, s0 = chunk
+        starts, bias_refs, db_ref, s0 = chunk
         weights, output, d_weights, centred, dv_t, q_t = state
         d_scores = weights * (d_weights - centred)
         if column == 0:
@@ -366,16 +369,16 @@
     return jax.ShapeDtypeStruct(shape, F32)
 
 
-def attend_call(place, keep, data, own, other):
+def attend_call(place, keep, data, *bias):
     smem, vmem = pl.BlockSpec(memory_space=pltpu.SMEM), pl.BlockSpec(memory_space=pltpu.VMEM)
     return call(
         attend_kernel,
         [shaped(32, 64, 128), shaped(8, 32, 512), shaped(8, 32, 512)],
         "attend",
         12,
-        in_specs=[smem] + [vmem] * 4,
+        in_specs=[smem] + [vmem] * 6,
         scratch_shapes=[pltpu.VMEM(shape, BF16) for shape in ((256, 768), (256, 256), (128, 256))],
-    )(place, keep, data, own, other)
+    )(place, keep, data, *bias)
 
 
 def swap(value, axes):
@@ -419,11 +422,13 @@
     piece, send = lax.optimization_barrier((piece, send))
     data = swap(send.reshape(32, 64, 128), ROWS)
     own = jnp.transpose(piece.reshape(32, 32, 16), (1, 0, 2)).reshape(1, 32, 512)
-    own = jnp.concatenate([own] + [partner(own, "y", flip) for flip in (4, 2, 6)], axis=0)
-    own = jnp.concatenate([own, partner(own, "y", 1)], axis=0)
-    other = partner(own, "core", 1)
-
-    back, d_own, d_other = attend_call(place, keep, data, own, other)
+    near = jnp.concatenate([own, partner(own, "y", 4)], axis=0)
+    far = jnp.concatenate([partner(own, "y", 2), partner(own, "y", 6)], axis=0)
+    low = jnp.concatenate([near, far], axis=0)
+    high = jnp.concatenate([partner(near, "y", 1), partner(far, "y", 1)], axis=0)
+    bias = [low, high, partner(low, "core", 1), partner(high, "core", 1)]
+
+    back, d_own, d_other = attend_call(place, keep, data, *bias)
 
     got = swap(back, ROWS)
     d_bias = d_own + partner(d_other, "core", 1)

time: 174 us -> 171 us (0.983)
  waiting for transfers between devices: 33.4 us -> 21.1 us
  starting transfers between devices: 79 us -> 89 us
    ppermute x12 -> x14, waiting for transfers between devices: 23.4 us -> 11.6 us  [partner(): lax.ppermute(value, axis, [(at, at ^ flip) for at in range(lax.axis_size(...]
    ppermute x12 -> x14, starting transfers between devices: 48.4 us -> 55.5 us  [partner(): lax.ppermute(value, axis, [(at, at ^ flip) for at in range(lax.axis_size(...]
    all_to_all x4, starting transfers between devices: 30.6 us -> 33.5 us  [swap(): return lax.all_to_all(value, axes, 0, 0, tiled=False)]
  transfers between devices with their start and end apart: 16 -> 18, of which waited for: 11 -> 10; matrix products, arithmetic and copies ran while one was open for 1% -> 1% of each run, Pallas kernels for 4% -> 4%
where the time goes in v5:
time: 171 us; the launch traced here: 170 us
  starting transfers between devices  89 us (52%)
  blocking collectives  33.5 us (20%)
  Pallas kernels  22.6 us (13%)
  waiting for transfers between devices  21.1 us (12%)
    ppermute x14, starting transfers between devices, partner(): lax.ppermute(value, axis, [(at, at ^ flip) for at in range(lax.axis_size(...  55.5 us
    all_to_all x4, starting transfers between devices, swap(): return lax.all_to_all(value, axes, 0, 0, tiled=False)  33.5 us
    all_to_all x2, blocking collectives, swap(): return lax.all_to_all(value, axes, 0, 0, tiled=False)  33.5 us
    ppermute x14, waiting for transfers between devices, partner(): lax.ppermute(value, axis, [(at, at ^ flip) for at in range(lax.axis_size(...  11.6 us
    pallas_call x1, Pallas kernels, attend_call(): call(attend_kernel, [shaped(32, 64, 128), shaped(8, 32, 512), shaped(8, 3...  10.6 us
    all_to_all x4, waiting for transfers between devices, swap(): return lax.all_to_all(value, axes, 0, 0, tiled=False)  9.44 us
  transfers between devices with their start and end apart: 18, of which 10 were waited for; matrix products, arithmetic and copies ran while one was open for 1% of the time, Pallas kernels for 4%

profile of v5, /device:TPU:1, one launch (start us, length us, event | category | flops | bytes accessed | tf_op | source)
XLA Modules:
  0.0 169.8 jit_solution(4805153211206901845)
XLA Ops:
  0.6 2.1 %norm_bias.1 = (f32[8,4,4,128]{3,2,1,0:T(4,128)}, f32[512,128]{1,0:T(8,128)}, f32[512,128]{1,0:T(8,128)}) custom-call(f32[16,32,128]{2,1,0:T(8,128)} %x_ref.1, f32[1,128]{1,0:T(1,128)} %bitcast.31, f32[4,128]{1,0:T(4,128)} %refs_8_.1), custom_call_target="tpu_custom_call" | custom-call | flops 1000000000 | bytes 2000000 | tf_op jit(solution)/shard_map/norm_bias/pallas_call | solution.py:405
  2.7 13.7 %all-to-all-start = ((f32[32,4,128]{2,1,0:T(4,128)}), f32[32,4,128]{2,1,0:T(4,128)S(1)}, u32[]{:S(2)}, u32[]{:S(2)}) async-start(f32[32,4,128]{2,1,0:T(4,128)} %bitcast.40), calls=%async_computation | async-start | bytes 131072 | tf_op jit(solution)/shard_map/all_to_all | solution.py:385
  16.4 0.6 pad_add_fusion.refs_0_.place_ref
  17.0 2.9 %project.1 = (f32[8,4,64,128]{3,2,1,0:T(8,128)}, f32[512,128]{1,0:T(8,128)}, f32[512,128]{1,0:T(8,128)}, s32[4,512]{1,0:T(4,128)}) custom-call(s32[3]{0:T(128)} %pad_add_fusion.refs_0_.place_ref, f32[512,128]{1,0:T(8,128)} %get-tuple-element.39.refs_1_.scaled_ref, f32[16,32,128]{2,1,0:T(8,128)} %cot_ref.1, f32[1,128]{1,0:T(1,128)} %bitcast.32, ...), custom_call_target="tpu_custom_call" | custom-call | flops 2000000000 | bytes 4000000 | tf_op jit(solution)/shard_map/project/pallas_call | solution.py:409
  20.0 5.3 %all-to-all-done = f32[32,4,128]{2,1,0:T(4,128)S(1)} async-done(((f32[32,4,128]{2,1,0:T(4,128)}), f32[32,4,128]{2,1,0:T(4,128)S(1)}, u32[]{:S(2)}, u32[]{:S(2)}) %all-to-all-start) | async-done | bytes 65568 | tf_op jit(solution)/shard_map/all_to_all | solution.py:385
  25.3 3.9 %all-to-all-start.1 = ((f32[32,64,128]{2,1,0:T(8,128)}), f32[32,64,128]{2,1,0:T(8,128)S(1)}, u32[]{:S(2)}, u32[]{:S(2)}) async-start(f32[32,64,128]{2,1,0:T(8,128)} %bitcast.39), calls=%async_computation.1 | async-start | bytes 2097152 | tf_op jit(solution)/shard_map/all_to_all | solution.py:385
  29.2 0.1 copy.33
  29.3 0.2 copy.34
  29.5 0.1 copy.38
  29.6 7.5 %collective-permute-start = (f32[1,32,512]{2,1,0:T(8,128)S(1)}, f32[1,32,512]{2,1,0:T(8,128)S(1)}, u32[]{:S(2)}, u32[]{:S(2)}) collective-permute-start(f32[1,32,512]{2,1,0:T(8,128)S(1)} %copy.38), channel_id=1, source_target_pairs={{0,256},{64,320},{128,384},{192,448},{256,0},{320,64},{384,128},{4... | collective-permute-start | bytes 196616 | tf_op jit(solution)/shard_map/ppermute | solution.py:389
  37.1 2.0 %collective-permute-start.2 = (f32[1,32,512]{2,1,0:T(8,128)S(1)}, f32[1,32,512]{2,1,0:T(8,128)S(1)}, u32[]{:S(2)}, u32[]{:S(2)}) collective-permute-start(f32[1,32,512]{2,1,0:T(8,128)S(1)} %copy.38), channel_id=1, source_target_pairs={{0,384},{64,448},{128,256},{192,320},{256,128},{320,192},{384,0},{... | collective-permute-start | bytes 196616 | tf_op jit(solution)/shard_map/ppermute | solution.py:389
  39.1 2.4 %collective-permute-start.1 = (f32[1,32,512]{2,1,0:T(8,128)S(1)}, f32[1,32,512]{2,1,0:T(8,128)S(1)}, u32[]{:S(2)}, u32[]{:S(2)}) collective-permute-start(f32[1,32,512]{2,1,0:T(8,128)S(1)} %copy.38), channel_id=1, source_target_pairs={{0,128},{64,192},{128,0},{192,64},{256,384},{320,448},{384,256},{4... | collective-permute-start | bytes 196616 | tf_op jit(solution)/shard_map/ppermute | solution.py:389
  41.5 2.8 %collective-permute-start.3 = (f32[2,32,512]{2,1,0:T(8,128)S(1)}, f32[2,32,512]{2,1,0:T(8,128)S(1)}, u32[]{:S(2)}, u32[]{:S(2)}) collective-permute-start(f32[2,32,512]{2,1,0:T(8,128)S(1)} %pad_maximum_fusion.2), channel_id=1, source_target_pairs={{0,64},{64,0},{128,192},{192,128},{256,320},{320,256},{384,448},{4... | collective-permute-start | bytes 393224 | tf_op jit(solution)/shard_map/ppermute | solution.py:389
  44.3 0.2 collective-permute-done.2
  44.5 0.8 collective-permute-done.1
  45.3 3.6 %collective-permute-start.4 = (f32[2,32,512]{2,1,0:T(8,128)S(1)}, f32[2,32,512]{2,1,0:T(8,128)S(1)}, u32[]{:S(2)}, u32[]{:S(2)}) collective-permute-start(f32[2,32,512]{2,1,0:T(8,128)S(1)} %pad_maximum_fusion.3), channel_id=1, source_target_pairs={{0,64},{64,0},{128,192},{192,128},{256,320},{320,256},{384,448},{4... | collective-permute-start | bytes 393224 | tf_op jit(solution)/shard_map/ppermute | solution.py:389
  48.9 6.0 %collective-permute-start.5 = (f32[4,32,512]{2,1,0:T(8,128)S(1)}, f32[4,32,512]{2,1,0:T(8,128)S(1)}, u32[]{:S(2)}, u32[]{:S(2)}) collective-permute-start(f32[4,32,512]{2,1,0:T(8,128)S(1)} %pad_maximum_fusion.own_low_ref), channel_id=1, source_target_pairs={{0,32},{32,0},{1,33},{33,1},{2,34},{34,2},{3,35},{35,3},{4,36},{36... | collective-permute-start | bytes 786440 | tf_op jit(solution)/shard_map/ppermute | solution.py:389
  55.0 0.0 copy-start.13
  55.0 2.8 %collective-permute-start.6 = (f32[4,32,512]{2,1,0:T(8,128)S(1)}, f32[4,32,512]{2,1,0:T(8,128)S(1)}, u32[]{:S(2)}, u32[]{:S(2)}) collective-permute-start(f32[4,32,512]{2,1,0:T(8,128)S(1)} %constant_dynamic-update-slice_fusion.own_high_ref), channel_id=1, source_target_pairs={{0,32},{32,0},{1,33},{33,1},{2,34},{34,2},{3,35},{35,3},{4,36},{36... | collective-permute-start | bytes 786440 | tf_op jit(solution)/shard_map/ppermute | solution.py:389
  57.9 1.1 collective-permute-done.6.other_high_ref
  59.0 10.6 %attend.1 = (f32[32,64,128]{2,1,0:T(8,128)}, f32[8,32,512]{2,1,0:T(8,128)S(1)}, f32[8,32,512]{2,1,0:T(8,128)S(1)}) custom-call(s32[3]{0:T(128)S(1)} %copy-done, s32[4,512]{1,0:T(4,128)S(1)} %copy-done.13, f32[32,64,128]{2,1,0:T(8,128)S(1)} %all-to-all-done.1.data_ref, f32[4,32,512]{2,1,0:T(8,128)S(1)} %pad_maximum_fusion.own_low_ref, ...), custom_call_target="tpu_custom_call" | custom-call | flops 12000000000 | bytes 24000000 | tf_op jit(solution)/shard_map/attend/pallas_call | solution.py:374
  69.6 9.4 %all-to-all-start.2 = ((f32[32,64,128]{2,1,0:T(8,128)}), f32[32,64,128]{2,1,0:T(8,128)S(1)}, u32[]{:S(2)}, u32[]{:S(2)}) async-start(f32[32,64,128]{2,1,0:T(8,128)} %get-tuple-element.45), calls=%async_computation.2 | async-start | bytes 2097152 | tf_op jit(solution)/shard_map/all_to_all | solution.py:385
  79.0 2.6 %collective-permute-start.8 = (f32[8,32,512]{2,1,0:T(8,128)S(1)}, f32[8,32,512]{2,1,0:T(8,128)S(1)}, u32[]{:S(2)}, u32[]{:S(2)}) collective-permute-start(f32[8,32,512]{2,1,0:T(8,128)S(1)} %get-tuple-element.51), channel_id=1, source_target_pairs={{0,32},{32,0},{1,33},{33,1},{2,34},{34,2},{3,35},{35,3},{4,36},{36... | collective-permute-start | bytes 1572872 | tf_op jit(solution)/shard_map/ppermute | solution.py:389
  81.6 1.5 collective-permute-done.8
  83.1 0.1 add.27
  83.2 3.6 %collective-permute-start.9 = (f32[4,32,512]{2,1,0:T(8,128)S(1)}, f32[4,32,512]{2,1,0:T(8,128)S(1)}, u32[]{:S(2)}, u32[]{:S(2)}) collective-permute-start(f32[4,32,512]{2,1,0:T(8,128)S(1)} %slice.25), channel_id=1, source_target_pairs={{0,64},{64,0},{128,192},{192,128},{256,320},{320,256},{384,448},{4... | collective-permute-start | bytes 786440 | tf_op jit(solution)/shard_map/ppermute | solution.py:389
  86.9 6.4 %collective-permute-done.9 = f32[4,32,512]{2,1,0:T(8,128)S(1)} collective-permute-done((f32[4,32,512]{2,1,0:T(8,128)S(1)}, f32[4,32,512]{2,1,0:T(8,128)S(1)}, u32[]{:S(2)}, u32[]{:S(2)}) %collective-permute-start.9) | collective-permute-done | bytes 262176 | tf_op jit(solution)/shard_map/ppermute | solution.py:389
  93.3 2.9 %collective-permute-start.11 = (f32[32,512]{1,0:T(8,128)S(1)}, f32[32,512]{1,0:T(8,128)S(1)}, u32[]{:S(2)}, u32[]{:S(2)}) collective-permute-start(f32[32,512]{1,0:T(8,128)S(1)} %get-tuple-element.68), channel_id=1, source_target_pairs={{0,128},{64,192},{128,0},{192,64},{256,384},{320,448},{384,256},{4... | collective-permute-start | bytes 196616 | tf_op jit(solution)/shard_map/ppermute | solution.py:389
  96.2 5.0 %collective-permute-start.12 = (f32[32,512]{1,0:T(8,128)S(1)}, f32[32,512]{1,0:T(8,128)S(1)}, u32[]{:S(2)}, u32[]{:S(2)}) collective-permute-start(f32[32,512]{1,0:T(8,128)S(1)} %get-tuple-element.69), channel_id=1, source_target_pairs={{0,384},{64,448},{128,256},{192,320},{256,128},{320,192},{384,0},{... | collective-permute-start | bytes 196616 | tf_op jit(solution)/shard_map/ppermute | solution.py:389
  101.2 3.8 %collective-permute-start.10 = (f32[32,512]{1,0:T(8,128)S(1)}, f32[32,512]{1,0:T(8,128)S(1)}, u32[]{:S(2)}, u32[]{:S(2)}) collective-permute-start(f32[32,512]{1,0:T(8,128)S(1)} %get-tuple-element.70), channel_id=1, source_target_pairs={{0,256},{64,320},{128,384},{192,448},{256,0},{320,64},{384,128},{4... | collective-permute-start | bytes 196616 | tf_op jit(solution)/shard_map/ppermute | solution.py:389
  105.0 0.3 all-to-all-done.2
  105.4 1.7 %param_grads.1 = (f32[320,128]{1,0:T(8,128)S(1)}, f32[320,128]{1,0:T(8,128)S(1)}) custom-call(s32[3]{0:T(128)S(1)} %copy-done, f32[8,4,64,128]{3,2,1,0:T(8,128)S(1)} %bitcast.29, f32[512,128]{1,0:T(8,128)S(1)} %copy-done.9, f32[512,128]{1,0:T(8,128)S(1)} %copy-done.11, f32[512,128]{1,0:T(8,128)S(1)} %copy-done.12, f32[16,32,128]{2,1,0:T(8,128)S(1)} %copy-done.1), custom_call_target="tpu_custom_call" | custom-call | flops 2000000000 | bytes 4000000 | tf_op jit(solution)/shard_map/param_grads/pallas_call | solution.py:440
  107.1 4.6 %collective-permute-start.7 = (f32[320,128]{1,0:T(8,128)S(1)}, f32[320,128]{1,0:T(8,128)S(1)}, u32[]{:S(2)}, u32[]{:S(2)}) collective-permute-start(f32[320,128]{1,0:T(8,128)S(1)} %get-tuple-element.49), channel_id=1, source_target_pairs={{0,32},{32,0},{1,33},{33,1},{2,34},{34,2},{3,35},{35,3},{4,36},{36... | collective-permute-start | bytes 491528 | tf_op jit(solution)/shard_map/ppermute | solution.py:389
  111.8 0.1 copy.40
  111.9 0.2 copy.41
  112.1 0.1 copy.42
  112.2 0.5 collective-permute-done.7
  112.8 18.5 %all_to_all.30.recv_ref = f32[32,14,128]{2,1,0:T(8,128)S(1)} all-to-all(f32[32,14,128]{2,1,0:T(8,128)S(1)} %pad_maximum_fusion.1), channel_id=1, replica_groups=mesh['y'=8,'core'=2,'z'=8,'x'=4] {'z','x'}, dimensions={0} | all-to-all | bytes 458752 | tf_op jit(solution)/shard_map/all_to_all | solution.py:385
  131.3 0.8 tail.1
  132.2 6.5 %all-to-all-start.4 = ((f32[8,16,128]{2,1,0:T(8,128)}), f32[8,16,128]{2,1,0:T(8,128)S(1)}, u32[]{:S(2)}, u32[]{:S(2)}) async-start(f32[8,16,128]{2,1,0:T(8,128)} %get-tuple-element.52), calls=%async_computation.4 | async-start | bytes 131072 | tf_op jit(solution)/shard_map/all_to_all | solution.py:385
  138.7 1.4 update.1
  140.2 0.7 copy-done.7
  140.8 1.2 norm_back.1
  142.1 3.8 %all-to-all-done.4.recv_ref = f32[8,16,128]{2,1,0:T(8,128)S(1)} async-done(((f32[8,16,128]{2,1,0:T(8,128)}), f32[8,16,128]{2,1,0:T(8,128)S(1)}, u32[]{:S(2)}, u32[]{:S(2)}) %all-to-all-start.4) | async-done | bytes 65568 | tf_op jit(solution)/shard_map/all_to_all | solution.py:385
  145.9 14.9 %all_to_all.31.refs_1_ = f32[32,16,128]{2,1,0:T(8,128)S(1)} all-to-all(f32[32,16,128]{2,1,0:T(8,128)S(1)} %share.1), channel_id=1, replica_groups=mesh['y'=8,'core'=2,'z'=8,'x'=4] {'z','x'}, dimensions={0} | all-to-all | bytes 524288 | tf_op jit(solution)/shard_map/all_to_all | solution.py:385
  160.9 6.0 %collective-permute-start.13 = (f32[32,16,128]{2,1,0:T(8,128)S(1)}, f32[32,16,128]{2,1,0:T(8,128)S(1)}, u32[]{:S(2)}, u32[]{:S(2)}) collective-permute-start(f32[32,16,128]{2,1,0:T(8,128)S(1)} %all_to_all.31.refs_1_), channel_id=1, source_target_pairs={{0,32},{32,0},{1,33},{33,1},{2,34},{34,2},{3,35},{35,3},{4,36},{36... | collective-permute-start | bytes 786440 | tf_op jit(solution)/shard_map/ppermute | solution.py:389
  166.8 1.1 collective-permute-done.13.refs_2_
  168.0 1.8 %finish.1 = (f32[128,128]{1,0:T(8,128)}, f32[128,128]{1,0:T(8,128)}, f32[128,128]{1,0:T(8,128)}, f32[128,128]{1,0:T(8,128)}, f32[1,128]{1,0:T(1,128)}, /*index=5...) custom-call(s32[3]{0:T(128)S(1)} %copy-done, f32[32,16,128]{2,1,0:T(8,128)S(1)} %all_to_all.31.refs_1_, ...), custom_call_target="tpu_custom_call" | custom-call | flops 1000000000 | bytes 2000000 | tf_op jit(solution)/shard_map/finish/pallas_call | solution.py:462
  (47 shorter events, 0.3 us)
Async XLA Ops:
  2.7 22.5 %all-to-all-start = ((f32[32,4,128]{2,1,0:T(4,128)}), f32[32,4,128]{2,1,0:T(4,128)S(1)}, u32[]{:S(2)}, u32[]{:S(2)}) async-start(f32[32,4,128]{2,1,0:T(4,128)} %bitcast.40), calls=%async_computation | async-start | bytes 131072 | tf_op jit(solution)/shard_map/all_to_all | solution.py:385
  25.3 33.8 %all-to-all-start.1 = ((f32[32,64,128]{2,1,0:T(8,128)}), f32[32,64,128]{2,1,0:T(8,128)S(1)}, u32[]{:S(2)}, u32[]{:S(2)}) async-start(f32[32,64,128]{2,1,0:T(8,128)} %bitcast.39), calls=%async_computation.1 | async-start | bytes 2097152 | tf_op jit(solution)/shard_map/all_to_all | solution.py:385
  29.6 11.8 %collective-permute-start = (f32[1,32,512]{2,1,0:T(8,128)S(1)}, f32[1,32,512]{2,1,0:T(8,128)S(1)}, u32[]{:S(2)}, u32[]{:S(2)}) collective-permute-start(f32[1,32,512]{2,1,0:T(8,128)S(1)} %copy.38), channel_id=1, source_target_pairs={{0,256},{64,320},{128,384},{192,448},{256,0},{320,64},{384,128},{4... | collective-permute-start | bytes 196616 | tf_op jit(solution)/shard_map/ppermute | solution.py:389
  37.1 7.4 %collective-permute-start.2 = (f32[1,32,512]{2,1,0:T(8,128)S(1)}, f32[1,32,512]{2,1,0:T(8,128)S(1)}, u32[]{:S(2)}, u32[]{:S(2)}) collective-permute-start(f32[1,32,512]{2,1,0:T(8,128)S(1)} %copy.38), channel_id=1, source_target_pairs={{0,384},{64,448},{128,256},{192,320},{256,128},{320,192},{384,0},{... | collective-permute-start | bytes 196616 | tf_op jit(solution)/shard_map/ppermute | solution.py:389
  39.1 6.2 %collective-permute-start.1 = (f32[1,32,512]{2,1,0:T(8,128)S(1)}, f32[1,32,512]{2,1,0:T(8,128)S(1)}, u32[]{:S(2)}, u32[]{:S(2)}) collective-permute-start(f32[1,32,512]{2,1,0:T(8,128)S(1)} %copy.38), channel_id=1, source_target_pairs={{0,128},{64,192},{128,0},{192,64},{256,384},{320,448},{384,256},{4... | collective-permute-start | bytes 196616 | tf_op jit(solution)/shard_map/ppermute | solution.py:389
  41.5 13.5 %collective-permute-start.3 = (f32[2,32,512]{2,1,0:T(8,128)S(1)}, f32[2,32,512]{2,1,0:T(8,128)S(1)}, u32[]{:S(2)}, u32[]{:S(2)}) collective-permute-start(f32[2,32,512]{2,1,0:T(8,128)S(1)} %pad_maximum_fusion.2), channel_id=1, source_target_pairs={{0,64},{64,0},{128,192},{192,128},{256,320},{320,256},{384,448},{4... | collective-permute-start | bytes 393224 | tf_op jit(solution)/shard_map/ppermute | solution.py:389
  45.3 9.7 %collective-permute-start.4 = (f32[2,32,512]{2,1,0:T(8,128)S(1)}, f32[2,32,512]{2,1,0:T(8,128)S(1)}, u32[]{:S(2)}, u32[]{:S(2)}) collective-permute-start(f32[2,32,512]{2,1,0:T(8,128)S(1)} %pad_maximum_fusion.3), channel_id=1, source_target_pairs={{0,64},{64,0},{128,192},{192,128},{256,320},{320,256},{384,448},{4... | collective-permute-start | bytes 393224 | tf_op jit(solution)/shard_map/ppermute | solution.py:389
  48.9 9.0 %collective-permute-start.5 = (f32[4,32,512]{2,1,0:T(8,128)S(1)}, f32[4,32,512]{2,1,0:T(8,128)S(1)}, u32[]{:S(2)}, u32[]{:S(2)}) collective-permute-start(f32[4,32,512]{2,1,0:T(8,128)S(1)} %pad_maximum_fusion.own_low_ref), channel_id=1, source_target_pairs={{0,32},{32,0},{1,33},{33,1},{2,34},{34,2},{3,35},{35,3},{4,36},{36... | collective-permute-start | bytes 786440 | tf_op jit(solution)/shard_map/ppermute | solution.py:389
  55.0 4.0 %copy-start.13 = (s32[4,512]{1,0:T(4,128)S(1)}, s32[4,512]{1,0:T(4,128)}, u32[]{:S(2)}) copy-start(s32[4,512]{1,0:T(4,128)} %get-tuple-element.40.keep_ref) | copy-start | bytes 24580
  55.0 4.0 %copy-start = (s32[3]{0:T(128)S(1)}, s32[3]{0:T(128)}, u32[]{:S(2)}) copy-start(s32[3]{0:T(128)} %pad_add_fusion.refs_0_.place_ref) | copy-start | bytes 40
  55.0 4.0 %collective-permute-start.6 = (f32[4,32,512]{2,1,0:T(8,128)S(1)}, f32[4,32,512]{2,1,0:T(8,128)S(1)}, u32[]{:S(2)}, u32[]{:S(2)}) collective-permute-start(f32[4,32,512]{2,1,0:T(8,128)S(1)} %constant_dynamic-update-slice_fusion.own_high_ref), channel_id=1, source_target_pairs={{0,32},{32,0},{1,33},{33,1},{2,34},{34,2},{3,35},{35,3},{4,36},{36... | collective-permute-start | bytes 786440 | tf_op jit(solution)/shard_map/ppermute | solution.py:389
  69.6 35.7 %all-to-all-start.2 = ((f32[32,64,128]{2,1,0:T(8,128)}), f32[32,64,128]{2,1,0:T(8,128)S(1)}, u32[]{:S(2)}, u32[]{:S(2)}) async-start(f32[32,64,128]{2,1,0:T(8,128)} %get-tuple-element.45), calls=%async_computation.2 | async-start | bytes 2097152 | tf_op jit(solution)/shard_map/all_to_all | solution.py:385
  79.0 4.1 %collective-permute-start.8 = (f32[8,32,512]{2,1,0:T(8,128)S(1)}, f32[8,32,512]{2,1,0:T(8,128)S(1)}, u32[]{:S(2)}, u32[]{:S(2)}) collective-permute-start(f32[8,32,512]{2,1,0:T(8,128)S(1)} %get-tuple-element.51), channel_id=1, source_target_pairs={{0,32},{32,0},{1,33},{33,1},{2,34},{34,2},{3,35},{35,3},{4,36},{36... | collective-permute-start | bytes 1572872 | tf_op jit(solution)/shard_map/ppermute | solution.py:389
  83.2 10.0 %collective-permute-start.9 = (f32[4,32,512]{2,1,0:T(8,128)S(1)}, f32[4,32,512]{2,1,0:T(8,128)S(1)}, u32[]{:S(2)}, u32[]{:S(2)}) collective-permute-start(f32[4,32,512]{2,1,0:T(8,128)S(1)} %slice.25), channel_id=1, source_target_pairs={{0,64},{64,0},{128,192},{192,128},{256,320},{320,256},{384,448},{4... | collective-permute-start | bytes 786440 | tf_op jit(solution)/shard_map/ppermute | solution.py:389
  93.2 12.1 %copy-start.9 = (f32[512,128]{1,0:T(8,128)S(1)}, f32[512,128]{1,0:T(8,128)}, u32[]{:S(2)}) copy-start(f32[512,128]{1,0:T(8,128)} %get-tuple-element.39.refs_1_.scaled_ref) | copy-start | bytes 786436
  93.2 12.1 %copy-start.11 = (f32[512,128]{1,0:T(8,128)S(1)}, f32[512,128]{1,0:T(8,128)}, u32[]{:S(2)}) copy-start(f32[512,128]{1,0:T(8,128)} %get-tuple-element.46.gate_ref.refs_1_) | copy-start | bytes 786436
  93.2 12.1 %copy-start.12 = (f32[512,128]{1,0:T(8,128)S(1)}, f32[512,128]{1,0:T(8,128)}, u32[]{:S(2)}) copy-start(f32[512,128]{1,0:T(8,128)} %get-tuple-element.47.dgated_ref.refs_2_) | copy-start | bytes 786436
  93.3 12.1 %copy-start.1 = (f32[16,32,128]{2,1,0:T(8,128)S(1)}, f32[16,32,128]{2,1,0:T(8,128)}, u32[]{:S(2)}) copy-start(f32[16,32,128]{2,1,0:T(8,128)} %cot_ref.1) | copy-start | bytes 786436
  93.3 18.4 %collective-permute-start.11 = (f32[32,512]{1,0:T(8,128)S(1)}, f32[32,512]{1,0:T(8,128)S(1)}, u32[]{:S(2)}, u32[]{:S(2)}) collective-permute-start(f32[32,512]{1,0:T(8,128)S(1)} %get-tuple-element.68), channel_id=1, source_target_pairs={{0,128},{64,192},{128,0},{192,64},{256,384},{320,448},{384,256},{4... | collective-permute-start | bytes 196616 | tf_op jit(solution)/shard_map/ppermute | solution.py:389
  96.2 15.5 %collective-permute-start.12 = (f32[32,512]{1,0:T(8,128)S(1)}, f32[32,512]{1,0:T(8,128)S(1)}, u32[]{:S(2)}, u32[]{:S(2)}) collective-permute-start(f32[32,512]{1,0:T(8,128)S(1)} %get-tuple-element.69), channel_id=1, source_target_pairs={{0,384},{64,448},{128,256},{192,320},{256,128},{320,192},{384,0},{... | collective-permute-start | bytes 196616 | tf_op jit(solution)/shard_map/ppermute | solution.py:389
  101.2 10.5 %collective-permute-start.10 = (f32[32,512]{1,0:T(8,128)S(1)}, f32[32,512]{1,0:T(8,128)S(1)}, u32[]{:S(2)}, u32[]{:S(2)}) collective-permute-start(f32[32,512]{1,0:T(8,128)S(1)} %get-tuple-element.70), channel_id=1, source_target_pairs={{0,256},{64,320},{128,384},{192,448},{256,0},{320,64},{384,128},{4... | collective-permute-start | bytes 196616 | tf_op jit(solution)/shard_map/ppermute | solution.py:389
  107.1 5.6 %collective-permute-start.7 = (f32[320,128]{1,0:T(8,128)S(1)}, f32[320,128]{1,0:T(8,128)S(1)}, u32[]{:S(2)}, u32[]{:S(2)}) collective-permute-start(f32[320,128]{1,0:T(8,128)S(1)} %get-tuple-element.49), channel_id=1, source_target_pairs={{0,32},{32,0},{1,33},{33,1},{2,34},{34,2},{3,35},{35,3},{4,36},{36... | collective-permute-start | bytes 491528 | tf_op jit(solution)/shard_map/ppermute | solution.py:389
  131.3 7.3 %copy-start.4 = (f32[128,128]{1,0:T(8,128)S(1)}, f32[128,128]{1,0:T(8,128)}, u32[]{:S(2)}) copy-start(f32[128,128]{1,0:T(8,128)} %refs_5_.5) | copy-start | bytes 196612
  131.3 7.3 %copy-start.5 = (f32[128,128]{1,0:T(8,128)S(1)}, f32[128,128]{1,0:T(8,128)}, u32[]{:S(2)}) copy-start(f32[128,128]{1,0:T(8,128)} %refs_6_.5) | copy-start | bytes 196612
  131.3 7.3 %copy-start.6 = (f32[128,128]{1,0:T(8,128)S(1)}, f32[128,128]{1,0:T(8,128)}, u32[]{:S(2)}) copy-start(f32[128,128]{1,0:T(8,128)} %refs_7_.5) | copy-start | bytes 196612
  132.2 6.5 %copy-start.2 = (f32[128,128]{1,0:T(8,128)S(1)}, f32[128,128]{1,0:T(8,128)}, u32[]{:S(2)}) copy-start(f32[128,128]{1,0:T(8,128)} %refs_7_.4) | copy-start | bytes 196612
  132.2 6.5 %copy-start.3 = (f32[128,128]{1,0:T(8,128)S(1)}, f32[128,128]{1,0:T(8,128)}, u32[]{:S(2)}) copy-start(f32[128,128]{1,0:T(8,128)} %refs_4_.5) | copy-start | bytes 196612
  132.2 13.7 %all-to-all-start.4 = ((f32[8,16,128]{2,1,0:T(8,128)}), f32[8,16,128]{2,1,0:T(8,128)S(1)}, u32[]{:S(2)}, u32[]{:S(2)}) async-start(f32[8,16,128]{2,1,0:T(8,128)} %get-tuple-element.52), calls=%async_computation.4 | async-start | bytes 131072 | tf_op jit(solution)/shard_map/all_to_all | solution.py:385
  138.7 1.5 copy-start.10
  140.2 0.7 copy-start.7
  140.2 0.7 copy-start.8
  160.9 7.1 %collective-permute-start.13 = (f32[32,16,128]{2,1,0:T(8,128)S(1)}, f32[32,16,128]{2,1,0:T(8,128)S(1)}, u32[]{:S(2)}, u32[]{:S(2)}) collective-permute-start(f32[32,16,128]{2,1,0:T(8,128)S(1)} %all_to_all.31.refs_1_), channel_id=1, source_target_pairs={{0,32},{32,0},{1,33},{33,1},{2,34},{34,2},{3,35},{35,3},{4,36},{36... | collective-permute-start | bytes 786440 | tf_op jit(solution)/shard_map/ppermute | solution.py:389

commit v6 on v5

--- a/solution.py
+++ b/solution.py
@@ -185,14 +185,14 @@
         d_left = bdot(d_both, rows_ref[:, 128:256]).astype(BF16)
         d_weights = bdot(d_left, v_right, NT)
         d_t = bdot(turns_ref[64:128], d_both, NT).astype(BF16)
-        both = bdot(d_t, wh)
-        dv_t = both[0:32] + both[32:64] + bdot(d_t[0:32], wl)
-        return weights, output, d_weights, centred, dv_t, q_t
+        return weights, output, d_weights, centred, (d_t, wh, wl), q_t
 
     def third(column, keys, chunk, state):
         k_right, v_right, k_both, k_first, v_both, v_first, keep = keys
         starts, bias_refs, db_ref, s0 = chunk
-        weights, output, d_weights, centred, dv_t, q_t = state
+        weights, output, d_weights, centred, (d_t, wh, wl), q_t = state
+        both = bdot(d_t, wh)
+        dv_t = both[0:32] + both[32:64] + bdot(d_t[0:32], wl)
         d_scores = weights * (d_weights - centred)
         if column == 0:
             db_ref[s0 : s0 + per] = d_scores.reshape(per, 32, 512)

time: 171 us -> 170 us (level)
  no operation moved by 1% of the time
where the time goes in v6:
time: 170 us; the launch traced here: 169 us
  starting transfers between devices  89.1 us (52%)
  blocking collectives  33.4 us (20%)
  Pallas kernels  21.9 us (13%)
  waiting for transfers between devices  21.1 us (12%)
    ppermute x14, starting transfers between devices, partner(): lax.ppermute(value, axis, [(at, at ^ flip) for at in range(lax.axis_size(...  55.5 us
    all_to_all x4, starting transfers between devices, swap(): return lax.all_to_all(value, axes, 0, 0, tiled=False)  33.6 us
    all_to_all x2, blocking collectives, swap(): return lax.all_to_all(value, axes, 0, 0, tiled=False)  33.4 us
    ppermute x14, waiting for transfers between devices, partner(): lax.ppermute(value, axis, [(at, at ^ flip) for at in range(lax.axis_size(...  11.6 us
    pallas_call x1, Pallas kernels, attend_call(): call(attend_kernel, [shaped(32, 64, 128), shaped(8, 32, 512), shaped(8, 3...  9.84 us
    all_to_all x4, waiting for transfers between devices, swap(): return lax.all_to_all(value, axes, 0, 0, tiled=False)  9.42 us
  transfers between devices with their start and end apart: 18, of which 10 were waited for; matrix products, arithmetic and copies ran while one was open for 1% of the time, Pallas kernels for 4%

profile of v6, /device:TPU:1, one launch (start us, length us, event | category | flops | bytes accessed | tf_op | source)
XLA Modules:
  0.0 169.0 jit_solution(15365007130876398520)
XLA Ops:
  0.6 2.1 %norm_bias.1 = (f32[8,4,4,128]{3,2,1,0:T(4,128)}, f32[512,128]{1,0:T(8,128)}, f32[512,128]{1,0:T(8,128)}) custom-call(f32[16,32,128]{2,1,0:T(8,128)} %x_ref.1, f32[1,128]{1,0:T(1,128)} %bitcast.31, f32[4,128]{1,0:T(4,128)} %refs_8_.1), custom_call_target="tpu_custom_call" | custom-call | flops 1000000000 | bytes 2000000 | tf_op jit(solution)/shard_map/norm_bias/pallas_call | solution.py:405
  2.7 13.7 %all-to-all-start = ((f32[32,4,128]{2,1,0:T(4,128)}), f32[32,4,128]{2,1,0:T(4,128)S(1)}, u32[]{:S(2)}, u32[]{:S(2)}) async-start(f32[32,4,128]{2,1,0:T(4,128)} %bitcast.40), calls=%async_computation | async-start | bytes 131072 | tf_op jit(solution)/shard_map/all_to_all | solution.py:385
  16.4 0.6 pad_add_fusion.refs_0_.place_ref
  17.0 2.9 %project.1 = (f32[8,4,64,128]{3,2,1,0:T(8,128)}, f32[512,128]{1,0:T(8,128)}, f32[512,128]{1,0:T(8,128)}, s32[4,512]{1,0:T(4,128)}) custom-call(s32[3]{0:T(128)} %pad_add_fusion.refs_0_.place_ref, f32[512,128]{1,0:T(8,128)} %get-tuple-element.39.refs_1_.scaled_ref, f32[16,32,128]{2,1,0:T(8,128)} %cot_ref.1, f32[1,128]{1,0:T(1,128)} %bitcast.32, ...), custom_call_target="tpu_custom_call" | custom-call | flops 2000000000 | bytes 4000000 | tf_op jit(solution)/shard_map/project/pallas_call | solution.py:409
  20.0 5.3 %all-to-all-done = f32[32,4,128]{2,1,0:T(4,128)S(1)} async-done(((f32[32,4,128]{2,1,0:T(4,128)}), f32[32,4,128]{2,1,0:T(4,128)S(1)}, u32[]{:S(2)}, u32[]{:S(2)}) %all-to-all-start) | async-done | bytes 65568 | tf_op jit(solution)/shard_map/all_to_all | solution.py:385
  25.3 3.9 %all-to-all-start.1 = ((f32[32,64,128]{2,1,0:T(8,128)}), f32[32,64,128]{2,1,0:T(8,128)S(1)}, u32[]{:S(2)}, u32[]{:S(2)}) async-start(f32[32,64,128]{2,1,0:T(8,128)} %bitcast.39), calls=%async_computation.1 | async-start | bytes 2097152 | tf_op jit(solution)/shard_map/all_to_all | solution.py:385
  29.2 0.1 copy.33
  29.3 0.2 copy.34
  29.5 0.1 copy.38
  29.6 7.5 %collective-permute-start = (f32[1,32,512]{2,1,0:T(8,128)S(1)}, f32[1,32,512]{2,1,0:T(8,128)S(1)}, u32[]{:S(2)}, u32[]{:S(2)}) collective-permute-start(f32[1,32,512]{2,1,0:T(8,128)S(1)} %copy.38), channel_id=1, source_target_pairs={{0,256},{64,320},{128,384},{192,448},{256,0},{320,64},{384,128},{4... | collective-permute-start | bytes 196616 | tf_op jit(solution)/shard_map/ppermute | solution.py:389
  37.1 2.0 %collective-permute-start.2 = (f32[1,32,512]{2,1,0:T(8,128)S(1)}, f32[1,32,512]{2,1,0:T(8,128)S(1)}, u32[]{:S(2)}, u32[]{:S(2)}) collective-permute-start(f32[1,32,512]{2,1,0:T(8,128)S(1)} %copy.38), channel_id=1, source_target_pairs={{0,384},{64,448},{128,256},{192,320},{256,128},{320,192},{384,0},{... | collective-permute-start | bytes 196616 | tf_op jit(solution)/shard_map/ppermute | solution.py:389
  39.1 2.4 %collective-permute-start.1 = (f32[1,32,512]{2,1,0:T(8,128)S(1)}, f32[1,32,512]{2,1,0:T(8,128)S(1)}, u32[]{:S(2)}, u32[]{:S(2)}) collective-permute-start(f32[1,32,512]{2,1,0:T(8,128)S(1)} %copy.38), channel_id=1, source_target_pairs={{0,128},{64,192},{128,0},{192,64},{256,384},{320,448},{384,256},{4... | collective-permute-start | bytes 196616 | tf_op jit(solution)/shard_map/ppermute | solution.py:389
  41.5 2.8 %collective-permute-start.3 = (f32[2,32,512]{2,1,0:T(8,128)S(1)}, f32[2,32,512]{2,1,0:T(8,128)S(1)}, u32[]{:S(2)}, u32[]{:S(2)}) collective-permute-start(f32[2,32,512]{2,1,0:T(8,128)S(1)} %pad_maximum_fusion.2), channel_id=1, source_target_pairs={{0,64},{64,0},{128,192},{192,128},{256,320},{320,256},{384,448},{4... | collective-permute-start | bytes 393224 | tf_op jit(solution)/shard_map/ppermute | solution.py:389
  44.3 0.2 collective-permute-done.2
  44.5 0.8 collective-permute-done.1
  45.3 3.6 %collective-permute-start.4 = (f32[2,32,512]{2,1,0:T(8,128)S(1)}, f32[2,32,512]{2,1,0:T(8,128)S(1)}, u32[]{:S(2)}, u32[]{:S(2)}) collective-permute-start(f32[2,32,512]{2,1,0:T(8,128)S(1)} %pad_maximum_fusion.3), channel_id=1, source_target_pairs={{0,64},{64,0},{128,192},{192,128},{256,320},{320,256},{384,448},{4... | collective-permute-start | bytes 393224 | tf_op jit(solution)/shard_map/ppermute | solution.py:389
  48.9 6.0 %collective-permute-start.5 = (f32[4,32,512]{2,1,0:T(8,128)S(1)}, f32[4,32,512]{2,1,0:T(8,128)S(1)}, u32[]{:S(2)}, u32[]{:S(2)}) collective-permute-start(f32[4,32,512]{2,1,0:T(8,128)S(1)} %pad_maximum_fusion.own_low_ref), channel_id=1, source_target_pairs={{0,32},{32,0},{1,33},{33,1},{2,34},{34,2},{3,35},{35,3},{4,36},{36... | collective-permute-start | bytes 786440 | tf_op jit(solution)/shard_map/ppermute | solution.py:389
  55.0 0.0 copy-start.13
  55.0 2.8 %collective-permute-start.6 = (f32[4,32,512]{2,1,0:T(8,128)S(1)}, f32[4,32,512]{2,1,0:T(8,128)S(1)}, u32[]{:S(2)}, u32[]{:S(2)}) collective-permute-start(f32[4,32,512]{2,1,0:T(8,128)S(1)} %constant_dynamic-update-slice_fusion.own_high_ref), channel_id=1, source_target_pairs={{0,32},{32,0},{1,33},{33,1},{2,34},{34,2},{3,35},{35,3},{4,36},{36... | collective-permute-start | bytes 786440 | tf_op jit(solution)/shard_map/ppermute | solution.py:389
  57.9 1.1 collective-permute-done.6.other_high_ref
  59.0 9.8 %attend.1 = (f32[32,64,128]{2,1,0:T(8,128)}, f32[8,32,512]{2,1,0:T(8,128)S(1)}, f32[8,32,512]{2,1,0:T(8,128)S(1)}) custom-call(s32[3]{0:T(128)S(1)} %copy-done, s32[4,512]{1,0:T(4,128)S(1)} %copy-done.13, f32[32,64,128]{2,1,0:T(8,128)S(1)} %all-to-all-done.1.data_ref, f32[4,32,512]{2,1,0:T(8,128)S(1)} %pad_maximum_fusion.own_low_ref, ...), custom_call_target="tpu_custom_call" | custom-call | flops 12000000000 | bytes 24000000 | tf_op jit(solution)/shard_map/attend/pallas_call | solution.py:374
  68.9 9.4 %all-to-all-start.2 = ((f32[32,64,128]{2,1,0:T(8,128)}), f32[32,64,128]{2,1,0:T(8,128)S(1)}, u32[]{:S(2)}, u32[]{:S(2)}) async-start(f32[32,64,128]{2,1,0:T(8,128)} %get-tuple-element.45), calls=%async_computation.2 | async-start | bytes 2097152 | tf_op jit(solution)/shard_map/all_to_all | solution.py:385
  78.3 2.6 %collective-permute-start.8 = (f32[8,32,512]{2,1,0:T(8,128)S(1)}, f32[8,32,512]{2,1,0:T(8,128)S(1)}, u32[]{:S(2)}, u32[]{:S(2)}) collective-permute-start(f32[8,32,512]{2,1,0:T(8,128)S(1)} %get-tuple-element.51), channel_id=1, source_target_pairs={{0,32},{32,0},{1,33},{33,1},{2,34},{34,2},{3,35},{35,3},{4,36},{36... | collective-permute-start | bytes 1572872 | tf_op jit(solution)/shard_map/ppermute | solution.py:389
  80.9 1.5 collective-permute-done.8
  82.4 0.1 add.27
  82.5 3.6 %collective-permute-start.9 = (f32[4,32,512]{2,1,0:T(8,128)S(1)}, f32[4,32,512]{2,1,0:T(8,128)S(1)}, u32[]{:S(2)}, u32[]{:S(2)}) collective-permute-start(f32[4,32,512]{2,1,0:T(8,128)S(1)} %slice.25), channel_id=1, source_target_pairs={{0,64},{64,0},{128,192},{192,128},{256,320},{320,256},{384,448},{4... | collective-permute-start | bytes 786440 | tf_op jit(solution)/shard_map/ppermute | solution.py:389
  86.1 6.4 %collective-permute-done.9 = f32[4,32,512]{2,1,0:T(8,128)S(1)} collective-permute-done((f32[4,32,512]{2,1,0:T(8,128)S(1)}, f32[4,32,512]{2,1,0:T(8,128)S(1)}, u32[]{:S(2)}, u32[]{:S(2)}) %collective-permute-start.9) | collective-permute-done | bytes 262176 | tf_op jit(solution)/shard_map/ppermute | solution.py:389
  92.6 2.9 %collective-permute-start.11 = (f32[32,512]{1,0:T(8,128)S(1)}, f32[32,512]{1,0:T(8,128)S(1)}, u32[]{:S(2)}, u32[]{:S(2)}) collective-permute-start(f32[32,512]{1,0:T(8,128)S(1)} %get-tuple-element.68), channel_id=1, source_target_pairs={{0,128},{64,192},{128,0},{192,64},{256,384},{320,448},{384,256},{4... | collective-permute-start | bytes 196616 | tf_op jit(solution)/shard_map/ppermute | solution.py:389
  95.4 5.0 %collective-permute-start.12 = (f32[32,512]{1,0:T(8,128)S(1)}, f32[32,512]{1,0:T(8,128)S(1)}, u32[]{:S(2)}, u32[]{:S(2)}) collective-permute-start(f32[32,512]{1,0:T(8,128)S(1)} %get-tuple-element.69), channel_id=1, source_target_pairs={{0,384},{64,448},{128,256},{192,320},{256,128},{320,192},{384,0},{... | collective-permute-start | bytes 196616 | tf_op jit(solution)/shard_map/ppermute | solution.py:389
  100.5 3.8 %collective-permute-start.10 = (f32[32,512]{1,0:T(8,128)S(1)}, f32[32,512]{1,0:T(8,128)S(1)}, u32[]{:S(2)}, u32[]{:S(2)}) collective-permute-start(f32[32,512]{1,0:T(8,128)S(1)} %get-tuple-element.70), channel_id=1, source_target_pairs={{0,256},{64,320},{128,384},{192,448},{256,0},{320,64},{384,128},{4... | collective-permute-start | bytes 196616 | tf_op jit(solution)/shard_map/ppermute | solution.py:389
  104.3 0.3 all-to-all-done.2
  104.6 1.7 %param_grads.1 = (f32[320,128]{1,0:T(8,128)S(1)}, f32[320,128]{1,0:T(8,128)S(1)}) custom-call(s32[3]{0:T(128)S(1)} %copy-done, f32[8,4,64,128]{3,2,1,0:T(8,128)S(1)} %bitcast.29, f32[512,128]{1,0:T(8,128)S(1)} %copy-done.9, f32[512,128]{1,0:T(8,128)S(1)} %copy-done.11, f32[512,128]{1,0:T(8,128)S(1)} %copy-done.12, f32[16,32,128]{2,1,0:T(8,128)S(1)} %copy-done.1), custom_call_target="tpu_custom_call" | custom-call | flops 2000000000 | bytes 4000000 | tf_op jit(solution)/shard_map/param_grads/pallas_call | solution.py:440
  106.3 4.6 %collective-permute-start.7 = (f32[320,128]{1,0:T(8,128)S(1)}, f32[320,128]{1,0:T(8,128)S(1)}, u32[]{:S(2)}, u32[]{:S(2)}) collective-permute-start(f32[320,128]{1,0:T(8,128)S(1)} %get-tuple-element.49), channel_id=1, source_target_pairs={{0,32},{32,0},{1,33},{33,1},{2,34},{34,2},{3,35},{35,3},{4,36},{36... | collective-permute-start | bytes 491528 | tf_op jit(solution)/shard_map/ppermute | solution.py:389
  111.0 0.1 copy.40
  111.1 0.2 copy.41
  111.3 0.1 copy.42
  111.5 0.5 collective-permute-done.7
  112.0 18.5 %all_to_all.30.recv_ref = f32[32,14,128]{2,1,0:T(8,128)S(1)} all-to-all(f32[32,14,128]{2,1,0:T(8,128)S(1)} %pad_maximum_fusion.1), channel_id=1, replica_groups=mesh['y'=8,'core'=2,'z'=8,'x'=4] {'z','x'}, dimensions={0} | all-to-all | bytes 458752 | tf_op jit(solution)/shard_map/all_to_all | solution.py:385
  130.5 0.8 tail.1
  131.3 6.5 %all-to-all-start.4 = ((f32[8,16,128]{2,1,0:T(8,128)}), f32[8,16,128]{2,1,0:T(8,128)S(1)}, u32[]{:S(2)}, u32[]{:S(2)}) async-start(f32[8,16,128]{2,1,0:T(8,128)} %get-tuple-element.52), calls=%async_computation.4 | async-start | bytes 131072 | tf_op jit(solution)/shard_map/all_to_all | solution.py:385
  137.9 1.4 update.1
  139.4 0.7 copy-done.7
  140.1 1.2 norm_back.1
  141.3 3.8 %all-to-all-done.4.recv_ref = f32[8,16,128]{2,1,0:T(8,128)S(1)} async-done(((f32[8,16,128]{2,1,0:T(8,128)}), f32[8,16,128]{2,1,0:T(8,128)S(1)}, u32[]{:S(2)}, u32[]{:S(2)}) %all-to-all-start.4) | async-done | bytes 65568 | tf_op jit(solution)/shard_map/all_to_all | solution.py:385
  145.1 14.9 %all_to_all.31.refs_1_ = f32[32,16,128]{2,1,0:T(8,128)S(1)} all-to-all(f32[32,16,128]{2,1,0:T(8,128)S(1)} %share.1), channel_id=1, replica_groups=mesh['y'=8,'core'=2,'z'=8,'x'=4] {'z','x'}, dimensions={0} | all-to-all | bytes 524288 | tf_op jit(solution)/shard_map/all_to_all | solution.py:385
  160.1 6.0 %collective-permute-start.13 = (f32[32,16,128]{2,1,0:T(8,128)S(1)}, f32[32,16,128]{2,1,0:T(8,128)S(1)}, u32[]{:S(2)}, u32[]{:S(2)}) collective-permute-start(f32[32,16,128]{2,1,0:T(8,128)S(1)} %all_to_all.31.refs_1_), channel_id=1, source_target_pairs={{0,32},{32,0},{1,33},{33,1},{2,34},{34,2},{3,35},{35,3},{4,36},{36... | collective-permute-start | bytes 786440 | tf_op jit(solution)/shard_map/ppermute | solution.py:389
  166.0 1.1 collective-permute-done.13.refs_2_
  167.2 1.8 %finish.1 = (f32[128,128]{1,0:T(8,128)}, f32[128,128]{1,0:T(8,128)}, f32[128,128]{1,0:T(8,128)}, f32[128,128]{1,0:T(8,128)}, f32[1,128]{1,0:T(1,128)}, /*index=5...) custom-call(s32[3]{0:T(128)S(1)} %copy-done, f32[32,16,128]{2,1,0:T(8,128)S(1)} %all_to_all.31.refs_1_, ...), custom_call_target="tpu_custom_call" | custom-call | flops 1000000000 | bytes 2000000 | tf_op jit(solution)/shard_map/finish/pallas_call | solution.py:462
  (47 shorter events, 0.3 us)
Async XLA Ops:
  2.7 22.5 %all-to-all-start = ((f32[32,4,128]{2,1,0:T(4,128)}), f32[32,4,128]{2,1,0:T(4,128)S(1)}, u32[]{:S(2)}, u32[]{:S(2)}) async-start(f32[32,4,128]{2,1,0:T(4,128)} %bitcast.40), calls=%async_computation | async-start | bytes 131072 | tf_op jit(solution)/shard_map/all_to_all | solution.py:385
  25.3 33.8 %all-to-all-start.1 = ((f32[32,64,128]{2,1,0:T(8,128)}), f32[32,64,128]{2,1,0:T(8,128)S(1)}, u32[]{:S(2)}, u32[]{:S(2)}) async-start(f32[32,64,128]{2,1,0:T(8,128)} %bitcast.39), calls=%async_computation.1 | async-start | bytes 2097152 | tf_op jit(solution)/shard_map/all_to_all | solution.py:385
  29.6 11.8 %collective-permute-start = (f32[1,32,512]{2,1,0:T(8,128)S(1)}, f32[1,32,512]{2,1,0:T(8,128)S(1)}, u32[]{:S(2)}, u32[]{:S(2)}) collective-permute-start(f32[1,32,512]{2,1,0:T(8,128)S(1)} %copy.38), channel_id=1, source_target_pairs={{0,256},{64,320},{128,384},{192,448},{256,0},{320,64},{384,128},{4... | collective-permute-start | bytes 196616 | tf_op jit(solution)/shard_map/ppermute | solution.py:389
  37.1 7.4 %collective-permute-start.2 = (f32[1,32,512]{2,1,0:T(8,128)S(1)}, f32[1,32,512]{2,1,0:T(8,128)S(1)}, u32[]{:S(2)}, u32[]{:S(2)}) collective-permute-start(f32[1,32,512]{2,1,0:T(8,128)S(1)} %copy.38), channel_id=1, source_target_pairs={{0,384},{64,448},{128,256},{192,320},{256,128},{320,192},{384,0},{... | collective-permute-start | bytes 196616 | tf_op jit(solution)/shard_map/ppermute | solution.py:389
  39.1 6.2 %collective-permute-start.1 = (f32[1,32,512]{2,1,0:T(8,128)S(1)}, f32[1,32,512]{2,1,0:T(8,128)S(1)}, u32[]{:S(2)}, u32[]{:S(2)}) collective-permute-start(f32[1,32,512]{2,1,0:T(8,128)S(1)} %copy.38), channel_id=1, source_target_pairs={{0,128},{64,192},{128,0},{192,64},{256,384},{320,448},{384,256},{4... | collective-permute-start | bytes 196616 | tf_op jit(solution)/shard_map/ppermute | solution.py:389
  41.5 13.5 %collective-permute-start.3 = (f32[2,32,512]{2,1,0:T(8,128)S(1)}, f32[2,32,512]{2,1,0:T(8,128)S(1)}, u32[]{:S(2)}, u32[]{:S(2)}) collective-permute-start(f32[2,32,512]{2,1,0:T(8,128)S(1)} %pad_maximum_fusion.2), channel_id=1, source_target_pairs={{0,64},{64,0},{128,192},{192,128},{256,320},{320,256},{384,448},{4... | collective-permute-start | bytes 393224 | tf_op jit(solution)/shard_map/ppermute | solution.py:389
  45.3 9.7 %collective-permute-start.4 = (f32[2,32,512]{2,1,0:T(8,128)S(1)}, f32[2,32,512]{2,1,0:T(8,128)S(1)}, u32[]{:S(2)}, u32[]{:S(2)}) collective-permute-start(f32[2,32,512]{2,1,0:T(8,128)S(1)} %pad_maximum_fusion.3), channel_id=1, source_target_pairs={{0,64},{64,0},{128,192},{192,128},{256,320},{320,256},{384,448},{4... | collective-permute-start | bytes 393224 | tf_op jit(solution)/shard_map/ppermute | solution.py:389
  48.9 9.0 %collective-permute-start.5 = (f32[4,32,512]{2,1,0:T(8,128)S(1)}, f32[4,32,512]{2,1,0:T(8,128)S(1)}, u32[]{:S(2)}, u32[]{:S(2)}) collective-permute-start(f32[4,32,512]{2,1,0:T(8,128)S(1)} %pad_maximum_fusion.own_low_ref), channel_id=1, source_target_pairs={{0,32},{32,0},{1,33},{33,1},{2,34},{34,2},{3,35},{35,3},{4,36},{36... | collective-permute-start | bytes 786440 | tf_op jit(solution)/shard_map/ppermute | solution.py:389
  55.0 4.0 %copy-start.13 = (s32[4,512]{1,0:T(4,128)S(1)}, s32[4,512]{1,0:T(4,128)}, u32[]{:S(2)}) copy-start(s32[4,512]{1,0:T(4,128)} %get-tuple-element.40.keep_ref) | copy-start | bytes 24580
  55.0 4.0 %copy-start = (s32[3]{0:T(128)S(1)}, s32[3]{0:T(128)}, u32[]{:S(2)}) copy-start(s32[3]{0:T(128)} %pad_add_fusion.refs_0_.place_ref) | copy-start | bytes 40
  55.0 4.0 %collective-permute-start.6 = (f32[4,32,512]{2,1,0:T(8,128)S(1)}, f32[4,32,512]{2,1,0:T(8,128)S(1)}, u32[]{:S(2)}, u32[]{:S(2)}) collective-permute-start(f32[4,32,512]{2,1,0:T(8,128)S(1)} %constant_dynamic-update-slice_fusion.own_high_ref), channel_id=1, source_target_pairs={{0,32},{32,0},{1,33},{33,1},{2,34},{34,2},{3,35},{35,3},{4,36},{36... | collective-permute-start | bytes 786440 | tf_op jit(solution)/shard_map/ppermute | solution.py:389
  68.9 35.7 %all-to-all-start.2 = ((f32[32,64,128]{2,1,0:T(8,128)}), f32[32,64,128]{2,1,0:T(8,128)S(1)}, u32[]{:S(2)}, u32[]{:S(2)}) async-start(f32[32,64,128]{2,1,0:T(8,128)} %get-tuple-element.45), calls=%async_computation.2 | async-start | bytes 2097152 | tf_op jit(solution)/shard_map/all_to_all | solution.py:385
  78.3 4.1 %collective-permute-start.8 = (f32[8,32,512]{2,1,0:T(8,128)S(1)}, f32[8,32,512]{2,1,0:T(8,128)S(1)}, u32[]{:S(2)}, u32[]{:S(2)}) collective-permute-start(f32[8,32,512]{2,1,0:T(8,128)S(1)} %get-tuple-element.51), channel_id=1, source_target_pairs={{0,32},{32,0},{1,33},{33,1},{2,34},{34,2},{3,35},{35,3},{4,36},{36... | collective-permute-start | bytes 1572872 | tf_op jit(solution)/shard_map/ppermute | solution.py:389
  82.5 10.0 %collective-permute-start.9 = (f32[4,32,512]{2,1,0:T(8,128)S(1)}, f32[4,32,512]{2,1,0:T(8,128)S(1)}, u32[]{:S(2)}, u32[]{:S(2)}) collective-permute-start(f32[4,32,512]{2,1,0:T(8,128)S(1)} %slice.25), channel_id=1, source_target_pairs={{0,64},{64,0},{128,192},{192,128},{256,320},{320,256},{384,448},{4... | collective-permute-start | bytes 786440 | tf_op jit(solution)/shard_map/ppermute | solution.py:389
  92.5 12.1 %copy-start.9 = (f32[512,128]{1,0:T(8,128)S(1)}, f32[512,128]{1,0:T(8,128)}, u32[]{:S(2)}) copy-start(f32[512,128]{1,0:T(8,128)} %get-tuple-element.39.refs_1_.scaled_ref) | copy-start | bytes 786436
  92.5 12.1 %copy-start.11 = (f32[512,128]{1,0:T(8,128)S(1)}, f32[512,128]{1,0:T(8,128)}, u32[]{:S(2)}) copy-start(f32[512,128]{1,0:T(8,128)} %get-tuple-element.46.gate_ref.refs_1_) | copy-start | bytes 786436
  92.5 12.1 %copy-start.12 = (f32[512,128]{1,0:T(8,128)S(1)}, f32[512,128]{1,0:T(8,128)}, u32[]{:S(2)}) copy-start(f32[512,128]{1,0:T(8,128)} %get-tuple-element.47.dgated_ref.refs_2_) | copy-start | bytes 786436
  92.5 12.1 %copy-start.1 = (f32[16,32,128]{2,1,0:T(8,128)S(1)}, f32[16,32,128]{2,1,0:T(8,128)}, u32[]{:S(2)}) copy-start(f32[16,32,128]{2,1,0:T(8,128)} %cot_ref.1) | copy-start | bytes 786436
  92.6 18.4 %collective-permute-start.11 = (f32[32,512]{1,0:T(8,128)S(1)}, f32[32,512]{1,0:T(8,128)S(1)}, u32[]{:S(2)}, u32[]{:S(2)}) collective-permute-start(f32[32,512]{1,0:T(8,128)S(1)} %get-tuple-element.68), channel_id=1, source_target_pairs={{0,128},{64,192},{128,0},{192,64},{256,384},{320,448},{384,256},{4... | collective-permute-start | bytes 196616 | tf_op jit(solution)/shard_map/ppermute | solution.py:389
  95.4 15.5 %collective-permute-start.12 = (f32[32,512]{1,0:T(8,128)S(1)}, f32[32,512]{1,0:T(8,128)S(1)}, u32[]{:S(2)}, u32[]{:S(2)}) collective-permute-start(f32[32,512]{1,0:T(8,128)S(1)} %get-tuple-element.69), channel_id=1, source_target_pairs={{0,384},{64,448},{128,256},{192,320},{256,128},{320,192},{384,0},{... | collective-permute-start | bytes 196616 | tf_op jit(solution)/shard_map/ppermute | solution.py:389
  100.5 10.5 %collective-permute-start.10 = (f32[32,512]{1,0:T(8,128)S(1)}, f32[32,512]{1,0:T(8,128)S(1)}, u32[]{:S(2)}, u32[]{:S(2)}) collective-permute-start(f32[32,512]{1,0:T(8,128)S(1)} %get-tuple-element.70), channel_id=1, source_target_pairs={{0,256},{64,320},{128,384},{192,448},{256,0},{320,64},{384,128},{4... | collective-permute-start | bytes 196616 | tf_op jit(solution)/shard_map/ppermute | solution.py:389
  106.3 5.6 %collective-permute-start.7 = (f32[320,128]{1,0:T(8,128)S(1)}, f32[320,128]{1,0:T(8,128)S(1)}, u32[]{:S(2)}, u32[]{:S(2)}) collective-permute-start(f32[320,128]{1,0:T(8,128)S(1)} %get-tuple-element.49), channel_id=1, source_target_pairs={{0,32},{32,0},{1,33},{33,1},{2,34},{34,2},{3,35},{35,3},{4,36},{36... | collective-permute-start | bytes 491528 | tf_op jit(solution)/shard_map/ppermute | solution.py:389
  130.5 7.4 %copy-start.4 = (f32[128,128]{1,0:T(8,128)S(1)}, f32[128,128]{1,0:T(8,128)}, u32[]{:S(2)}) copy-start(f32[128,128]{1,0:T(8,128)} %refs_5_.5) | copy-start | bytes 196612
  130.5 7.4 %copy-start.5 = (f32[128,128]{1,0:T(8,128)S(1)}, f32[128,128]{1,0:T(8,128)}, u32[]{:S(2)}) copy-start(f32[128,128]{1,0:T(8,128)} %refs_6_.5) | copy-start | bytes 196612
  130.5 7.4 %copy-start.6 = (f32[128,128]{1,0:T(8,128)S(1)}, f32[128,128]{1,0:T(8,128)}, u32[]{:S(2)}) copy-start(f32[128,128]{1,0:T(8,128)} %refs_7_.5) | copy-start | bytes 196612
  131.3 6.6 %copy-start.2 = (f32[128,128]{1,0:T(8,128)S(1)}, f32[128,128]{1,0:T(8,128)}, u32[]{:S(2)}) copy-start(f32[128,128]{1,0:T(8,128)} %refs_7_.4) | copy-start | bytes 196612
  131.3 6.6 %copy-start.3 = (f32[128,128]{1,0:T(8,128)S(1)}, f32[128,128]{1,0:T(8,128)}, u32[]{:S(2)}) copy-start(f32[128,128]{1,0:T(8,128)} %refs_4_.5) | copy-start | bytes 196612
  131.3 13.8 %all-to-all-start.4 = ((f32[8,16,128]{2,1,0:T(8,128)}), f32[8,16,128]{2,1,0:T(8,128)S(1)}, u32[]{:S(2)}, u32[]{:S(2)}) async-start(f32[8,16,128]{2,1,0:T(8,128)} %get-tuple-element.52), calls=%async_computation.4 | async-start | bytes 131072 | tf_op jit(solution)/shard_map/all_to_all | solution.py:385
  137.9 1.5 copy-start.10
  139.4 0.7 copy-start.7
  139.4 0.7 copy-start.8
  160.1 7.1 %collective-permute-start.13 = (f32[32,16,128]{2,1,0:T(8,128)S(1)}, f32[32,16,128]{2,1,0:T(8,128)S(1)}, u32[]{:S(2)}, u32[]{:S(2)}) collective-permute-start(f32[32,16,128]{2,1,0:T(8,128)S(1)} %all_to_all.31.refs_1_), channel_id=1, source_target_pairs={{0,32},{32,0},{1,33},{33,1},{2,34},{34,2},{3,35},{35,3},{4,36},{36... | collective-permute-start | bytes 786440 | tf_op jit(solution)/shard_map/ppermute | solution.py:389

commit v7 on v6

--- a/solution.py
+++ b/solution.py
@@ -194,10 +194,10 @@
         both = bdot(d_t, wh)
         dv_t = both[0:32] + both[32:64] + bdot(d_t[0:32], wl)
         d_scores = weights * (d_weights - centred)
-        if column == 0:
-            db_ref[s0 : s0 + per] = d_scores.reshape(per, 32, 512)
-        else:
-            db_ref[s0 : s0 + per] += d_scores.reshape(per, 32, 512)
+        for slot in range(8):
+            piece = d_scores[slot * 32 : (slot + 1) * 32]
+            at = (slot & 3) * 2 + (slot >> 2)
+            db_ref[at] = piece if column == 0 else db_ref[at] + piece
         sh, sl = split(d_scores)
         d_query = bdot(sh, k_both) + bdot(sl, k_first)
         d_query = d_query + pltpu.roll(d_query, 96, 1)
@@ -431,9 +431,11 @@
     back, d_own, d_other = attend_call(place, keep, data, *bias)
 
     got = swap(back, ROWS)
-    d_bias = d_own + partner(d_other, "core", 1)
-    d_bias = d_bias[:4] + partner(d_bias[4:], "y", 1)
-    d_bias = d_bias[0] + sum(partner(d_bias[s], "y", flip) for s, flip in ((1, 4), (2, 2), (3, 6)))
+    far = d_own[2:8] + partner(d_other[2:8], "core", 1)
+    pairs = d_own[0:2] + partner(d_other[0:2], "core", 1)
+    for at, flip in ((0, 4), (2, 2), (4, 6)):
+        pairs = pairs + partner(far[at : at + 2], "y", flip)
+    d_bias = pairs[0] + partner(pairs[1], "y", 1)
     d_bias = jnp.transpose(d_bias.reshape(32, 32, 16), (1, 0, 2)).reshape(32, 4, 128)
 
     got = got.reshape(8, 4, 64, 128)

time: 170 us -> 171 us (level)
    ppermute x14 -> x15, waiting for transfers between devices: 11.6 us -> 12.5 us  [partner(): lax.ppermute(value, axis, [(at, at ^ flip) for at in range(lax.axis_size(...]
    ppermute x14 -> x15, starting transfers between devices: 55.5 us -> 54.8 us  [partner(): lax.ppermute(value, axis, [(at, at ^ flip) for at in range(lax.axis_size(...]
  transfers between devices with their start and end apart: 18 -> 19, of which waited for: 10 -> 9; matrix products, arithmetic and copies ran while one was open for 1% -> 1% of each run, Pallas kernels for 4% -> 4%
where the time goes in v7:
time: 171 us; the launch traced here: 170 us
  starting transfers between devices  87.8 us (51%)
  blocking collectives  34.9 us (20%)
  Pallas kernels  22.1 us (13%)
  waiting for transfers between devices  21.6 us (13%)
  local copies, waits for them, and re-layouts  1.71 us (1%)
    ppermute x15, starting transfers between devices, partner(): lax.ppermute(value, axis, [(at, at ^ flip) for at in range(lax.axis_size(...  54.8 us
    all_to_all x2, blocking collectives, swap(): return lax.all_to_all(value, axes, 0, 0, tiled=False)  34.9 us
    all_to_all x4, starting transfers between devices, swap(): return lax.all_to_all(value, axes, 0, 0, tiled=False)  32.9 us
    ppermute x15, waiting for transfers between devices, partner(): lax.ppermute(value, axis, [(at, at ^ flip) for at in range(lax.axis_size(...  12.5 us
    pallas_call x1, Pallas kernels, attend_call(): call(attend_kernel, [shaped(32, 64, 128), shaped(8, 32, 512), shaped(8, 3...  10.1 us
    all_to_all x4, waiting for transfers between devices, swap(): return lax.all_to_all(value, axes, 0, 0, tiled=False)  9.13 us
  transfers between devices with their start and end apart: 19, of which 9 were waited for; matrix products, arithmetic and copies ran while one was open for 1% of the time, Pallas kernels for 4%

profile of v7, /device:TPU:1, one launch (start us, length us, event | category | flops | bytes accessed | tf_op | source)
XLA Modules:
  0.0 170.0 jit_solution(13426600941011904504)
XLA Ops:
  0.6 2.1 %norm_bias.1 = (f32[8,4,4,128]{3,2,1,0:T(4,128)}, f32[512,128]{1,0:T(8,128)}, f32[512,128]{1,0:T(8,128)}) custom-call(f32[16,32,128]{2,1,0:T(8,128)} %x_ref.1, f32[1,128]{1,0:T(1,128)} %bitcast.27, f32[4,128]{1,0:T(4,128)} %refs_8_.1), custom_call_target="tpu_custom_call" | custom-call | flops 1000000000 | bytes 2000000 | tf_op jit(solution)/shard_map/norm_bias/pallas_call | solution.py:405
  2.7 13.7 %all-to-all-start = ((f32[32,4,128]{2,1,0:T(4,128)}), f32[32,4,128]{2,1,0:T(4,128)S(1)}, u32[]{:S(2)}, u32[]{:S(2)}) async-start(f32[32,4,128]{2,1,0:T(4,128)} %bitcast.36), calls=%async_computation | async-start | bytes 131072 | tf_op jit(solution)/shard_map/all_to_all | solution.py:385
  16.4 0.6 pad_add_fusion.refs_0_.place_ref
  17.0 2.9 %project.1 = (f32[8,4,64,128]{3,2,1,0:T(8,128)}, f32[512,128]{1,0:T(8,128)}, f32[512,128]{1,0:T(8,128)}, s32[4,512]{1,0:T(4,128)}) custom-call(s32[3]{0:T(128)} %pad_add_fusion.refs_0_.place_ref, f32[512,128]{1,0:T(8,128)} %get-tuple-element.39.refs_1_.scaled_ref, f32[16,32,128]{2,1,0:T(8,128)} %cot_ref.1, f32[1,128]{1,0:T(1,128)} %bitcast.28, ...), custom_call_target="tpu_custom_call" | custom-call | flops 2000000000 | bytes 4000000 | tf_op jit(solution)/shard_map/project/pallas_call | solution.py:409
  20.0 5.3 %all-to-all-done = f32[32,4,128]{2,1,0:T(4,128)S(1)} async-done(((f32[32,4,128]{2,1,0:T(4,128)}), f32[32,4,128]{2,1,0:T(4,128)S(1)}, u32[]{:S(2)}, u32[]{:S(2)}) %all-to-all-start) | async-done | bytes 65568 | tf_op jit(solution)/shard_map/all_to_all | solution.py:385
  25.3 3.9 %all-to-all-start.1 = ((f32[32,64,128]{2,1,0:T(8,128)}), f32[32,64,128]{2,1,0:T(8,128)S(1)}, u32[]{:S(2)}, u32[]{:S(2)}) async-start(f32[32,64,128]{2,1,0:T(8,128)} %bitcast.35), calls=%async_computation.1 | async-start | bytes 2097152 | tf_op jit(solution)/shard_map/all_to_all | solution.py:385
  29.2 0.1 copy.33
  29.3 0.2 copy.34
  29.5 0.1 copy.38
  29.6 7.5 %collective-permute-start = (f32[1,32,512]{2,1,0:T(8,128)S(1)}, f32[1,32,512]{2,1,0:T(8,128)S(1)}, u32[]{:S(2)}, u32[]{:S(2)}) collective-permute-start(f32[1,32,512]{2,1,0:T(8,128)S(1)} %copy.38), channel_id=1, source_target_pairs={{0,256},{64,320},{128,384},{192,448},{256,0},{320,64},{384,128},{4... | collective-permute-start | bytes 196616 | tf_op jit(solution)/shard_map/ppermute | solution.py:389
  37.1 2.0 %collective-permute-start.2 = (f32[1,32,512]{2,1,0:T(8,128)S(1)}, f32[1,32,512]{2,1,0:T(8,128)S(1)}, u32[]{:S(2)}, u32[]{:S(2)}) collective-permute-start(f32[1,32,512]{2,1,0:T(8,128)S(1)} %copy.38), channel_id=1, source_target_pairs={{0,384},{64,448},{128,256},{192,320},{256,128},{320,192},{384,0},{... | collective-permute-start | bytes 196616 | tf_op jit(solution)/shard_map/ppermute | solution.py:389
  39.1 2.4 %collective-permute-start.1 = (f32[1,32,512]{2,1,0:T(8,128)S(1)}, f32[1,32,512]{2,1,0:T(8,128)S(1)}, u32[]{:S(2)}, u32[]{:S(2)}) collective-permute-start(f32[1,32,512]{2,1,0:T(8,128)S(1)} %copy.38), channel_id=1, source_target_pairs={{0,128},{64,192},{128,0},{192,64},{256,384},{320,448},{384,256},{4... | collective-permute-start | bytes 196616 | tf_op jit(solution)/shard_map/ppermute | solution.py:389
  41.5 2.8 %collective-permute-start.3 = (f32[2,32,512]{2,1,0:T(8,128)S(1)}, f32[2,32,512]{2,1,0:T(8,128)S(1)}, u32[]{:S(2)}, u32[]{:S(2)}) collective-permute-start(f32[2,32,512]{2,1,0:T(8,128)S(1)} %pad_maximum_fusion.2), channel_id=1, source_target_pairs={{0,64},{64,0},{128,192},{192,128},{256,320},{320,256},{384,448},{4... | collective-permute-start | bytes 393224 | tf_op jit(solution)/shard_map/ppermute | solution.py:389
  44.3 0.2 collective-permute-done.2
  44.5 0.8 collective-permute-done.1
  45.3 3.6 %collective-permute-start.4 = (f32[2,32,512]{2,1,0:T(8,128)S(1)}, f32[2,32,512]{2,1,0:T(8,128)S(1)}, u32[]{:S(2)}, u32[]{:S(2)}) collective-permute-start(f32[2,32,512]{2,1,0:T(8,128)S(1)} %pad_maximum_fusion.3), channel_id=1, source_target_pairs={{0,64},{64,0},{128,192},{192,128},{256,320},{320,256},{384,448},{4... | collective-permute-start | bytes 393224 | tf_op jit(solution)/shard_map/ppermute | solution.py:389
  48.9 6.0 %collective-permute-start.5 = (f32[4,32,512]{2,1,0:T(8,128)S(1)}, f32[4,32,512]{2,1,0:T(8,128)S(1)}, u32[]{:S(2)}, u32[]{:S(2)}) collective-permute-start(f32[4,32,512]{2,1,0:T(8,128)S(1)} %pad_maximum_fusion.own_low_ref), channel_id=1, source_target_pairs={{0,32},{32,0},{1,33},{33,1},{2,34},{34,2},{3,35},{35,3},{4,36},{36... | collective-permute-start | bytes 786440 | tf_op jit(solution)/shard_map/ppermute | solution.py:389
  55.0 2.8 %collective-permute-start.6 = (f32[4,32,512]{2,1,0:T(8,128)S(1)}, f32[4,32,512]{2,1,0:T(8,128)S(1)}, u32[]{:S(2)}, u32[]{:S(2)}) collective-permute-start(f32[4,32,512]{2,1,0:T(8,128)S(1)} %constant_dynamic-update-slice_fusion.own_high_ref), channel_id=1, source_target_pairs={{0,32},{32,0},{1,33},{33,1},{2,34},{34,2},{3,35},{35,3},{4,36},{36... | collective-permute-start | bytes 786440 | tf_op jit(solution)/shard_map/ppermute | solution.py:389
  57.9 1.1 collective-permute-done.6.other_high_ref
  59.0 10.1 %attend.1 = (f32[32,64,128]{2,1,0:T(8,128)}, f32[8,32,512]{2,1,0:T(8,128)S(1)}, f32[8,32,512]{2,1,0:T(8,128)S(1)}) custom-call(s32[3]{0:T(128)S(1)} %copy-done, s32[4,512]{1,0:T(4,128)S(1)} %copy-done.13, f32[32,64,128]{2,1,0:T(8,128)S(1)} %all-to-all-done.1.data_ref, f32[4,32,512]{2,1,0:T(8,128)S(1)} %pad_maximum_fusion.own_low_ref, ...), custom_call_target="tpu_custom_call" | custom-call | flops 12000000000 | bytes 24000000 | tf_op jit(solution)/shard_map/attend/pallas_call | solution.py:374
  69.1 9.4 %all-to-all-start.2 = ((f32[32,64,128]{2,1,0:T(8,128)}), f32[32,64,128]{2,1,0:T(8,128)S(1)}, u32[]{:S(2)}, u32[]{:S(2)}) async-start(f32[32,64,128]{2,1,0:T(8,128)} %get-tuple-element.45), calls=%async_computation.2 | async-start | bytes 2097152 | tf_op jit(solution)/shard_map/all_to_all | solution.py:385
  78.6 2.6 %collective-permute-start.9 = (f32[6,32,512]{2,1,0:T(8,128)S(1)}, f32[6,32,512]{2,1,0:T(8,128)S(1)}, u32[]{:S(2)}, u32[]{:S(2)}) collective-permute-start(f32[6,32,512]{2,1,0:T(8,128)S(1)} %slice.30), channel_id=1, source_target_pairs={{0,32},{32,0},{1,33},{33,1},{2,34},{34,2},{3,35},{35,3},{4,36},{36... | collective-permute-start | bytes 1179656 | tf_op jit(solution)/shard_map/ppermute | solution.py:389
  81.2 1.9 %collective-permute-start.8 = (f32[2,32,512]{2,1,0:T(8,128)S(1)}, f32[2,32,512]{2,1,0:T(8,128)S(1)}, u32[]{:S(2)}, u32[]{:S(2)}) collective-permute-start(f32[2,32,512]{2,1,0:T(8,128)S(1)} %slice.28), channel_id=1, source_target_pairs={{0,32},{32,0},{1,33},{33,1},{2,34},{34,2},{3,35},{35,3},{4,36},{36... | collective-permute-start | bytes 393224 | tf_op jit(solution)/shard_map/ppermute | solution.py:389
  83.1 0.1 slice_add_fusion
  83.2 6.3 %collective-permute-start.10 = (f32[2,32,512]{2,1,0:T(8,128)S(1)}, f32[2,32,512]{2,1,0:T(8,128)S(1)}, u32[]{:S(2)}, u32[]{:S(2)}) collective-permute-start(f32[2,32,512]{2,1,0:T(8,128)S(1)} %get-tuple-element.68), channel_id=1, source_target_pairs={{0,256},{64,320},{128,384},{192,448},{256,0},{320,64},{384,128},{4... | collective-permute-start | bytes 393224 | tf_op jit(solution)/shard_map/ppermute | solution.py:389
  89.5 2.4 %collective-permute-start.12 = (f32[2,32,512]{2,1,0:T(8,128)S(1)}, f32[2,32,512]{2,1,0:T(8,128)S(1)}, u32[]{:S(2)}, u32[]{:S(2)}) collective-permute-start(f32[2,32,512]{2,1,0:T(8,128)S(1)} %get-tuple-element.69), channel_id=1, source_target_pairs={{0,384},{64,448},{128,256},{192,320},{256,128},{320,192},{384,0},{... | collective-permute-start | bytes 393224 | tf_op jit(solution)/shard_map/ppermute | solution.py:389
  91.9 3.1 %collective-permute-start.11 = (f32[2,32,512]{2,1,0:T(8,128)S(1)}, f32[2,32,512]{2,1,0:T(8,128)S(1)}, u32[]{:S(2)}, u32[]{:S(2)}) collective-permute-start(f32[2,32,512]{2,1,0:T(8,128)S(1)} %get-tuple-element.70), channel_id=1, source_target_pairs={{0,128},{64,192},{128,0},{192,64},{256,384},{320,448},{384,256},{4... | collective-permute-start | bytes 393224 | tf_op jit(solution)/shard_map/ppermute | solution.py:389
  95.1 6.2 %collective-permute-done.12 = f32[2,32,512]{2,1,0:T(8,128)S(1)} collective-permute-done((f32[2,32,512]{2,1,0:T(8,128)S(1)}, f32[2,32,512]{2,1,0:T(8,128)S(1)}, u32[]{:S(2)}, u32[]{:S(2)}) %collective-permute-start.12) | collective-permute-done | bytes 131104 | tf_op jit(solution)/shard_map/ppermute | solution.py:389
  101.2 2.5 %collective-permute-done.11 = f32[2,32,512]{2,1,0:T(8,128)S(1)} collective-permute-done((f32[2,32,512]{2,1,0:T(8,128)S(1)}, f32[2,32,512]{2,1,0:T(8,128)S(1)}, u32[]{:S(2)}, u32[]{:S(2)}) %collective-permute-start.11) | collective-permute-done | bytes 131104 | tf_op jit(solution)/shard_map/ppermute | solution.py:389
  103.7 0.1 add_add_fusion
  103.8 2.1 %collective-permute-start.13 = (f32[32,512]{1,0:T(8,128)S(1)}, f32[32,512]{1,0:T(8,128)S(1)}, u32[]{:S(2)}, u32[]{:S(2)}) collective-permute-start(f32[32,512]{1,0:T(8,128)S(1)} %slice_bitcast_fusion), channel_id=1, source_target_pairs={{0,64},{64,0},{128,192},{192,128},{256,320},{320,256},{384,448},{4... | collective-permute-start | bytes 196616 | tf_op jit(solution)/shard_map/ppermute | solution.py:389
  106.0 1.7 %param_grads.1 = (f32[320,128]{1,0:T(8,128)S(1)}, f32[320,128]{1,0:T(8,128)S(1)}) custom-call(s32[3]{0:T(128)S(1)} %copy-done, f32[8,4,64,128]{3,2,1,0:T(8,128)S(1)} %bitcast.25, f32[512,128]{1,0:T(8,128)S(1)} %copy-done.9, f32[512,128]{1,0:T(8,128)S(1)} %copy-done.11, f32[512,128]{1,0:T(8,128)S(1)} %copy-done.12, f32[16,32,128]{2,1,0:T(8,128)S(1)} %copy-done.1), custom_call_target="tpu_custom_call" | custom-call | flops 2000000000 | bytes 4000000 | tf_op jit(solution)/shard_map/param_grads/pallas_call | solution.py:442
  107.7 3.5 %collective-permute-start.7 = (f32[320,128]{1,0:T(8,128)S(1)}, f32[320,128]{1,0:T(8,128)S(1)}, u32[]{:S(2)}, u32[]{:S(2)}) collective-permute-start(f32[320,128]{1,0:T(8,128)S(1)} %get-tuple-element.49), channel_id=1, source_target_pairs={{0,32},{32,0},{1,33},{33,1},{2,34},{34,2},{3,35},{35,3},{4,36},{36... | collective-permute-start | bytes 491528 | tf_op jit(solution)/shard_map/ppermute | solution.py:389
  111.2 0.1 copy.40
  111.3 0.2 copy.41
  111.6 0.1 copy.42
  111.7 0.5 collective-permute-done.7
  112.3 19.9 %all_to_all.30.recv_ref = f32[32,14,128]{2,1,0:T(8,128)S(1)} all-to-all(f32[32,14,128]{2,1,0:T(8,128)S(1)} %pad_maximum_fusion.1), channel_id=1, replica_groups=mesh['y'=8,'core'=2,'z'=8,'x'=4] {'z','x'}, dimensions={0} | all-to-all | bytes 458752 | tf_op jit(solution)/shard_map/all_to_all | solution.py:385
  132.2 0.8 tail.1
  133.0 5.9 %all-to-all-start.4 = ((f32[8,16,128]{2,1,0:T(8,128)}), f32[8,16,128]{2,1,0:T(8,128)S(1)}, u32[]{:S(2)}, u32[]{:S(2)}) async-start(f32[8,16,128]{2,1,0:T(8,128)} %get-tuple-element.52), calls=%async_computation.4 | async-start | bytes 131072 | tf_op jit(solution)/shard_map/all_to_all | solution.py:385
  138.9 1.4 update.1
  140.4 0.7 copy-done.7
  141.1 1.2 norm_back.1
  142.3 3.8 %all-to-all-done.4.recv_ref = f32[8,16,128]{2,1,0:T(8,128)S(1)} async-done(((f32[8,16,128]{2,1,0:T(8,128)}), f32[8,16,128]{2,1,0:T(8,128)S(1)}, u32[]{:S(2)}, u32[]{:S(2)}) %all-to-all-start.4) | async-done | bytes 65568 | tf_op jit(solution)/shard_map/all_to_all | solution.py:385
  146.1 14.9 %all_to_all.31.refs_1_ = f32[32,16,128]{2,1,0:T(8,128)S(1)} all-to-all(f32[32,16,128]{2,1,0:T(8,128)S(1)} %share.1), channel_id=1, replica_groups=mesh['y'=8,'core'=2,'z'=8,'x'=4] {'z','x'}, dimensions={0} | all-to-all | bytes 524288 | tf_op jit(solution)/shard_map/all_to_all | solution.py:385
  161.1 6.0 %collective-permute-start.14 = (f32[32,16,128]{2,1,0:T(8,128)S(1)}, f32[32,16,128]{2,1,0:T(8,128)S(1)}, u32[]{:S(2)}, u32[]{:S(2)}) collective-permute-start(f32[32,16,128]{2,1,0:T(8,128)S(1)} %all_to_all.31.refs_1_), channel_id=1, source_target_pairs={{0,32},{32,0},{1,33},{33,1},{2,34},{34,2},{3,35},{35,3},{4,36},{36... | collective-permute-start | bytes 786440 | tf_op jit(solution)/shard_map/ppermute | solution.py:389
  167.1 1.1 collective-permute-done.14.refs_2_
  168.2 1.8 %finish.1 = (f32[128,128]{1,0:T(8,128)}, f32[128,128]{1,0:T(8,128)}, f32[128,128]{1,0:T(8,128)}, f32[128,128]{1,0:T(8,128)}, f32[1,128]{1,0:T(1,128)}, /*index=5...) custom-call(s32[3]{0:T(128)S(1)} %copy-done, f32[32,16,128]{2,1,0:T(8,128)S(1)} %all_to_all.31.refs_1_, ...), custom_call_target="tpu_custom_call" | custom-call | flops 1000000000 | bytes 2000000 | tf_op jit(solution)/shard_map/finish/pallas_call | solution.py:464
  (51 shorter events, 0.3 us)
Async XLA Ops:
  2.7 22.5 %all-to-all-start = ((f32[32,4,128]{2,1,0:T(4,128)}), f32[32,4,128]{2,1,0:T(4,128)S(1)}, u32[]{:S(2)}, u32[]{:S(2)}) async-start(f32[32,4,128]{2,1,0:T(4,128)} %bitcast.36), calls=%async_computation | async-start | bytes 131072 | tf_op jit(solution)/shard_map/all_to_all | solution.py:385
  25.3 33.8 %all-to-all-start.1 = ((f32[32,64,128]{2,1,0:T(8,128)}), f32[32,64,128]{2,1,0:T(8,128)S(1)}, u32[]{:S(2)}, u32[]{:S(2)}) async-start(f32[32,64,128]{2,1,0:T(8,128)} %bitcast.35), calls=%async_computation.1 | async-start | bytes 2097152 | tf_op jit(solution)/shard_map/all_to_all | solution.py:385
  29.6 11.8 %collective-permute-start = (f32[1,32,512]{2,1,0:T(8,128)S(1)}, f32[1,32,512]{2,1,0:T(8,128)S(1)}, u32[]{:S(2)}, u32[]{:S(2)}) collective-permute-start(f32[1,32,512]{2,1,0:T(8,128)S(1)} %copy.38), channel_id=1, source_target_pairs={{0,256},{64,320},{128,384},{192,448},{256,0},{320,64},{384,128},{4... | collective-permute-start | bytes 196616 | tf_op jit(solution)/shard_map/ppermute | solution.py:389
  37.1 7.4 %collective-permute-start.2 = (f32[1,32,512]{2,1,0:T(8,128)S(1)}, f32[1,32,512]{2,1,0:T(8,128)S(1)}, u32[]{:S(2)}, u32[]{:S(2)}) collective-permute-start(f32[1,32,512]{2,1,0:T(8,128)S(1)} %copy.38), channel_id=1, source_target_pairs={{0,384},{64,448},{128,256},{192,320},{256,128},{320,192},{384,0},{... | collective-permute-start | bytes 196616 | tf_op jit(solution)/shard_map/ppermute | solution.py:389
  39.1 6.2 %collective-permute-start.1 = (f32[1,32,512]{2,1,0:T(8,128)S(1)}, f32[1,32,512]{2,1,0:T(8,128)S(1)}, u32[]{:S(2)}, u32[]{:S(2)}) collective-permute-start(f32[1,32,512]{2,1,0:T(8,128)S(1)} %copy.38), channel_id=1, source_target_pairs={{0,128},{64,192},{128,0},{192,64},{256,384},{320,448},{384,256},{4... | collective-permute-start | bytes 196616 | tf_op jit(solution)/shard_map/ppermute | solution.py:389
  41.5 13.5 %collective-permute-start.3 = (f32[2,32,512]{2,1,0:T(8,128)S(1)}, f32[2,32,512]{2,1,0:T(8,128)S(1)}, u32[]{:S(2)}, u32[]{:S(2)}) collective-permute-start(f32[2,32,512]{2,1,0:T(8,128)S(1)} %pad_maximum_fusion.2), channel_id=1, source_target_pairs={{0,64},{64,0},{128,192},{192,128},{256,320},{320,256},{384,448},{4... | collective-permute-start | bytes 393224 | tf_op jit(solution)/shard_map/ppermute | solution.py:389
  45.3 9.7 %collective-permute-start.4 = (f32[2,32,512]{2,1,0:T(8,128)S(1)}, f32[2,32,512]{2,1,0:T(8,128)S(1)}, u32[]{:S(2)}, u32[]{:S(2)}) collective-permute-start(f32[2,32,512]{2,1,0:T(8,128)S(1)} %pad_maximum_fusion.3), channel_id=1, source_target_pairs={{0,64},{64,0},{128,192},{192,128},{256,320},{320,256},{384,448},{4... | collective-permute-start | bytes 393224 | tf_op jit(solution)/shard_map/ppermute | solution.py:389
  48.9 9.0 %collective-permute-start.5 = (f32[4,32,512]{2,1,0:T(8,128)S(1)}, f32[4,32,512]{2,1,0:T(8,128)S(1)}, u32[]{:S(2)}, u32[]{:S(2)}) collective-permute-start(f32[4,32,512]{2,1,0:T(8,128)S(1)} %pad_maximum_fusion.own_low_ref), channel_id=1, source_target_pairs={{0,32},{32,0},{1,33},{33,1},{2,34},{34,2},{3,35},{35,3},{4,36},{36... | collective-permute-start | bytes 786440 | tf_op jit(solution)/shard_map/ppermute | solution.py:389
  55.0 4.0 %copy-start.13 = (s32[4,512]{1,0:T(4,128)S(1)}, s32[4,512]{1,0:T(4,128)}, u32[]{:S(2)}) copy-start(s32[4,512]{1,0:T(4,128)} %get-tuple-element.40.keep_ref) | copy-start | bytes 24580
  55.0 4.0 %copy-start = (s32[3]{0:T(128)S(1)}, s32[3]{0:T(128)}, u32[]{:S(2)}) copy-start(s32[3]{0:T(128)} %pad_add_fusion.refs_0_.place_ref) | copy-start | bytes 40
  55.0 4.0 %collective-permute-start.6 = (f32[4,32,512]{2,1,0:T(8,128)S(1)}, f32[4,32,512]{2,1,0:T(8,128)S(1)}, u32[]{:S(2)}, u32[]{:S(2)}) collective-permute-start(f32[4,32,512]{2,1,0:T(8,128)S(1)} %constant_dynamic-update-slice_fusion.own_high_ref), channel_id=1, source_target_pairs={{0,32},{32,0},{1,33},{33,1},{2,34},{34,2},{3,35},{35,3},{4,36},{36... | collective-permute-start | bytes 786440 | tf_op jit(solution)/shard_map/ppermute | solution.py:389
  69.1 36.8 %all-to-all-start.2 = ((f32[32,64,128]{2,1,0:T(8,128)}), f32[32,64,128]{2,1,0:T(8,128)S(1)}, u32[]{:S(2)}, u32[]{:S(2)}) async-start(f32[32,64,128]{2,1,0:T(8,128)} %get-tuple-element.45), calls=%async_computation.2 | async-start | bytes 2097152 | tf_op jit(solution)/shard_map/all_to_all | solution.py:385
  78.6 4.5 %collective-permute-start.9 = (f32[6,32,512]{2,1,0:T(8,128)S(1)}, f32[6,32,512]{2,1,0:T(8,128)S(1)}, u32[]{:S(2)}, u32[]{:S(2)}) collective-permute-start(f32[6,32,512]{2,1,0:T(8,128)S(1)} %slice.30), channel_id=1, source_target_pairs={{0,32},{32,0},{1,33},{33,1},{2,34},{34,2},{3,35},{35,3},{4,36},{36... | collective-permute-start | bytes 1179656 | tf_op jit(solution)/shard_map/ppermute | solution.py:389
  81.2 13.9 %collective-permute-start.8 = (f32[2,32,512]{2,1,0:T(8,128)S(1)}, f32[2,32,512]{2,1,0:T(8,128)S(1)}, u32[]{:S(2)}, u32[]{:S(2)}) collective-permute-start(f32[2,32,512]{2,1,0:T(8,128)S(1)} %slice.28), channel_id=1, source_target_pairs={{0,32},{32,0},{1,33},{33,1},{2,34},{34,2},{3,35},{35,3},{4,36},{36... | collective-permute-start | bytes 393224 | tf_op jit(solution)/shard_map/ppermute | solution.py:389
  83.2 22.8 %copy-start.12 = (f32[512,128]{1,0:T(8,128)S(1)}, f32[512,128]{1,0:T(8,128)}, u32[]{:S(2)}) copy-start(f32[512,128]{1,0:T(8,128)} %get-tuple-element.47.dgated_ref.refs_2_) | copy-start | bytes 786436
  83.2 11.8 %collective-permute-start.10 = (f32[2,32,512]{2,1,0:T(8,128)S(1)}, f32[2,32,512]{2,1,0:T(8,128)S(1)}, u32[]{:S(2)}, u32[]{:S(2)}) collective-permute-start(f32[2,32,512]{2,1,0:T(8,128)S(1)} %get-tuple-element.68), channel_id=1, source_target_pairs={{0,256},{64,320},{128,384},{192,448},{256,0},{320,64},{384,128},{4... | collective-permute-start | bytes 393224 | tf_op jit(solution)/shard_map/ppermute | solution.py:389
  89.5 11.7 %collective-permute-start.12 = (f32[2,32,512]{2,1,0:T(8,128)S(1)}, f32[2,32,512]{2,1,0:T(8,128)S(1)}, u32[]{:S(2)}, u32[]{:S(2)}) collective-permute-start(f32[2,32,512]{2,1,0:T(8,128)S(1)} %get-tuple-element.69), channel_id=1, source_target_pairs={{0,384},{64,448},{128,256},{192,320},{256,128},{320,192},{384,0},{... | collective-permute-start | bytes 393224 | tf_op jit(solution)/shard_map/ppermute | solution.py:389
  91.9 14.1 %copy-start.1 = (f32[16,32,128]{2,1,0:T(8,128)S(1)}, f32[16,32,128]{2,1,0:T(8,128)}, u32[]{:S(2)}) copy-start(f32[16,32,128]{2,1,0:T(8,128)} %cot_ref.1) | copy-start | bytes 786436
  91.9 14.1 %copy-start.9 = (f32[512,128]{1,0:T(8,128)S(1)}, f32[512,128]{1,0:T(8,128)}, u32[]{:S(2)}) copy-start(f32[512,128]{1,0:T(8,128)} %get-tuple-element.39.refs_1_.scaled_ref) | copy-start | bytes 786436
  91.9 14.1 %copy-start.11 = (f32[512,128]{1,0:T(8,128)S(1)}, f32[512,128]{1,0:T(8,128)}, u32[]{:S(2)}) copy-start(f32[512,128]{1,0:T(8,128)} %get-tuple-element.46.gate_ref.refs_1_) | copy-start | bytes 786436
  91.9 11.8 %collective-permute-start.11 = (f32[2,32,512]{2,1,0:T(8,128)S(1)}, f32[2,32,512]{2,1,0:T(8,128)S(1)}, u32[]{:S(2)}, u32[]{:S(2)}) collective-permute-start(f32[2,32,512]{2,1,0:T(8,128)S(1)} %get-tuple-element.70), channel_id=1, source_target_pairs={{0,128},{64,192},{128,0},{192,64},{256,384},{320,448},{384,256},{4... | collective-permute-start | bytes 393224 | tf_op jit(solution)/shard_map/ppermute | solution.py:389
  103.8 7.4 %collective-permute-start.13 = (f32[32,512]{1,0:T(8,128)S(1)}, f32[32,512]{1,0:T(8,128)S(1)}, u32[]{:S(2)}, u32[]{:S(2)}) collective-permute-start(f32[32,512]{1,0:T(8,128)S(1)} %slice_bitcast_fusion), channel_id=1, source_target_pairs={{0,64},{64,0},{128,192},{192,128},{256,320},{320,256},{384,448},{4... | collective-permute-start | bytes 196616 | tf_op jit(solution)/shard_map/ppermute | solution.py:389
  107.7 4.5 %collective-permute-start.7 = (f32[320,128]{1,0:T(8,128)S(1)}, f32[320,128]{1,0:T(8,128)S(1)}, u32[]{:S(2)}, u32[]{:S(2)}) collective-permute-start(f32[320,128]{1,0:T(8,128)S(1)} %get-tuple-element.49), channel_id=1, source_target_pairs={{0,32},{32,0},{1,33},{33,1},{2,34},{34,2},{3,35},{35,3},{4,36},{36... | collective-permute-start | bytes 491528 | tf_op jit(solution)/shard_map/ppermute | solution.py:389
  132.2 6.7 %copy-start.4 = (f32[128,128]{1,0:T(8,128)S(1)}, f32[128,128]{1,0:T(8,128)}, u32[]{:S(2)}) copy-start(f32[128,128]{1,0:T(8,128)} %refs_5_.5) | copy-start | bytes 196612
  132.2 6.7 %copy-start.5 = (f32[128,128]{1,0:T(8,128)S(1)}, f32[128,128]{1,0:T(8,128)}, u32[]{:S(2)}) copy-start(f32[128,128]{1,0:T(8,128)} %refs_6_.5) | copy-start | bytes 196612
  132.2 6.7 %copy-start.6 = (f32[128,128]{1,0:T(8,128)S(1)}, f32[128,128]{1,0:T(8,128)}, u32[]{:S(2)}) copy-start(f32[128,128]{1,0:T(8,128)} %refs_7_.5) | copy-start | bytes 196612
  133.0 5.9 %copy-start.2 = (f32[128,128]{1,0:T(8,128)S(1)}, f32[128,128]{1,0:T(8,128)}, u32[]{:S(2)}) copy-start(f32[128,128]{1,0:T(8,128)} %refs_7_.4) | copy-start | bytes 196612
  133.0 5.9 %copy-start.3 = (f32[128,128]{1,0:T(8,128)S(1)}, f32[128,128]{1,0:T(8,128)}, u32[]{:S(2)}) copy-start(f32[128,128]{1,0:T(8,128)} %refs_4_.5) | copy-start | bytes 196612
  133.0 13.1 %all-to-all-start.4 = ((f32[8,16,128]{2,1,0:T(8,128)}), f32[8,16,128]{2,1,0:T(8,128)S(1)}, u32[]{:S(2)}, u32[]{:S(2)}) async-start(f32[8,16,128]{2,1,0:T(8,128)} %get-tuple-element.52), calls=%async_computation.4 | async-start | bytes 131072 | tf_op jit(solution)/shard_map/all_to_all | solution.py:385
  138.9 1.5 copy-start.10
  140.4 0.7 copy-start.7
  140.4 0.7 copy-start.8
  161.1 7.1 %collective-permute-start.14 = (f32[32,16,128]{2,1,0:T(8,128)S(1)}, f32[32,16,128]{2,1,0:T(8,128)S(1)}, u32[]{:S(2)}, u32[]{:S(2)}) collective-permute-start(f32[32,16,128]{2,1,0:T(8,128)S(1)} %all_to_all.31.refs_1_), channel_id=1, source_target_pairs={{0,32},{32,0},{1,33},{33,1},{2,34},{34,2},{3,35},{35,3},{4,36},{36... | collective-permute-start | bytes 786440 | tf_op jit(solution)/shard_map/ppermute | solution.py:389
